TPU v7x, 32 devices: a whole 2x2x4 slice. The times are simulated.
32 devices in a mesh: grp: 2 (over x), ka: 16 (over z, y, core).
Axes of the slice: x: 2, y: 2, z: 4, core: 2. Of those that a mesh axis runs over, the one named last changes fastest.
Arguments:
- sources: bfloat16 [1024, 512, 64], P('ka', None, 'grp'), parts along dimension 2, may hold values from -6 to 6
- bessel: bfloat16 [512, 1024, 512], P('ka'), may hold values from -0.25 to 0.25
- multipoles: int32 [512], P('ka'), may hold values from 2 to 5000
- window_low: int32 [64], P('grp'), parts along dimension 0, may hold values from 0 to 127
- window_high: int32 [64], P('grp'), parts along dimension 0, may hold values from 384 to 512
- params: float32 [6, 64], P(None, 'grp'), parts along dimension 1, may hold values from -1 to 1
- weight_in: float32 [512, 6], replicated, may hold values from -2.5 to 2.5
- bias_in: float32 [512], replicated, may hold values from -3 to 3
- weight_mid: float32 [512, 512], replicated, may hold values from -0.25 to 0.25
- bias_mid: float32 [512], replicated, may hold values from -3 to 3
- weight_out: float32 [64, 512], replicated, may hold values from -0.25 to 0.25
- bias_out: float32 [64], replicated, may hold values from -4 to 4
- pca_basis: float32 [512, 64], P('ka'), may hold values from -0.75 to 0.75
- offset: float32 [512], P('ka'), may hold values from -4 to 4
Outputs:
- spectra: float32 [512, 64], P('ka', 'grp'), parts along dimension 1
- grad_basis: float32 [1024, 64], P(('grp', 'ka')), parts along dimension 0
- grad_weight_in: float32 [1024, 6], P('grp'), parts along dimension 0
- grad_weight_mid: float32 [1024, 512], P('grp'), parts along dimension 0
- grad_weight_out: float32 [128, 512], P('grp'), parts along dimension 0
There are 2 independent parts, one for each index of `grp`. A program takes and returns all parts, laid end to end along the dimension named above; an argument that names none is the same for every part. Nothing has to cross between parts.
All inputs are finite; a program needn't handle non-finite values.
Results may differ from a plain program's by a relative error of at most 0.0003.
Values may be sent and summed in bfloat16 or wider, within the bound.
No kernel may reach another device: no remote copies, remote signals or barrier semaphores. Data moves between devices by JAX's collectives and lax.ppermute only.
A program may use at most 128 MiB of HBM per device.

v0:
```python
import math

import jax
import jax.numpy as jnp
from jax import lax
from jax.sharding import PartitionSpec as P

LMAX = 5000


def primordial(params, window_low, window_high, first_wave, wave_count, total_waves):
    wave_index = first_wave + jnp.arange(wave_count, dtype=jnp.int32)
    log_ratio = math.log(0.002) + wave_index.astype(jnp.float32) * (math.log(5000.0) / total_waves)
    tilted = 0.5 * params[0][None, :] + 0.3 * params[1][None, :] * log_ratio[:, None]
    inside = (wave_index[:, None] >= window_low[None, :]) & (
        wave_index[:, None] < window_high[None, :]
    )
    return jnp.where(inside, jnp.exp(tilted), jnp.zeros_like(tilted)) / total_waves


def silu_slope(value):
    sigma = jax.nn.sigmoid(value)
    return sigma * (1.0 + value * (1.0 - sigma))


def mat(left, right):
    return jnp.dot(left, right, precision=lax.Precision.HIGHEST)


def backward(
    coef_grad, inner_pre, inner_act, middle_pre, middle_act, params, weight_mid, weight_out
):
    grad_out = mat(coef_grad, middle_act.T)
    middle_delta = mat(weight_out.T, coef_grad) * silu_slope(middle_pre)
    grad_mid = mat(middle_delta, inner_act.T)
    inner_delta = mat(weight_mid.T, middle_delta) * silu_slope(inner_pre)
    grad_in = mat(inner_delta, params.T)
    return (grad_in, grad_mid, grad_out)


def local(
    sources,
    bessel,
    multipoles,
    window_low,
    window_high,
    params,
    weight_in,
    bias_in,
    weight_mid,
    bias_mid,
    weight_out,
    bias_out,
    pca_basis,
    offset,
):
    local_waves = bessel.shape[0]
    total_waves = sources.shape[1]
    cosmos = params.shape[1]
    first_wave = lax.axis_index("ka") * local_waves
    factor = primordial(params, window_low, window_high, first_wave, local_waves, total_waves)
    regrouped = lax.all_to_all(sources, "ka", split_axis=1, concat_axis=0, tiled=True)
    transfer = jnp.einsum("tkc,ktl->klc", regrouped, bessel, preferred_element_type=jnp.float32)
    power = lax.psum_scatter(
        jnp.einsum("klc,kc->lc", transfer * transfer, factor, precision=lax.Precision.HIGHEST),
        "ka",
        scatter_dimension=0,
        tiled=True,
    )
    degree = multipoles.astype(jnp.float32)
    smoothing = jnp.exp(-2.0 * degree * (degree + 1.0) / (LMAX * (LMAX + 1.0)))
    spectra = smoothing[:, None] * power
    inner_pre = mat(weight_in, params) + bias_in[:, None]
    inner_act = jax.nn.silu(inner_pre)
    middle_pre = mat(weight_mid, inner_act) + bias_mid[:, None]
    middle_act = jax.nn.silu(middle_pre)
    coeffs = mat(weight_out, middle_act) + bias_out[:, None]
    residual = offset[:, None] + mat(pca_basis, coeffs) - spectra
    grad_basis = mat(residual, coeffs.T) / cosmos
    coef_part = mat(pca_basis.T, residual) / cosmos
    coef_grad = lax.psum(coef_part, "ka")
    grad_in, grad_mid, grad_out = backward(
        coef_grad, inner_pre, inner_act, middle_pre, middle_act, params, weight_mid, weight_out
    )
    return (spectra, grad_basis, grad_in, grad_mid, grad_out)


def solution(mesh):
    return jax.shard_map(
        local,
        mesh=mesh,
        in_specs=(
            P("ka", None, "grp"),
            P("ka", None, None),
            P("ka"),
            P("grp"),
            P("grp"),
            P(None, "grp"),
            P(),
            P(),
            P(),
            P(),
            P(),
            P(),
            P("ka", None),
            P("ka"),
        ),
        out_specs=(
            P("ka", "grp"),
            P(("grp", "ka"), None),
            P("grp", None),
            P("grp", None),
            P("grp", None),
        ),
        check_vma=False,
    )
```

profile of v0, /device:TPU:0, one launch (start us, length us, event | category | flops | bytes accessed | tf_op | source)
XLA Modules:
  0.0 241.9 jit_solution(14362213318819871211)
XLA Ops:
  7.2 0.0 copy-start
  7.2 8.9 %copy.23 = bf16[64,512,32]{0,2,1:T(8,128)(2,1)} copy(bf16[64,512,32]{1,2,0:T(8,128)(2,1)} %param.14) | data formatting | bytes 4194304 | tf_op args[0]
  16.1 7.5 %reshape.30 = bf16[16,2,32768]{2,1,0:T(2,128)(2,1)} reshape(bf16[512,32,64]{2,1,0:T(8,128)(2,1)} %bitcast.57) | data formatting | bytes 4194304
  23.6 0.0 copy-start.4
  23.6 7.5 %all-to-all-start = ((bf16[16,2,32768]{2,1,0:T(2,128)(2,1)}), bf16[16,2,32768]{2,1,0:T(2,128)(2,1)S(1)}, u32[]{:S(2)}, u32[]{:S(2)}) async-start(bf16[16,2,32768]{2,1,0:T(2,128)(2,1)} %reshape.30), calls=%async_computation | async-start | bytes 4194304 | tf_op jit(solution)/shard_map/all_to_all | solution.py:62
  31.2 0.0 reduce-scatter.4.cloned.1.call-start
  31.3 0.1 multiply_bitcast_fusion
  31.4 0.1 copy.26
  31.5 0.3 convolution_add_fusion.1
  31.7 1.0 fusion.4
  32.8 0.2 convolution_add_fusion.3
  33.1 39.2 %all-to-all-done = bf16[16,2,32768]{2,1,0:T(2,128)(2,1)S(1)} async-done(((bf16[16,2,32768]{2,1,0:T(2,128)(2,1)}), bf16[16,2,32768]{2,1,0:T(2,128)(2,1)S(1)}, u32[]{:S(2)}, u32[]{:S(2)}) %all-to-all-start) | async-done | bytes 2097184 | tf_op jit(solution)/shard_map/all_to_all | solution.py:62
  72.3 5.0 %reshape.31 = bf16[512,32,64]{2,1,0:T(8,128)(2,1)} reshape(bf16[16,2,32768]{2,1,0:T(2,128)(2,1)S(1)} %all-to-all-done) | data formatting | bytes 4194304
  77.3 9.0 %copy.24 = bf16[16,64,32,32]{1,0,3,2:T(8,128)(2,1)} copy(bf16[16,64,32,32]{1,3,2,0:T(8,128)(2,1)} %bitcast.58) | data formatting | bytes 4194304 | tf_op jit(solution)/shard_map/all_to_all | solution.py:62
  86.3 5.5 %all_to_all.16 = bf16[1024,32,32]{0,2,1:T(8,128)(2,1)S(1)} reshape(bf16[16,64,32,32]{1,0,3,2:T(8,128)(2,1)} %copy.24) | data formatting | bytes 4194304 | tf_op jit(solution)/shard_map/all_to_all | solution.py:62
  91.7 13.2 %convolution_multiply_fusion = f32[32,512,32]{1,2,0:T(8,128)S(1)} fusion(bf16[1024,32,32]{0,2,1:T(8,128)(2,1)S(1)} %all_to_all.16, bf16[32,1024,512]{2,1,0:T(8,128)(2,1)} %param.15), kind=kOutput, calls=%fused_computation.2 | convolution fusion | flops 1074266112 | bytes 37748736 | tf_op jit(solution)/shard_map/tkc,ktl->klc/dot_general | solution.py:63
  105.0 0.0 copy-start.11
  105.0 2.2 fusion
  107.3 0.8 copy.31
  108.1 0.0 reduce-scatter.4.cloned.1.call-update
  108.2 62.0 %reduce-scatter.4.cloned.1.call-done = f32[32,32]{1,0:T(8,128)} async-done(((f32[512,32]{1,0:T(8,128)}), f32[32,32]{1,0:T(8,128)}) %reduce-scatter.4.cloned.1.call-update) | async-done | bytes 4112
  170.1 0.8 copy.30
  170.9 0.1 fusion.7
  171.1 0.1 fusion.5
  171.2 57.6 %psum.7 = f32[64,32]{0,1:T(8,128)S(1)} all-reduce(f32[64,32]{0,1:T(8,128)S(1)} %fusion.5), channel_id=1, replica_groups=mesh['grp'=2,'ka'=16] {'ka'}, use_global_device_ids=true, to_apply=%region_1.2 | all-reduce | flops 2048 | bytes 16384 | tf_op jit(solution)/shard_map/psum | solution.py:81
  228.9 0.2 fusion.3
  229.1 2.0 fusion.10
  231.1 0.7 fusion.2
  231.8 1.0 fusion.13
  232.8 0.8 convolution_multiply_fusion.2
  233.6 0.7 copy.25
  234.3 0.8 fusion.20
  (26 shorter events, 0.1 us)
Async XLA Ops:
  7.2 24.6 %copy-start = (f32[512,512]{1,0:T(8,128)S(1)}, f32[512,512]{1,0:T(8,128)}, u32[]{:S(2)}) copy-start(f32[512,512]{1,0:T(8,128)} %param.22) | copy-start | bytes 3145732
  23.6 7.7 %copy-start.2 = (f32[6,32]{1,0:T(8,128)S(1)}, f32[6,32]{1,0:T(8,128)}, u32[]{:S(2)}) copy-start(f32[6,32]{1,0:T(8,128)} %param.19) | copy-start | bytes 2308
  23.6 7.7 %copy-start.7 = (s32[32]{0:T(128)S(1)}, s32[32]{0:T(128)}, u32[]{:S(2)}) copy-start(s32[32]{0:T(128)} %param.18) | copy-start | bytes 388
  23.6 7.7 %copy-start.8 = (s32[32]{0:T(128)S(1)}, s32[32]{0:T(128)}, u32[]{:S(2)}) copy-start(s32[32]{0:T(128)} %param.17) | copy-start | bytes 388
  23.6 7.9 %copy-start.3 = (f32[512,6]{0,1:T(8,128)S(1)}, f32[512,6]{0,1:T(8,128)}, u32[]{:S(2)}) copy-start(f32[512,6]{0,1:T(8,128)} %param.20) | copy-start | bytes 36868
  23.6 7.9 %copy-start.5 = (f32[512]{0:T(512)S(1)}, f32[512]{0:T(512)}, u32[]{:S(2)}) copy-start(f32[512]{0:T(512)} %param.21) | copy-start | bytes 6148
  23.6 8.1 %copy-start.4 = (f32[512]{0:T(512)S(1)}, f32[512]{0:T(512)}, u32[]{:S(2)}) copy-start(f32[512]{0:T(512)} %param.23) | copy-start | bytes 6148
  23.6 9.2 %copy-start.9 = (f32[64,512]{1,0:T(8,128)S(1)}, f32[64,512]{1,0:T(8,128)}, u32[]{:S(2)}) copy-start(f32[64,512]{1,0:T(8,128)} %param.24) | copy-start | bytes 393220
  23.6 9.2 %copy-start.10 = (f32[64]{0:T(128)S(1)}, f32[64]{0:T(128)}, u32[]{:S(2)}) copy-start(f32[64]{0:T(128)} %param.25) | copy-start | bytes 772
  23.6 48.6 %all-to-all-start = ((bf16[16,2,32768]{2,1,0:T(2,128)(2,1)}), bf16[16,2,32768]{2,1,0:T(2,128)(2,1)S(1)}, u32[]{:S(2)}, u32[]{:S(2)}) async-start(bf16[16,2,32768]{2,1,0:T(2,128)(2,1)} %reshape.30), calls=%async_computation | async-start | bytes 4194304 | tf_op jit(solution)/shard_map/all_to_all | solution.py:62
  31.2 139.0 %reduce-scatter.4.cloned.1.call-start = ((), (), s32[]{:S(2)}) async-start(), calls=%async_computation.2 | async-start | bytes 278528
  105.0 3.2 %copy-start.11 = (s32[32]{0:T(128)S(1)}, s32[32]{0:T(128)}, u32[]{:S(2)}) copy-start(s32[32]{0:T(128)} %param.16) | copy-start | bytes 388
  105.0 65.9 %copy-start.1 = (f32[32,64]{1,0:T(8,128)S(1)}, f32[32,64]{1,0:T(8,128)}, u32[]{:S(2)}) copy-start(f32[32,64]{1,0:T(8,128)} %param.26) | copy-start | bytes 24580
  105.0 65.9 %copy-start.6 = (f32[32]{0:T(128)S(1)}, f32[32]{0:T(128)}, u32[]{:S(2)}) copy-start(f32[32]{0:T(128)} %param.27) | copy-start | bytes 388
Sparse Core Ops, SparseCore 0:
  108.3 61.8 reduce-scatter.3
where the time goes:
time: 242 us
  waiting for transfers between devices  101 us (42%)
  blocking collectives  57.6 us (24%)
  local copies, waits for them, and re-layouts  38.3 us (16%)
  matrix products  22.8 us (9%)
  between operations  14.3 us (6%)
  starting transfers between devices  7.57 us (3%)
    unnamed x2, waiting for transfers between devices  62 us
    psum x1, blocking collectives, local(): coef_grad = lax.psum(coef_part, 'ka')  57.6 us
    all_to_all x1, waiting for transfers between devices, local(): lax.all_to_all(sources, 'ka', split_axis=1, concat_axis=0, tiled=True)  39.2 us
    unnamed x29, local copies, waits for them, and re-layouts  22.9 us
    all_to_all x2, local copies, waits for them, and re-layouts, local(): lax.all_to_all(sources, 'ka', split_axis=1, concat_axis=0, tiled=True)  14.5 us
    dot_general x1, matrix products, local(): jnp.einsum('tkc,ktl->klc', regrouped, bessel, preferred_element_type=jnp....  13.2 us
    all_to_all x1, starting transfers between devices, local(): lax.all_to_all(sources, 'ka', split_axis=1, concat_axis=0, tiled=True)  7.53 us
    dot_general x11, matrix products, mat(): return jnp.dot(left, right, precision=lax.Precision.HIGHEST)  7.29 us
  transfers between devices with their start and end apart: 2, of which 2 were waited for; matrix products, arithmetic and copies ran while one was open for 1% of the time, Pallas kernels for 0%

commit v1 on v0

v1 whole, which is shorter than its diff:
```python
import functools
import math

import jax
import jax.numpy as jnp
from jax import lax
from jax.experimental import pallas as pl
from jax.experimental.pallas import tpu as pltpu
from jax.sharding import PartitionSpec as P

LMAX = 5000
LANES = 128
HIGHEST = lax.Precision.HIGHEST


def silu_slope(value):
    sigma = jax.nn.sigmoid(value)
    return sigma * (1.0 + value * (1.0 - sigma))


def mat(left, right, dims=((1,), (0,))):
    return lax.dot_general(
        left, right, (dims, ((), ())), precision=HIGHEST, preferred_element_type=jnp.float32
    )


def split_two(value):
    high = value.astype(jnp.bfloat16)
    low = (value - high.astype(jnp.float32)).astype(jnp.bfloat16)
    return high, low


def arrange_kernel(source_ref, extra_ref, *refs):
    *out_refs, rows_ref, turned_ref = refs
    times, cosmos, block = source_ref.shape
    packs = LANES // times
    low_count = cosmos // packs
    owners = out_refs[0].shape[0]
    extras = extra_ref.shape[0]
    rows_ref[...] = source_ref[...].astype(jnp.float32).reshape(times * cosmos, block)
    for low in range(low_count):
        pieces = [
            rows_ref[pl.ds(high * low_count + low, times, stride=cosmos), :]
            for high in range(packs)
        ]
        turned_ref[pl.ds(low, block, stride=low_count), :] = jnp.concatenate(pieces, axis=0).T
    turned = turned_ref[...].astype(jnp.bfloat16).reshape(owners, -1, low_count, LANES)
    start = 0
    for part, out_ref in enumerate(out_refs):
        last = part == len(out_refs) - 1
        waves = out_ref.shape[1] - (extras if last else 0)
        out_ref[:, :waves] = turned[:, start : start + waves]
        start += waves
    out_refs[-1][:, waves:] = jnp.broadcast_to(extra_ref[...][None], (owners,) + extra_ref.shape)


def arrange(sources, extra, chunks):
    times, cosmos, total = sources.shape
    low_count = cosmos // (LANES // times)
    block = LANES
    waves = sum(chunks)
    slots = chunks[:-1] + (chunks[-1] + extra.shape[0],)
    return pl.pallas_call(
        arrange_kernel,
        grid=(total // block,),
        in_specs=[
            pl.BlockSpec((times, cosmos, block), lambda b: (0, 0, b)),
            pl.BlockSpec(extra.shape, lambda b: (0, 0, 0)),
        ],
        out_specs=[
            pl.BlockSpec((block // waves, count, low_count, LANES), lambda b: (b, 0, 0, 0))
            for count in slots
        ],
        out_shape=[
            jax.ShapeDtypeStruct((total // waves, count, low_count, LANES), jnp.bfloat16)
            for count in slots
        ],
        scratch_shapes=[
            pltpu.VMEM((times * cosmos, block), jnp.float32),
            pltpu.VMEM((block * low_count, LANES), jnp.float32),
        ],
        compiler_params=pltpu.CompilerParams(vmem_limit_bytes=60 << 20),
        name="arrange",
    )(sources, extra)


def add_waves(total, first, received_ref, bessel_ref, column_refs, total_waves):
    first_param_ref, second_param_ref, low_ref, high_ref = column_refs
    peers, waves = received_ref.shape[:2]
    times = bessel_ref.shape[1] // peers
    packs = LANES // times
    for wave in range(waves):
        groups = []
        for group in range(peers // packs):
            tiles = [received_ref[group * packs + peer, wave] for peer in range(packs)]
            groups.append(
                jnp.concatenate(
                    [
                        jnp.concatenate(
                            [tile[:, high * times : (high + 1) * times] for tile in tiles], axis=1
                        )
                        for high in range(packs)
                    ],
                    axis=0,
                )
            )
        source = jnp.concatenate(groups, axis=1)
        transfer = jnp.dot(source, bessel_ref[wave], preferred_element_type=jnp.float32)
        index = first + wave
        log_ratio = math.log(0.002) + index.astype(jnp.float32) * (math.log(5000.0) / total_waves)
        tilted = 0.5 * first_param_ref[...] + 0.3 * second_param_ref[...] * log_ratio
        inside = (index >= low_ref[...]) & (index < high_ref[...])
        factor = jnp.where(inside, jnp.exp(tilted), jnp.zeros_like(tilted)) / total_waves
        total = total + transfer * transfer * factor
    return total


def power_kernel(total_waves, first_ref, received_ref, bessel_ref, *refs):
    *column_refs, power_ref = refs
    step = pl.program_id(0)

    @pl.when(step == 0)
    def _():
        power_ref[...] = jnp.zeros_like(power_ref)

    first = first_ref[0] + step * received_ref.shape[1]
    power_ref[...] = add_waves(
        power_ref[...], first, received_ref, bessel_ref, column_refs, total_waves
    )


def last_kernel(total_waves, owned, first_ref, received_ref, bessel_ref, *refs):
    *column_refs, extra_ref, base_ref, so_far_ref, out_ref, power_ref = refs
    step = pl.program_id(0)
    peers = received_ref.shape[0]
    cosmos, comps = base_ref.shape

    @pl.when(step == 0)
    def _():
        power_ref[...] = so_far_ref[...]

    first = first_ref[0] + step * received_ref.shape[1]
    total = add_waves(power_ref[...], first, received_ref, bessel_ref, column_refs, total_waves)
    power_ref[...] = total

    @pl.when(step == pl.num_programs(0) - 1)
    def _():
        power_high, power_low = split_two(total)
        extra = extra_ref[...].reshape(peers, -1, LANES)
        part = base_ref[...]
        basis = jnp.concatenate([extra[peer, :owned] for peer in range(peers)], axis=0)
        basis_high, basis_low = basis[:, :comps], basis[:, comps:]
        for left, right in (
            (power_low, basis_high),
            (power_high, basis_low),
            (power_high, basis_high),
        ):
            part = part - jnp.dot(left, right, preferred_element_type=jnp.float32)
        spare = jnp.zeros((cosmos, LANES - owned - comps), jnp.float32)
        for peer in range(peers):
            own = total[:, peer * owned : (peer + 1) * owned]
            out_ref[peer] = jnp.concatenate([own, part, spare], axis=1)


def power_parts(first, received, start, waves, bessel, columns, total_waves, owned, rest=None):
    peers, slots, low_count, _ = received.shape
    times, multipoles = bessel.shape[1:]
    cosmos = columns[0].shape[0]
    block = math.gcd(math.gcd(waves, start), 4)
    whole = lambda shape: pl.BlockSpec(shape, lambda s: (0,) * len(shape))
    in_specs = [
        pl.BlockSpec(memory_space=pltpu.SMEM),
        pl.BlockSpec((peers, block, low_count, LANES), lambda s: (0, s, 0, 0)),
        pl.BlockSpec((block, times, multipoles), lambda s: (start // block + s, 0, 0)),
    ] + [whole((cosmos, 1))] * len(columns)
    operands = [first + start, received, bessel, *columns]
    if rest is None:
        kernel = functools.partial(power_kernel, total_waves)
        out_shape = (cosmos, multipoles)
        scratch = []
    else:
        extras = slots - waves
        base, so_far = rest
        kernel = functools.partial(last_kernel, total_waves, owned)
        in_specs += [
            pl.BlockSpec((peers, extras, low_count, LANES), lambda s: (0, waves // extras, 0, 0)),
            whole(base.shape),
            whole(so_far.shape),
        ]
        operands += [received, base, so_far]
        out_shape = (peers, cosmos, LANES)
        scratch = [pltpu.VMEM((cosmos, multipoles), jnp.float32)]
    return pl.pallas_call(
        kernel,
        grid=(waves // block,),
        in_specs=in_specs,
        out_specs=whole(out_shape),
        out_shape=jax.ShapeDtypeStruct(out_shape, jnp.float32),
        scratch_shapes=scratch,
        compiler_params=pltpu.CompilerParams(vmem_limit_bytes=56 << 20),
        cost_estimate=pl.CostEstimate(
            flops=2 * waves * times * multipoles * cosmos,
            bytes_accessed=2 * waves * times * multipoles,
            transcendentals=0,
        ),
        name="power_parts",
    )(*operands)


def gradients_kernel(
    parts_ref,
    params_ref,
    coeffs_ref,
    inner_act_ref,
    inner_slope_ref,
    middle_act_ref,
    middle_slope_ref,
    weight_mid_ref,
    weight_out_ref,
    basis_ref,
    offset_ref,
    smoothing_ref,
    spectra_ref,
    grad_basis_ref,
    grad_in_ref,
    grad_mid_ref,
    grad_out_ref,
):
    cosmos = params_ref.shape[1]
    owned, comps = basis_ref.shape
    summed = jnp.sum(parts_ref[...], axis=0)
    spectra = summed[:, :owned] * smoothing_ref[...]
    coef_grad = summed[:, owned : owned + comps] / cosmos
    coeffs = coeffs_ref[...]
    residual = offset_ref[...] + mat(coeffs, basis_ref[...], ((1,), (1,))) - spectra
    middle_delta = mat(coef_grad, weight_out_ref[...]) * middle_slope_ref[...]
    inner_delta = mat(middle_delta, weight_mid_ref[...]) * inner_slope_ref[...]
    rows = ((0,), (0,))
    spectra_ref[...] = spectra.T
    grad_basis_ref[...] = mat(residual, coeffs, rows) / cosmos
    grad_out_ref[...] = mat(coef_grad, middle_act_ref[...], rows)
    grad_mid_ref[...] = mat(middle_delta, inner_act_ref[...], rows)
    grad_in_ref[...] = mat(params_ref[...], inner_delta)


def gradients(parts, params, coeffs, hidden, weight_mid, weight_out, basis, offset, smoothing):
    count, cosmos = params.shape
    owned, comps = basis.shape
    width = weight_mid.shape[0]
    shape = lambda *dims: jax.ShapeDtypeStruct(dims, jnp.float32)
    return pl.pallas_call(
        gradients_kernel,
        out_shape=(
            shape(owned, cosmos),
            shape(owned, comps),
            shape(count, width),
            shape(width, width),
            shape(comps, width),
        ),
        compiler_params=pltpu.CompilerParams(vmem_limit_bytes=48 << 20),
        name="gradients",
    )(
        parts,
        params,
        coeffs,
        *hidden,
        weight_mid,
        weight_out,
        basis,
        offset.reshape(1, owned),
        smoothing.reshape(1, owned),
    )


def local(
    sources,
    bessel,
    multipoles,
    window_low,
    window_high,
    params,
    weight_in,
    bias_in,
    weight_mid,
    bias_mid,
    weight_out,
    bias_out,
    pca_basis,
    offset,
):
    waves = bessel.shape[0]
    total_waves = sources.shape[1]
    peers = total_waves // waves
    cosmos = params.shape[1]
    owned = multipoles.shape[0]

    degree = multipoles.astype(jnp.float32)
    smoothing = jnp.exp(-2.0 * degree * (degree + 1.0) / (LMAX * (LMAX + 1.0)))
    low_count = cosmos // (LANES // sources.shape[0])
    smooth_basis = smoothing[:, None] * pca_basis
    rounded = lax.reduce_precision(smooth_basis, exponent_bits=8, mantissa_bits=7)
    smooth_basis = jnp.concatenate([rounded, smooth_basis - rounded], axis=1).astype(jnp.bfloat16)
    smooth_basis = jnp.pad(smooth_basis, ((0, -owned % low_count), (0, 0)))
    extra = smooth_basis.reshape(-1, low_count, LANES)

    chunks = (waves - waves // 4, waves // 4)
    ready = arrange(jnp.transpose(sources, (0, 2, 1)), extra, chunks)
    received = [
        lax.all_to_all(part, "ka", split_axis=0, concat_axis=0, tiled=True) for part in ready
    ]

    inner_pre = mat(params.T, weight_in.T) + bias_in[None, :]
    inner_act = jax.nn.silu(inner_pre)
    middle_pre = mat(inner_act, weight_mid.T) + bias_mid[None, :]
    middle_act = jax.nn.silu(middle_pre)
    coeffs = mat(middle_act, weight_out.T) + bias_out[None, :]
    hidden = (inner_act, silu_slope(inner_pre), middle_act, silu_slope(middle_pre))
    base = mat(offset[None, :] + mat(coeffs, pca_basis.T), pca_basis)

    first = (lax.axis_index("ka") * waves).astype(jnp.int32).reshape(1)
    columns = [row.reshape(cosmos, 1) for row in (params[0], params[1], window_low, window_high)]
    power = power_parts(first, received[0], 0, chunks[0], bessel, columns, total_waves, owned)
    parts = power_parts(
        first,
        received[1],
        chunks[0],
        chunks[1],
        bessel,
        columns,
        total_waves,
        owned,
        (base, power),
    )
    gathered = lax.all_to_all(parts, "ka", split_axis=0, concat_axis=0, tiled=True)
    spectra, grad_basis, grad_in, grad_mid, grad_out = gradients(
        gathered, params, coeffs, hidden, weight_mid, weight_out, pca_basis, offset, smoothing
    )
    return (spectra, grad_basis, grad_in.T, grad_mid, grad_out)


def solution(mesh):
    return jax.shard_map(
        local,
        mesh=mesh,
        in_specs=(
            P("ka", None, "grp"),
            P("ka", None, None),
            P("ka"),
            P("grp"),
            P("grp"),
            P(None, "grp"),
            P(),
            P(),
            P(),
            P(),
            P(),
            P(),
            P("ka", None),
            P("ka"),
        ),
        out_specs=(
            P("ka", "grp"),
            P(("grp", "ka"), None),
            P("grp", None),
            P("grp", None),
            P("grp", None),
        ),
        check_vma=False,
    )
```

time: 242 us -> 98.2 us (0.41)
  waiting for transfers between devices: 101 us -> 41.3 us
  blocking collectives: 57.6 us -> 0 us
  local copies, waits for them, and re-layouts: 38.3 us -> 2.83 us
  Pallas kernels: 0 us -> 26.5 us
  matrix products: 22.8 us -> 2.5 us
  starting transfers between devices: 7.57 us -> 21.5 us
  between operations: 14.3 us -> 0.86 us
    unnamed x2 -> x0, waiting for transfers between devices: 62 us -> none
    psum x1 -> x0, blocking collectives: 57.6 us -> none  [local(): coef_grad = lax.psum(coef_part, 'ka')]
    pallas_call x0 -> x4, Pallas kernels: none -> 26.5 us  [the longest x2 17.6 us: power_parts(): pl.pallas_call(kernel, grid=(waves // block,), in_specs=in_specs, out_spe...]
    unnamed x29 -> x26, local copies, waits for them, and re-layouts: 22.9 us -> 0.07 us
    dot_general x13 -> x5, matrix products: 22.8 us -> 2.5 us  [mat(): lax.dot_general(left, right, (dims, ((), ())), precision=HIGHEST, preferr...]
    all_to_all x2 -> x0, local copies, waits for them, and re-layouts: 14.5 us -> none  [local(): lax.all_to_all(sources, 'ka', split_axis=1, concat_axis=0, tiled=True)]
    all_to_all x1 -> x3, starting transfers between devices: 7.53 us -> 21.5 us  [the longest x2 16.7 us: local(): lax.all_to_all(part, 'ka', split_axis=0, concat_axis=0, tiled=True)]
    all_to_all x1 -> x3, waiting for transfers between devices: 39.2 us -> 41.3 us  [the longest x2 31.3 us: local(): lax.all_to_all(part, 'ka', split_axis=0, concat_axis=0, tiled=True)]
  transfers between devices with their start and end apart: 2 -> 3, of which waited for: 2 -> 3; matrix products, arithmetic and copies ran while one was open for 1% -> 5% of each run, Pallas kernels for 0% -> 12%
where the time goes in v1:
time: 98.2 us; the launch traced here: 97.6 us
  waiting for transfers between devices  41.3 us (42%)
  Pallas kernels  26.5 us (27%)
  starting transfers between devices  21.5 us (22%)
  local copies, waits for them, and re-layouts  2.83 us (3%)
  matrix products  2.5 us (3%)
  other arithmetic  2.15 us (2%)
    all_to_all x2, waiting for transfers between devices, local(): lax.all_to_all(part, 'ka', split_axis=0, concat_axis=0, tiled=True)  31.3 us
    pallas_call x2, Pallas kernels, power_parts(): pl.pallas_call(kernel, grid=(waves // block,), in_specs=in_specs, out_spe...  17.6 us
    all_to_all x2, starting transfers between devices, local(): lax.all_to_all(part, 'ka', split_axis=0, concat_axis=0, tiled=True)  16.7 us
    all_to_all x1, waiting for transfers between devices, local(): lax.all_to_all(parts, 'ka', split_axis=0, concat_axis=0, tiled=True)  10 us
    pallas_call x1, Pallas kernels, arrange(): pl.pallas_call(arrange_kernel, grid=(total // block,), in_specs=[pl.Block...  6.01 us
    all_to_all x1, starting transfers between devices, local(): lax.all_to_all(parts, 'ka', split_axis=0, concat_axis=0, tiled=True)  4.77 us
    pallas_call x1, Pallas kernels, gradients(): pl.pallas_call(gradients_kernel, out_shape=(shape(owned, cosmos), shape(o...  2.9 us
    dot_general x5, matrix products, mat(): lax.dot_general(left, right, (dims, ((), ())), precision=HIGHEST, preferr...  2.5 us
  transfers between devices with their start and end apart: 3, of which 3 were waited for; matrix products, arithmetic and copies ran while one was open for 5% of the time, Pallas kernels for 12%

profile of v1, /device:TPU:0, one launch (start us, length us, event | category | flops | bytes accessed | tf_op | source)
XLA Modules:
  0.0 97.6 jit_solution(16076648552578854615)
XLA Ops:
  0.6 0.0 copy-start
  0.6 0.7 multiply_exponential_fusion
  1.3 0.8 reduce-precision_convert_fusion
  2.1 0.7 pad_maximum_fusion.extra_ref
  2.8 6.0 %arrange.1 = (bf16[16,24,16,128]{3,2,1,0:T(8,128)(2,1)}, bf16[16,10,16,128]{3,2,1,0:T(8,128)(2,1)}) custom-call(bf16[64,32,512]{2,1,0:T(8,128)(2,1)} %bitcast.23, bf16[2,16,128]{2,1,0:T(8,128)(2,1)} %pad_maximum_fusion.extra_ref), custom_call_target="tpu_custom_call" | custom-call | tf_op jit(solution)/shard_map/arrange/pallas_call | solution.py:63
  8.8 0.0 copy-start.10
  8.8 0.0 copy-start.1
  8.8 0.0 copy-start.7
  8.8 7.5 %all-to-all-start.1 = ((bf16[16,24,16,128]{3,2,1,0:T(8,128)(2,1)}), bf16[16,24,16,128]{3,2,1,0:T(8,128)(2,1)S(1)}, u32[]{:S(2)}, u32[]{:S(2)}) async-start(bf16[16,24,16,128]{3,2,1,0:T(8,128)(2,1)} %get-tuple-element.13), calls=%async_computation.1 | async-start | bytes 3145728 | tf_op jit(solution)/shard_map/all_to_all | solution.py:309
  16.4 0.0 copy-start.3
  16.4 0.0 copy-start.11
  16.4 0.0 copy-start.2
  16.4 0.0 copy-start.5
  16.4 0.0 copy-done.4
  16.5 0.7 copy.23.refs_0_
  17.1 0.7 copy.24.refs_1_
  17.8 0.0 copy-done.8
  17.8 0.7 copy.25.refs_2_
  18.5 0.7 copy.26.refs_3_
  19.2 29.1 %all-to-all-done.1.received_ref = bf16[16,24,16,128]{3,2,1,0:T(8,128)(2,1)S(1)} async-done(((bf16[16,24,16,128]{3,2,1,0:T(8,128)(2,1)}), bf16[16,24,16,128]{3,2,1,0:T(8,128)(2,1)S(1)}, u32[]{:S(2)}, u32[]{:S(2)}) %all-to-all-start.1) | async-done | bytes 1572896 | tf_op jit(solution)/shard_map/all_to_all | solution.py:309
  48.4 9.2 %all-to-all-start = ((bf16[16,10,16,128]{3,2,1,0:T(8,128)(2,1)}), bf16[16,10,16,128]{3,2,1,0:T(8,128)(2,1)}, u32[]{:S(2)}, u32[]{:S(2)}) async-start(bf16[16,10,16,128]{3,2,1,0:T(8,128)(2,1)} %get-tuple-element.12), calls=%async_computation | async-start | bytes 1310720 | tf_op jit(solution)/shard_map/all_to_all | solution.py:309
  57.5 0.3 add_multiply_fusion.1
  57.9 1.1 %add_multiply_fusion = (f32[32,512]{1,0:T(8,128)S(1)}, f32[32,512]{1,0:T(8,128)S(1)}, f32[32,512]{1,0:T(8,128)S(1)}) fusion(f32[512]{0:T(512)S(1)} %copy-done.7, f32[512,512]{1,0:T(8,128)S(1)} %copy-done.1, f32[32,512]{1,0:T(8,128)S(1)} %get-tuple-element.27), kind=kOutput, calls=%fused_computation.4 | convolution fusion | flops 100876288 | bytes 1312768 | tf_op jit(solution)/shard_map/dot_general | solution.py:22
  59.0 0.2 convolution_add_fusion.3.coeffs_ref
  59.2 0.1 convolution_add_fusion.2
  59.4 0.8 fusion.5.refs_5_
  60.1 11.9 %power_parts.2.refs_6_ = f32[32,512]{1,0:T(8,128)} custom-call(s32[1]{0:T(128)} %bitcast.first_ref, bf16[16,24,16,128]{3,2,1,0:T(8,128)(2,1)} %copy-done.6, bf16[32,1024,512]{2,1,0:T(8,128)(2,1)} %bessel_ref.3, f32[32,1]{1,0:T(8,128)} %copy.23.refs_0_, f32[32,1]{1,0:T(8,128)} %copy.24.refs_1_, s32[32,1]{1,0:T(8,128)} %copy.25.refs_2_, s32[32,1]{1,0:T(8,128)} %copy.26.refs_3_), custom_call_target="tpu_custom_call" | custom-call | flops 805306368 | bytes 25165824 | tf_op jit(solution)/shard_map/power_parts/pallas_call | solution.py:193
  72.1 2.1 %all-to-all-done.received_ref.refs_4_ = bf16[16,10,16,128]{3,2,1,0:T(8,128)(2,1)} async-done(((bf16[16,10,16,128]{3,2,1,0:T(8,128)(2,1)}), bf16[16,10,16,128]{3,2,1,0:T(8,128)(2,1)}, u32[]{:S(2)}, u32[]{:S(2)}) %all-to-all-start) | async-done | bytes 655392 | tf_op jit(solution)/shard_map/all_to_all | solution.py:309
  74.2 5.7 %power_parts.3 = f32[16,32,128]{2,1,0:T(8,128)} custom-call(s32[1]{0:T(128)S(6)} %add.56.first_ref, bf16[16,10,16,128]{3,2,1,0:T(8,128)(2,1)} %all-to-all-done.received_ref.refs_4_, bf16[32,1024,512]{2,1,0:T(8,128)(2,1)} %bessel_ref.3, f32[32,1]{1,0:T(8,128)} %copy.23.refs_0_, f32[32,1]{1,0:T(8,128)} %copy.24.refs_1_, s32[32,1]{1,0:T(8,128)} %copy.25.refs_2_, ...), custom_call_target="tpu_custom_call" | custom-call | flops 268435456 | bytes 8388608 | tf_op jit(solution)/shard_map/power_parts/pallas_call | solution.py:193
  79.9 4.8 %all-to-all-start.2 = ((f32[16,32,128]{2,1,0:T(8,128)}), f32[16,32,128]{2,1,0:T(8,128)S(1)}, u32[]{:S(2)}, u32[]{:S(2)}) async-start(f32[16,32,128]{2,1,0:T(8,128)} %power_parts.3), calls=%async_computation.2 | async-start | bytes 524288 | tf_op jit(solution)/shard_map/all_to_all | solution.py:334
  84.7 10.0 %all-to-all-done.2.parts_ref = f32[16,32,128]{2,1,0:T(8,128)S(1)} async-done(((f32[16,32,128]{2,1,0:T(8,128)}), f32[16,32,128]{2,1,0:T(8,128)S(1)}, u32[]{:S(2)}, u32[]{:S(2)}) %all-to-all-start.2) | async-done | bytes 262176 | tf_op jit(solution)/shard_map/all_to_all | solution.py:334
  94.7 2.9 %gradients.1 = (f32[32,32]{1,0:T(8,128)}, f32[32,64]{1,0:T(8,128)}, f32[6,512]{1,0:T(8,128)}, f32[512,512]{1,0:T(8,128)}, f32[64,512]{1,0:T(8,128)}) custom-call(f32[16,32,128]{2,1,0:T(8,128)S(1)} %all-to-all-done.2.parts_ref, f32[6,32]{1,0:T(8,128)S(1)} %copy-done.4, f32[32,64]{1,0:T(8,128)S(1)} %convolution_add_fusion.3.coeffs_ref, ...), custom_call_target="tpu_custom_call" | custom-call | tf_op jit(solution)/shard_map/gradients/pallas_call | solution.py:251
  (18 shorter events, 0.0 us)
Async XLA Ops:
  0.6 56.9 %copy-start = (f32[512,6]{0,1:T(8,128)S(1)}, f32[512,6]{0,1:T(8,128)}, u32[]{:S(2)}) copy-start(f32[512,6]{0,1:T(8,128)} %param.20) | copy-start | bytes 36868
  8.8 7.6 %copy-start.4 = (f32[6,32]{1,0:T(8,128)S(1)}, f32[6,32]{1,0:T(8,128)}, u32[]{:S(2)}) copy-start(f32[6,32]{1,0:T(8,128)} %params_ref.1) | copy-start | bytes 2308
  8.8 9.0 %copy-start.8 = (s32[32]{0:T(128)S(1)}, s32[32]{0:T(128)}, u32[]{:S(2)}) copy-start(s32[32]{0:T(128)} %param.17) | copy-start | bytes 388
  8.8 9.7 %copy-start.9 = (s32[32]{0:T(128)S(1)}, s32[32]{0:T(128)}, u32[]{:S(2)}) copy-start(s32[32]{0:T(128)} %param.18) | copy-start | bytes 388
  8.8 48.7 %copy-start.10 = (f32[512]{0:T(512)S(1)}, f32[512]{0:T(512)}, u32[]{:S(2)}) copy-start(f32[512]{0:T(512)} %param.21) | copy-start | bytes 6148
  8.8 49.0 %copy-start.1 = (f32[512,512]{1,0:T(8,128)S(1)}, f32[512,512]{1,0:T(8,128)}, u32[]{:S(2)}) copy-start(f32[512,512]{1,0:T(8,128)} %weight_mid_ref.1) | copy-start | bytes 3145732
  8.8 49.0 %copy-start.7 = (f32[512]{0:T(512)S(1)}, f32[512]{0:T(512)}, u32[]{:S(2)}) copy-start(f32[512]{0:T(512)} %param.23) | copy-start | bytes 6148
  8.8 39.5 %all-to-all-start.1 = ((bf16[16,24,16,128]{3,2,1,0:T(8,128)(2,1)}), bf16[16,24,16,128]{3,2,1,0:T(8,128)(2,1)S(1)}, u32[]{:S(2)}, u32[]{:S(2)}) async-start(bf16[16,24,16,128]{3,2,1,0:T(8,128)(2,1)} %get-tuple-element.13), calls=%async_computation.1 | async-start | bytes 3145728 | tf_op jit(solution)/shard_map/all_to_all | solution.py:309
  16.4 42.6 %copy-start.3 = (f32[64,512]{1,0:T(8,128)S(1)}, f32[64,512]{1,0:T(8,128)}, u32[]{:S(2)}) copy-start(f32[64,512]{1,0:T(8,128)} %weight_out_ref.1) | copy-start | bytes 393220
  16.4 42.6 %copy-start.11 = (f32[64]{0:T(128)S(1)}, f32[64]{0:T(128)}, u32[]{:S(2)}) copy-start(f32[64]{0:T(128)} %param.25) | copy-start | bytes 772
  16.4 42.8 %copy-start.2 = (f32[32,64]{1,0:T(8,128)S(1)}, f32[32,64]{1,0:T(8,128)}, u32[]{:S(2)}) copy-start(f32[32,64]{1,0:T(8,128)} %basis_ref.1) | copy-start | bytes 24580
  16.4 42.8 %copy-start.5 = (f32[32]{0:T(128)S(1)}, f32[32]{0:T(128)}, u32[]{:S(2)}) copy-start(f32[32]{0:T(128)} %param.27) | copy-start | bytes 388
  48.4 11.8 %copy-start.6 = (bf16[16,24,16,128]{3,2,1,0:T(8,128)(2,1)}, bf16[16,24,16,128]{3,2,1,0:T(8,128)(2,1)S(1)}, u32[]{:S(2)}) copy-start(bf16[16,24,16,128]{3,2,1,0:T(8,128)(2,1)S(1)} %all-to-all-done.1.received_ref) | copy-start | bytes 4718596
  48.4 25.8 %all-to-all-start = ((bf16[16,10,16,128]{3,2,1,0:T(8,128)(2,1)}), bf16[16,10,16,128]{3,2,1,0:T(8,128)(2,1)}, u32[]{:S(2)}, u32[]{:S(2)}) async-start(bf16[16,10,16,128]{3,2,1,0:T(8,128)(2,1)} %get-tuple-element.12), calls=%async_computation | async-start | bytes 1310720 | tf_op jit(solution)/shard_map/all_to_all | solution.py:309
  72.1 12.6 %copy-start.12 = (s32[32]{0:T(128)S(1)}, s32[32]{0:T(128)}, u32[]{:S(2)}) copy-start(s32[32]{0:T(128)} %param.16) | copy-start | bytes 388
  79.9 14.8 %all-to-all-start.2 = ((f32[16,32,128]{2,1,0:T(8,128)}), f32[16,32,128]{2,1,0:T(8,128)S(1)}, u32[]{:S(2)}, u32[]{:S(2)}) async-start(f32[16,32,128]{2,1,0:T(8,128)} %power_parts.3), calls=%async_computation.2 | async-start | bytes 524288 | tf_op jit(solution)/shard_map/all_to_all | solution.py:334

commit v2 on v0

v2 whole, which is shorter than its diff:
```python
import functools
import math

import jax
import jax.numpy as jnp
from jax import lax
from jax.experimental import pallas as pl
from jax.experimental.pallas import tpu as pltpu
from jax.sharding import PartitionSpec as P

LMAX = 5000
LANES = 128
TOPS = (2, 1, 0, 3)
HIGHEST = lax.Precision.HIGHEST


def silu_slope(value):
    sigma = jax.nn.sigmoid(value)
    return sigma * (1.0 + value * (1.0 - sigma))


def mat(left, right, dims=((1,), (0,))):
    return lax.dot_general(
        left, right, (dims, ((), ())), precision=HIGHEST, preferred_element_type=jnp.float32
    )


def split_two(value):
    high = value.astype(jnp.bfloat16)
    low = (value - high.astype(jnp.float32)).astype(jnp.bfloat16)
    return high, low


def smoothing_of(multipoles):
    degree = multipoles.astype(jnp.float32)
    return jnp.exp(-2.0 * degree * (degree + 1.0) / (LMAX * (LMAX + 1.0)))


def column(row):
    return jnp.broadcast_to(row.astype(jnp.float32), (8, row.shape[1])).T[:, :1]


def smooth_basis(multipoles_ref, basis_ref, low_count):
    value = column(smoothing_of(multipoles_ref[...])) * basis_ref[...]
    value = jnp.concatenate([part.astype(jnp.float32) for part in split_two(value)], axis=1)
    spare = -value.shape[0] % low_count
    if spare:
        value = jnp.concatenate([value, jnp.zeros((spare, LANES), jnp.float32)], axis=0)
    return value.astype(jnp.bfloat16).reshape(-1, low_count, LANES)


def arrange_kernel(group, last, waves, source_ref, multipoles_ref, basis_ref, *refs):
    *out_refs, block_ref, rows_ref, turned_ref, sems = refs
    blocks, times, cosmos, block = block_ref.shape
    packs = LANES // times
    low_count = cosmos // packs
    size = waves * low_count
    me = lax.axis_index("ka")
    copies = []
    for slot, top in enumerate(TOPS):
        start = pl.multiple_of(((me // group) ^ top) * block, block)
        copy = pltpu.make_async_copy(
            source_ref.at[:, :, pl.ds(start, block)], block_ref.at[slot], sems.at[slot]
        )
        copy.start()
        copies.append(copy)
    extra = smooth_basis(multipoles_ref, basis_ref, low_count)
    for slot, copy in enumerate(copies):
        copy.wait()
        rows_ref[...] = block_ref[slot].astype(jnp.float32).reshape(times * cosmos, block)
        for low in range(low_count):
            pieces = [
                rows_ref[pl.ds(high * low_count + low, times, stride=cosmos), :]
                for high in range(packs)
            ]
            turned_ref[pl.ds(low, block, stride=low_count), :] = jnp.concatenate(pieces, axis=0).T
        for peer in range(group):
            start = pl.multiple_of((peer ^ (me % group)) * size, size)
            piece = turned_ref[pl.ds(start, size), :].astype(jnp.bfloat16)
            piece = piece.reshape(waves, low_count, LANES)
            chip, core = TOPS[slot] * group // 2 + peer // 2, peer % 2
            if chip in (0, last):
                out_ref = out_refs[-1].at[int(chip == last)] if core else out_refs[chip]
                out_ref[:waves] = piece
                out_ref[waves:] = extra
            else:
                out_refs[chip][core * waves : (core + 1) * waves] = piece
                out_refs[chip][2 * waves :] = extra


def arrange(sources, multipoles, basis, waves, group, last):
    times, cosmos, total = sources.shape
    low_count = cosmos // (LANES // times)
    block = waves * group
    extras = -(-basis.shape[0] // low_count)
    one, two = (count * waves + extras for count in (1, 2))
    chips = total // waves // 2
    shapes = [(one if chip in (0, last) else two, low_count, LANES) for chip in range(chips)]
    shapes.append((2, one, low_count, LANES))
    vmem = pl.BlockSpec(memory_space=pltpu.VMEM)
    return pl.pallas_call(
        functools.partial(arrange_kernel, group, last, waves),
        in_specs=[pl.BlockSpec(memory_space=pl.ANY), vmem, vmem],
        out_specs=[vmem] * len(shapes),
        out_shape=[jax.ShapeDtypeStruct(shape, jnp.bfloat16) for shape in shapes],
        scratch_shapes=[
            pltpu.VMEM((len(TOPS), times, cosmos, block), jnp.bfloat16),
            pltpu.VMEM((times * cosmos, block), jnp.float32),
            pltpu.VMEM((block * low_count, LANES), jnp.float32),
            pltpu.SemaphoreType.DMA((len(TOPS),)),
        ],
        compiler_params=pltpu.CompilerParams(vmem_limit_bytes=24 << 20),
        cost_estimate=pl.CostEstimate(
            flops=0, bytes_accessed=16 * times * cosmos * total, transcendentals=0
        ),
        name="arrange",
    )(sources, multipoles, basis)


def source_rows(stage_ref, wave, times):
    tiles = [stage_ref[peer, wave] for peer in range(stage_ref.shape[0])]
    rows = [
        jnp.concatenate([tile[:, start : start + times] for tile in tiles], axis=1)
        for start in range(0, LANES, times)
    ]
    return jnp.concatenate(rows, axis=0)


def transfer_kernel(group, chips, times, me_ref, *refs):
    count = len(chips) * 2
    pieces, extras, refs = refs[:count], refs[count : 2 * count], refs[2 * count :]
    *bessel_refs, whole_ref, out_ref, held_ref, basis_ref, stage_ref, sem = refs
    me = me_ref[0]
    span = held_ref.shape[1]
    start = pl.multiple_of(((me // group) ^ TOPS[-1]) * span, span)
    copy = pltpu.make_async_copy(whole_ref.at[:, pl.ds(start, span), :], held_ref, sem)
    step = pl.program_id(0)

    @pl.when(step == 0)
    def _():
        copy.start()
        for number, extra_ref in enumerate(extras):
            apart = chips[number // 2] * 2 + number % 2
            basis_ref[apart] = extra_ref[...].reshape(basis_ref.shape[1:])

    for number in range(count):
        stage_ref[number // group, (number % group) ^ (me % group)] = pieces[number][...]
    for wave in range(out_ref.shape[0]):
        total = None
        for number, bessel_ref in enumerate(bessel_refs):
            part = jnp.dot(
                source_rows(stage_ref.at[number], wave, times),
                bessel_ref[wave],
                preferred_element_type=jnp.float32,
            )
            total = part if total is None else total + part
        out_ref[wave] = total
    pl.when(step == pl.num_programs(0) - 1)(copy.wait)


def tiles_spec(array, lead, start, size, moves):
    rest = array.shape[-2:]
    index = lambda s, me: (start // size + s * moves, 0, 0)
    if lead is None:
        return pl.BlockSpec((size,) + rest, index)
    return pl.BlockSpec((None, size) + rest, lambda s, me: (lead,) + index(s, me))


def add_groups(me, group, chips, members, bessel, times, extras):
    low_count = members[0][0].shape[-2]
    waves, _, multipoles = bessel.shape
    cosmos = low_count * (LANES // times)
    block = math.gcd(waves, 8)
    in_specs = [tiles_spec(array, lead, at, block, 1) for array, lead, at, _ in members]
    in_specs += [tiles_spec(array, lead, at, extras, 0) for array, lead, _, at in members]

    span = group * times
    in_specs += [
        pl.BlockSpec((block, span, multipoles), lambda s, me, top=top: (s, (me[0] // group) ^ top, 0))
        for top in TOPS[:-1]
    ]
    in_specs.append(pl.BlockSpec(memory_space=pl.ANY))
    arrays = [member[0] for member in members]
    basis = (len(members) + group, extras * low_count, LANES)
    return pl.pallas_call(
        functools.partial(transfer_kernel, group, chips, times),
        grid_spec=pltpu.PrefetchScalarGridSpec(
            num_scalar_prefetch=1,
            grid=(waves // block,),
            in_specs=in_specs,
            out_specs=[
                pl.BlockSpec((block, cosmos, multipoles), lambda s, me: (s, 0, 0)),
                pl.BlockSpec(memory_space=pltpu.VMEM),
                pl.BlockSpec(basis, lambda s, me: (0, 0, 0)),
            ],
            scratch_shapes=[
                pltpu.VMEM((len(TOPS) - 1, group, block, low_count, LANES), jnp.bfloat16),
                pltpu.SemaphoreType.DMA,
            ],
        ),
        out_shape=[
            jax.ShapeDtypeStruct((waves, cosmos, multipoles), jnp.float32),
            jax.ShapeDtypeStruct((waves, span, multipoles), bessel.dtype),
            jax.ShapeDtypeStruct(basis, jnp.bfloat16),
        ],
        compiler_params=pltpu.CompilerParams(vmem_limit_bytes=24 << 20),
        cost_estimate=pl.CostEstimate(
            flops=16 * math.prod(bessel.shape) * cosmos,
            bytes_accessed=2 * math.prod(bessel.shape),
            transcendentals=0,
        ),
        name="transfer",
    )(me, *arrays, *arrays, *[bessel] * len(TOPS))


def power_kernel(times, chips, total_waves, *refs):
    piece_refs, traded_ref, held_ref, rest_ref, *refs = refs[: len(chips)], *refs[len(chips) :]
    params_ref, low_ref, high_ref, basis_ref, base_ref, out_ref, stage_ref, all_ref = refs
    waves, cosmos, multipoles = rest_ref.shape
    comps = base_ref.shape[1]
    peers = all_ref.shape[0]
    owned = multipoles // peers
    group = 2 * len(chips)
    extras = traded_ref.shape[1] - waves
    me = lax.axis_index("ka")
    all_ref[...] = basis_ref[...]
    for low, (chip, piece_ref) in enumerate(zip(chips, piece_refs)):
        joined = low == len(chips) - 1
        for core in range(2):
            if core and not joined:
                piece, extra = traded_ref[low, :waves], traded_ref[low, waves:]
            else:
                start = 2 * waves + core * extras
                piece, extra = piece_ref[core * waves : (core + 1) * waves], piece_ref[start : start + extras]
            stage_ref[(2 * low + core) ^ (me % group)] = piece
            all_ref[2 * chip + core] = extra.reshape(all_ref.shape[1:])
    first_param, second_param = column(params_ref[0:1]), column(params_ref[1:2])
    low, high = column(low_ref[...]), column(high_ref[...])
    total = jnp.zeros((cosmos, multipoles), jnp.float32)
    for wave in range(waves):
        transfer = rest_ref[wave] + jnp.dot(
            source_rows(stage_ref, wave, times),
            held_ref[wave],
            preferred_element_type=jnp.float32,
        )
        index = (me * waves + wave).astype(jnp.float32)
        log_ratio = math.log(0.002) + index * (math.log(5000.0) / total_waves)
        tilted = 0.5 * first_param + 0.3 * second_param * log_ratio
        inside = (index >= low) & (index < high)
        factor = jnp.where(inside, jnp.exp(tilted), jnp.zeros_like(tilted)) / total_waves
        total = total + transfer * transfer * factor

    basis = jnp.concatenate([all_ref[peer ^ me][:owned] for peer in range(peers)], axis=0)
    power_high, power_low = split_two(total)
    basis_high, basis_low = basis[:, :comps], basis[:, comps:]
    part = base_ref[...]
    for left, right in (
        (power_low, basis_high),
        (power_high, basis_low),
        (power_high, basis_high),
    ):
        part = part - jnp.dot(left, right, preferred_element_type=jnp.float32)
    for peer in range(peers):
        own = total[:, peer * owned : (peer + 1) * owned]
        out_ref[peer] = fold(jnp.concatenate([own, part], axis=1))


def power_parts(pieces, traded, held, rest, times, chips, total_waves, extra):
    low_count = traded.shape[2]
    waves, cosmos, multipoles = rest.shape
    basis, base = extra[-2:]
    peers = basis.shape[0]
    operands = [*pieces, traded, held, rest, *extra]
    rows = folded_rows(cosmos, multipoles // peers + base.shape[1])
    return pl.pallas_call(
        functools.partial(power_kernel, times, chips, total_waves),
        in_specs=[pl.BlockSpec(memory_space=pltpu.VMEM)] * len(operands),
        out_specs=pl.BlockSpec(memory_space=pltpu.VMEM),
        out_shape=jax.ShapeDtypeStruct((peers, rows, LANES), jnp.float32),
        scratch_shapes=[
            pltpu.VMEM((2 * len(chips), waves, low_count, LANES), jnp.bfloat16),
            pltpu.VMEM(basis.shape, jnp.bfloat16),
        ],
        compiler_params=pltpu.CompilerParams(vmem_limit_bytes=24 << 20),
        cost_estimate=pl.CostEstimate(
            flops=16 * waves * held.shape[1] * multipoles * cosmos,
            bytes_accessed=2 * waves * held.shape[1] * multipoles,
            transcendentals=0,
        ),
        name="power",
    )(*operands)


def folds(rows, width):
    spare = LANES - width
    strips = width // spare if spare and width % spare == 0 else 0
    return strips if rows % (8 * (strips + 1)) == 0 else 0


def fold(value):
    rows, width = value.shape
    strips = folds(rows, width)
    if not strips:
        return jnp.concatenate([value, jnp.zeros((rows, LANES - width), value.dtype)], axis=1)
    spare = LANES - width
    head = rows * strips // (strips + 1)
    tail = [value[head:, strip * spare : (strip + 1) * spare] for strip in range(strips)]
    return jnp.concatenate([value[:head], jnp.concatenate(tail, axis=0)], axis=1)


def unfold(value, rows, width):
    strips = folds(rows, width)
    if not strips:
        return value[:, :width]
    size = rows // (strips + 1)
    tail = [value[strip * size : (strip + 1) * size, width:] for strip in range(strips)]
    return jnp.concatenate([value[:, :width], jnp.concatenate(tail, axis=1)], axis=0)


def folded_rows(rows, width):
    strips = folds(rows, width)
    return rows * strips // (strips + 1) if strips else rows


def gradients_kernel(
    parts_ref,
    params_ref,
    coeffs_ref,
    inner_act_ref,
    inner_slope_ref,
    middle_act_ref,
    middle_slope_ref,
    weight_mid_ref,
    weight_out_ref,
    basis_ref,
    offset_ref,
    multipoles_ref,
    spectra_ref,
    grad_basis_ref,
    grad_in_ref,
    grad_mid_ref,
    grad_out_ref,
):
    cosmos = params_ref.shape[1]
    owned, comps = basis_ref.shape
    summed = unfold(jnp.sum(parts_ref[...], axis=0), cosmos, owned + comps)
    spectra = summed[:, :owned] * smoothing_of(multipoles_ref[...])
    coef_grad = summed[:, owned : owned + comps] / cosmos
    coeffs = coeffs_ref[...]
    residual = offset_ref[...] + mat(coeffs, basis_ref[...], ((1,), (1,))) - spectra
    middle_delta = mat(coef_grad, weight_out_ref[...]) * middle_slope_ref[...]
    inner_delta = mat(middle_delta, weight_mid_ref[...]) * inner_slope_ref[...]
    rows = ((0,), (0,))
    spectra_ref[...] = spectra.T
    grad_basis_ref[...] = mat(residual, coeffs, rows) / cosmos
    grad_out_ref[...] = mat(coef_grad, middle_act_ref[...], rows)
    grad_mid_ref[...] = mat(middle_delta, inner_act_ref[...], rows)
    grad_in_ref[...] = mat(params_ref[...], inner_delta)


def gradients(parts, params, coeffs, hidden, weight_mid, weight_out, basis, offset, multipoles):
    count, cosmos = params.shape
    owned, comps = basis.shape
    width = weight_mid.shape[0]
    shape = lambda *dims: jax.ShapeDtypeStruct(dims, jnp.float32)
    return pl.pallas_call(
        gradients_kernel,
        out_shape=(
            shape(owned, cosmos),
            shape(owned, comps),
            shape(count, width),
            shape(width, width),
            shape(comps, width),
        ),
        compiler_params=pltpu.CompilerParams(vmem_limit_bytes=48 << 20),
        name="gradients",
    )(
        parts,
        params,
        coeffs,
        *hidden,
        weight_mid,
        weight_out,
        basis,
        offset.reshape(1, owned),
        multipoles,
    )


def exchange(value, apart, peers):
    return lax.ppermute(value, "ka", [(peer, peer ^ apart) for peer in range(peers)])


def after(value, *others):
    return lax.optimization_barrier((value, *others))[0]


def local(
    sources,
    bessel,
    multipoles,
    window_low,
    window_high,
    params,
    weight_in,
    bias_in,
    weight_mid,
    bias_mid,
    weight_out,
    bias_out,
    pca_basis,
    offset,
):
    waves = bessel.shape[0]
    total_waves = sources.shape[1]
    peers = total_waves // waves
    cosmos = params.shape[1]
    owned = multipoles.shape[0]
    group = LANES // waves
    half = group // 2
    times = sources.shape[0]
    extras = -(-owned // (cosmos * times // LANES))
    me = lax.axis_index("ka").astype(jnp.int32).reshape(1)
    own_multipoles = multipoles.reshape(1, owned)
    turned = jnp.transpose(sources, (0, 2, 1))

    chips = [top * half + low for top in TOPS for low in range(half)]
    late, last = chips[-half:], chips[-1]
    *ready, give = arrange(turned, own_multipoles, pca_basis, waves, group, last)
    given = exchange(give, 1, peers)
    got = {}
    near = [chip for chip in chips if 0 < chip < half]
    for chip in chips:
        if chip in (0, last):
            continue
        value = ready[chip]
        if chip in near:
            value = after(value, got[half + near.index(chip)])
        got[chip] = exchange(value, 2 * chip, peers)
    mine, other = ready[last], given[1]
    value = jnp.concatenate([mine[:waves], other[:waves], mine[waves:], other[waves:]])
    got[last] = exchange(value, 2 * last, peers)

    others = lambda part, *then: jnp.stack([after(got[chip], *then)[waves:] for chip in part])
    early = [chip for chip in chips[:-half] if chip]
    traded = exchange(others(early), 1, peers)
    members = []
    for chip in chips[:-half]:
        if chip:
            members += [(got[chip], None, 0, 2 * waves), (traded, early.index(chip), 0, waves)]
        else:
            members += [(ready[0], None, 0, waves), (given, 0, 0, waves)]
    rest, held, basis = add_groups(me, group, chips[:-half], members, bessel, times, extras)
    late_traded = exchange(others(late[:-1], rest), 1, peers)

    inner_pre = mat(params.T, weight_in.T) + bias_in[None, :]
    inner_act = jax.nn.silu(inner_pre)
    middle_pre = mat(inner_act, weight_mid.T) + bias_mid[None, :]
    middle_act = jax.nn.silu(middle_pre)
    coeffs = mat(middle_act, weight_out.T) + bias_out[None, :]
    hidden = (inner_act, silu_slope(inner_pre), middle_act, silu_slope(middle_pre))
    base = mat(offset[None, :] + mat(coeffs, pca_basis.T), pca_basis)

    extra = (params, window_low.reshape(1, cosmos), window_high.reshape(1, cosmos), basis, base)
    pieces = [got[chip] for chip in late]
    parts = power_parts(pieces, late_traded, held, rest, times, late, total_waves, extra)
    gathered = lax.all_to_all(parts, "ka", split_axis=0, concat_axis=0, tiled=True)
    spectra, grad_basis, grad_in, grad_mid, grad_out = gradients(
        gathered, params, coeffs, hidden, weight_mid, weight_out, pca_basis, offset, own_multipoles
    )
    return (spectra, grad_basis, grad_in.T, grad_mid, grad_out)


def solution(mesh):
    return jax.shard_map(
        local,
        mesh=mesh,
        in_specs=(
            P("ka", None, "grp"),
            P("ka", None, None),
            P("ka"),
            P("grp"),
            P("grp"),
            P(None, "grp"),
            P(),
            P(),
            P(),
            P(),
            P(),
            P(),
            P("ka", None),
            P("ka"),
        ),
        out_specs=(
            P("ka", "grp"),
            P(("grp", "ka"), None),
            P("grp", None),
            P("grp", None),
            P("grp", None),
        ),
        check_vma=False,
    )
```

time: 242 us -> 81.7 us (0.34)
  waiting for transfers between devices: 101 us -> 22 us
  blocking collectives: 57.6 us -> 11.6 us
  local copies, waits for them, and re-layouts: 38.3 us -> 3.74 us
  Pallas kernels: 0 us -> 21.7 us
  matrix products: 22.8 us -> 5.42 us
  between operations: 14.3 us -> 0.89 us
  starting transfers between devices: 7.57 us -> 15.2 us
    unnamed x2 -> x0, waiting for transfers between devices: 62 us -> none
    psum x1 -> x0, blocking collectives: 57.6 us -> none  [local(): coef_grad = lax.psum(coef_part, 'ka')]
    all_to_all x1 -> x0, waiting for transfers between devices: 39.2 us -> none  [local(): lax.all_to_all(sources, 'ka', split_axis=1, concat_axis=0, tiled=True)]
    ppermute x0 -> x10, waiting for transfers between devices: none -> 22 us  [exchange(): lax.ppermute(value, 'ka', [(peer, peer ^ apart) for peer in range(peers)])]
    pallas_call x0 -> x4, Pallas kernels: none -> 21.7 us  [the longest x1 12.2 us: add_groups(): pl.pallas_call(functools.partial(transfer_kernel, group, chips, times), g...]
    unnamed x29 -> x28, local copies, waits for them, and re-layouts: 22.9 us -> 3.08 us
    dot_general x13 -> x5, matrix products: 22.8 us -> 5.42 us  [mat(): lax.dot_general(left, right, (dims, ((), ())), precision=HIGHEST, preferr...]
    ppermute x0 -> x10, starting transfers between devices: none -> 15.2 us  [exchange(): lax.ppermute(value, 'ka', [(peer, peer ^ apart) for peer in range(peers)])]
  transfers between devices with their start and end apart: 2 -> 10, of which waited for: 2 -> 3; matrix products, arithmetic and copies ran while one was open for 1% -> 8% of each run, Pallas kernels for 0% -> 15%
where the time goes in v2:
time: 81.7 us; the launch traced here: 81.3 us
  waiting for transfers between devices  22 us (27%)
  Pallas kernels  21.7 us (27%)
  starting transfers between devices  15.2 us (19%)
  blocking collectives  11.6 us (14%)
  matrix products  5.42 us (7%)
  local copies, waits for them, and re-layouts  3.74 us (5%)
  between operations  0.89 us (1%)
    ppermute x10, waiting for transfers between devices, exchange(): lax.ppermute(value, 'ka', [(peer, peer ^ apart) for peer in range(peers)])  22 us
    ppermute x10, starting transfers between devices, exchange(): lax.ppermute(value, 'ka', [(peer, peer ^ apart) for peer in range(peers)])  15.2 us
    pallas_call x1, Pallas kernels, add_groups(): pl.pallas_call(functools.partial(transfer_kernel, group, chips, times), g...  12.2 us
    all_to_all x1, blocking collectives, local(): lax.all_to_all(parts, 'ka', split_axis=0, concat_axis=0, tiled=True)  11.6 us
    dot_general x5, matrix products, mat(): lax.dot_general(left, right, (dims, ((), ())), precision=HIGHEST, preferr...  5.42 us
    pallas_call x1, Pallas kernels, arrange(): pl.pallas_call(functools.partial(arrange_kernel, group, last, waves), in_...  4.46 us
    unnamed x28, local copies, waits for them, and re-layouts  3.08 us
    pallas_call x1, Pallas kernels, gradients(): pl.pallas_call(gradients_kernel, out_shape=(shape(owned, cosmos), shape(o...  2.94 us
  transfers between devices with their start and end apart: 10, of which 3 were waited for; matrix products, arithmetic and copies ran while one was open for 8% of the time, Pallas kernels for 15%

profile of v2, /device:TPU:0, one launch (start us, length us, event | category | flops | bytes accessed | tf_op | source)
XLA Modules:
  0.0 81.3 jit_solution(8810004727517360679)
XLA Ops:
  0.6 0.0 copy-start
  0.7 1.6 %copy-done.2 = bf16[64,512,32]{1,2,0:T(8,128)(2,1)S(1)} copy-done((bf16[64,512,32]{1,2,0:T(8,128)(2,1)S(1)}, bf16[64,512,32]{1,2,0:T(8,128)(2,1)}, u32[]{:S(2)}) %copy-start.2) | copy-done | bytes 2097176
  2.2 0.7 copy-done.3
  3.0 0.7 copy-done.7
  3.6 4.5 %arrange.1 = (bf16[34,16,128]{2,1,0:T(8,128)(2,1)S(1)}, bf16[66,16,128]{2,1,0:T(8,128)(2,1)S(1)}, bf16[66,16,128]{2,1,0:T(8,128)(2,1)}, bf16[66,16,128]{2,1,0:T(...) custom-call(bf16[64,32,512]{2,1,0:T(8,128)(2,1)S(1)} %bitcast.41, ...), custom_call_target="tpu_custom_call" | custom-call | bytes 16777216 | tf_op jit(solution)/shard_map/arrange/pallas_call | solution.py:101
  8.1 4.1 %collective-permute-start.3 = (bf16[66,16,128]{2,1,0:T(8,128)(2,1)S(1)}, bf16[66,16,128]{2,1,0:T(8,128)(2,1)S(1)}, u32[]{:S(2)}, u32[]{:S(2)}) collective-permute-start(bf16[66,16,128]{2,1,0:T(8,128)(2,1)S(1)} %get-tuple-element.27), channel_id=1, source_target_pairs={{0,8},{1,9},{2,10},{3,11},{4,12},{5,13},{6,14},{7,15},{8,0},{9,1},... | collective-permute-start | bytes 811016 | tf_op jit(solution)/shard_map/ppermute | solution.py:391
  12.2 1.3 %collective-permute-start.4 = (bf16[66,16,128]{2,1,0:T(8,128)(2,1)S(1)}, bf16[66,16,128]{2,1,0:T(8,128)(2,1)S(1)}, u32[]{:S(2)}, u32[]{:S(2)}) collective-permute-start(bf16[66,16,128]{2,1,0:T(8,128)(2,1)S(1)} %get-tuple-element.28), channel_id=1, source_target_pairs={{0,10},{1,11},{2,8},{3,9},{4,14},{5,15},{6,12},{7,13},{8,2},{9,3},... | collective-permute-start | bytes 811016 | tf_op jit(solution)/shard_map/ppermute | solution.py:391
  13.5 1.6 %collective-permute-start.5 = (bf16[66,16,128]{2,1,0:T(8,128)(2,1)}, bf16[66,16,128]{2,1,0:T(8,128)(2,1)S(1)}, u32[]{:S(2)}, u32[]{:S(2)}) collective-permute-start(bf16[66,16,128]{2,1,0:T(8,128)(2,1)} %get-tuple-element.29), channel_id=1, source_target_pairs={{0,4},{1,5},{2,6},{3,7},{4,0},{5,1},{6,2},{7,3},{8,12},{9,13},{10,... | collective-permute-start | bytes 811016 | tf_op jit(solution)/shard_map/ppermute | solution.py:391
  15.1 0.1 collective-permute-start.6
  15.2 1.0 %add_multiply_fusion.1 = (f32[32,512]{1,0:T(8,128)S(1)}, f32[32,512]{1,0:T(8,128)S(1)}, f32[32,512]{1,0:T(8,128)S(1)}) fusion(f32[512]{0:T(512)} %param.21, f32[6,32]{1,0:T(8,128)} %params_ref.1, f32[512,6]{0,1:T(8,128)S(1)} %copy-done), kind=kOutput, calls=%fused_computation.18 | convolution fusion | flops 1327104 | bytes 211712 | tf_op jit(solution)/shard_map/dot_general | solution.py:23
  16.2 2.3 %add_multiply_fusion = (f32[32,512]{1,0:T(8,128)S(1)}, f32[32,512]{1,0:T(8,128)S(1)}, f32[32,512]{1,0:T(8,128)S(1)}) fusion(f32[512]{0:T(512)} %param.23, f32[512,512]{1,0:T(8,128)} %weight_mid_ref.1, f32[32,512]{1,0:T(8,128)S(1)} %get-tuple-element.47), kind=kOutput, calls=%fused_computation.17 | convolution fusion | flops 100876288 | bytes 1312768 | tf_op jit(solution)/shard_map/dot_general | solution.py:23
  18.5 1.1 %convolution_add_fusion.3.coeffs_ref = f32[32,64]{1,0:T(8,128)S(1)} fusion(f32[64,512]{1,0:T(8,128)} %weight_out_ref.1, f32[64]{0:T(128)} %param.25, f32[32,512]{1,0:T(8,128)S(1)} %get-tuple-element.48), kind=kOutput, calls=%fused_computation.3 | convolution fusion | flops 12650496 | bytes 205056 | tf_op jit(solution)/shard_map/dot_general | solution.py:23
  19.7 0.6 slice.42
  20.3 10.5 %collective-permute-done.5.refs_4_.refs_16_ = bf16[66,16,128]{2,1,0:T(8,128)(2,1)S(1)} collective-permute-done((bf16[66,16,128]{2,1,0:T(8,128)(2,1)}, bf16[66,16,128]{2,1,0:T(8,128)(2,1)S(1)}, u32[]{:S(2)}, u32[]{:S(2)}) %collective-permute-start.5) | collective-permute-done | bytes 270368 | tf_op jit(solution)/shard_map/ppermute | solution.py:391
  30.8 1.3 %collective-permute-start = (bf16[66,16,128]{2,1,0:T(8,128)(2,1)S(1)}, bf16[66,16,128]{2,1,0:T(8,128)(2,1)S(1)}, u32[]{:S(2)}, u32[]{:S(2)}) collective-permute-start(bf16[66,16,128]{2,1,0:T(8,128)(2,1)S(1)} %get-tuple-element.24), channel_id=1, source_target_pairs={{0,12},{1,13},{2,14},{3,15},{4,8},{5,9},{6,10},{7,11},{8,4},{9,5},... | collective-permute-start | bytes 811016 | tf_op jit(solution)/shard_map/ppermute | solution.py:391
  32.1 1.5 %collective-permute-start.7 = (bf16[66,16,128]{2,1,0:T(8,128)(2,1)S(1)}, bf16[66,16,128]{2,1,0:T(8,128)(2,1)S(1)}, u32[]{:S(2)}, u32[]{:S(2)}) collective-permute-start(bf16[66,16,128]{2,1,0:T(8,128)(2,1)S(1)} %get-tuple-element.32), channel_id=1, source_target_pairs={{0,2},{1,3},{2,0},{3,1},{4,6},{5,7},{6,4},{7,5},{8,10},{9,11},{10,... | collective-permute-start | bytes 811016 | tf_op jit(solution)/shard_map/ppermute | solution.py:391
  33.7 10.4 %collective-permute-done.4.refs_2_.refs_14_ = bf16[66,16,128]{2,1,0:T(8,128)(2,1)S(1)} collective-permute-done((bf16[66,16,128]{2,1,0:T(8,128)(2,1)S(1)}, bf16[66,16,128]{2,1,0:T(8,128)(2,1)S(1)}, u32[]{:S(2)}, u32[]{:S(2)}) %collective-permute-start.4) | collective-permute-done | bytes 270368 | tf_op jit(solution)/shard_map/ppermute | solution.py:391
  44.2 0.1 collective-permute-start.8
  44.3 0.9 %convolution_add_fusion.2 = f32[32,32]{1,0:T(8,128)S(1)} fusion(f32[32,64]{1,0:T(8,128)S(1)} %convolution_add_fusion.3.coeffs_ref, f32[32,64]{1,0:T(8,128)} %basis_ref.3, f32[32]{0:T(128)} %param.27), kind=kOutput, calls=%fused_computation.2 | convolution fusion | flops 787456 | bytes 20608 | tf_op jit(solution)/shard_map/dot_general | solution.py:23
  45.2 0.7 pad_maximum_fusion
  45.9 4.9 %collective-permute-start.2 = (bf16[68,16,128]{2,1,0:T(8,128)(2,1)S(1)}, bf16[68,16,128]{2,1,0:T(8,128)(2,1)S(1)}, u32[]{:S(2)}, u32[]{:S(2)}) collective-permute-start(bf16[68,16,128]{2,1,0:T(8,128)(2,1)S(1)} %pad_maximum_fusion), channel_id=1, source_target_pairs={{0,14},{1,15},{2,12},{3,13},{4,10},{5,11},{6,8},{7,9},{8,6},{9,7},... | collective-permute-start | bytes 835592 | tf_op jit(solution)/shard_map/ppermute | solution.py:391
  50.9 0.0 copy-start.11
  50.9 12.2 %transfer.1 = (f32[32,32,512]{2,1,0:T(8,128)S(1)}, bf16[32,256,512]{2,1,0:T(8,128)(2,1)S(1)}, bf16[16,32,128]{2,1,0:T(8,128)(2,1)S(1)}) custom-call(s32[1]{0:T(128)} %bitcast.4.me_ref, bf16[66,16,128]{2,1,0:T(8,128)(2,1)S(1)} %collective-permute-done.3.refs_0_.refs_12_, ...), custom_call_target="tpu_custom_call" | custom-call | flops 8589934592 | bytes 33554432 | tf_op jit(solution)/shard_map/transfer/pallas_call | solution.py:185
  63.1 0.0 copy-start.8
  63.1 0.0 copy-start.9
  63.2 0.3 collective-permute-start.9
  63.5 0.1 fusion.9.refs_9_
  63.6 0.0 collective-permute-done.2.refs_1_
  63.6 1.0 %collective-permute-done.9.refs_2_ = bf16[1,34,16,128]{3,2,1,0:T(8,128)(2,1)S(1)} collective-permute-done((bf16[1,34,16,128]{3,2,1,0:T(8,128)(2,1)S(1)}, bf16[1,34,16,128]{3,2,1,0:T(8,128)(2,1)S(1)}, u32[]{:S(2)}, u32[]{:S(2)}) %collective-permute-start.9) | collective-permute-done | bytes 139296 | tf_op jit(solution)/shard_map/ppermute | solution.py:391
  64.6 2.1 %power.1 = f32[16,24,128]{2,1,0:T(8,128)S(1)} custom-call(bf16[66,16,128]{2,1,0:T(8,128)(2,1)S(1)} %collective-permute-done.refs_0_, bf16[68,16,128]{2,1,0:T(8,128)(2,1)S(1)} %collective-permute-done.2.refs_1_, bf16[1,34,16,128]{3,2,1,0:T(8,128)(2,1)S(1)} %collective-permute-done.9.refs_2_, bf16[32,256,512]{2,1,0:T(8,128)(2,1)S(1)} %get-tuple-element.36.refs_3_, ...), custom_call_target="tpu_custom_call" | custom-call | flops 2147483648 | bytes 8388608 | tf_op jit(solution)/shard_map/power/pallas_call | solution.py:275
  66.7 11.6 %all_to_all.5.parts_ref = f32[16,24,128]{2,1,0:T(8,128)S(1)} all-to-all(f32[16,24,128]{2,1,0:T(8,128)S(1)} %power.1), channel_id=1, replica_groups=mesh['grp'=2,'ka'=16] {'ka'}, dimensions={0} | all-to-all | bytes 393216 | tf_op jit(solution)/shard_map/all_to_all | solution.py:467
  78.3 2.9 %gradients.1 = (f32[32,32]{1,0:T(8,128)}, f32[32,64]{1,0:T(8,128)}, f32[6,512]{1,0:T(8,128)}, f32[512,512]{1,0:T(8,128)}, f32[64,512]{1,0:T(8,128)}) custom-call(f32[16,24,128]{2,1,0:T(8,128)S(1)} %all_to_all.5.parts_ref, f32[6,32]{1,0:T(8,128)S(1)} %copy-done.6, f32[32,64]{1,0:T(8,128)S(1)} %convolution_add_fusion.3.coeffs_ref, ...), custom_call_target="tpu_custom_call" | custom-call | tf_op jit(solution)/shard_map/gradients/pallas_call | solution.py:366
  (33 shorter events, 0.2 us)
Async XLA Ops:
  0.6 14.6 %copy-start = (f32[512,6]{0,1:T(8,128)S(1)}, f32[512,6]{0,1:T(8,128)}, u32[]{:S(2)}) copy-start(f32[512,6]{0,1:T(8,128)} %param.20) | copy-start | bytes 36868
  0.6 1.6 %copy-start.2 = (bf16[64,512,32]{1,2,0:T(8,128)(2,1)S(1)}, bf16[64,512,32]{1,2,0:T(8,128)(2,1)}, u32[]{:S(2)}) copy-start(bf16[64,512,32]{1,2,0:T(8,128)(2,1)} %param.14) | copy-start | bytes 6291460
  2.2 0.7 copy-start.3
  3.0 0.7 copy-start.7
  8.1 24.0 %collective-permute-start.3 = (bf16[66,16,128]{2,1,0:T(8,128)(2,1)S(1)}, bf16[66,16,128]{2,1,0:T(8,128)(2,1)S(1)}, u32[]{:S(2)}, u32[]{:S(2)}) collective-permute-start(bf16[66,16,128]{2,1,0:T(8,128)(2,1)S(1)} %get-tuple-element.27), channel_id=1, source_target_pairs={{0,8},{1,9},{2,10},{3,11},{4,12},{5,13},{6,14},{7,15},{8,0},{9,1},... | collective-permute-start | bytes 811016 | tf_op jit(solution)/shard_map/ppermute | solution.py:391
  12.2 31.9 %collective-permute-start.4 = (bf16[66,16,128]{2,1,0:T(8,128)(2,1)S(1)}, bf16[66,16,128]{2,1,0:T(8,128)(2,1)S(1)}, u32[]{:S(2)}, u32[]{:S(2)}) collective-permute-start(bf16[66,16,128]{2,1,0:T(8,128)(2,1)S(1)} %get-tuple-element.28), channel_id=1, source_target_pairs={{0,10},{1,11},{2,8},{3,9},{4,14},{5,15},{6,12},{7,13},{8,2},{9,3},... | collective-permute-start | bytes 811016 | tf_op jit(solution)/shard_map/ppermute | solution.py:391
  13.5 17.3 %collective-permute-start.5 = (bf16[66,16,128]{2,1,0:T(8,128)(2,1)}, bf16[66,16,128]{2,1,0:T(8,128)(2,1)S(1)}, u32[]{:S(2)}, u32[]{:S(2)}) collective-permute-start(bf16[66,16,128]{2,1,0:T(8,128)(2,1)} %get-tuple-element.29), channel_id=1, source_target_pairs={{0,4},{1,5},{2,6},{3,7},{4,0},{5,1},{6,2},{7,3},{8,12},{9,13},{10,... | collective-permute-start | bytes 811016 | tf_op jit(solution)/shard_map/ppermute | solution.py:391
  15.1 29.1 %collective-permute-start.6 = (bf16[66,16,128]{2,1,0:T(8,128)(2,1)S(1)}, bf16[66,16,128]{2,1,0:T(8,128)(2,1)S(1)}, u32[]{:S(2)}, u32[]{:S(2)}) collective-permute-start(bf16[66,16,128]{2,1,0:T(8,128)(2,1)S(1)} %get-tuple-element.30), channel_id=1, source_target_pairs={{0,6},{1,7},{2,4},{3,5},{4,2},{5,3},{6,0},{7,1},{8,14},{9,15},{10,... | collective-permute-start | bytes 811016 | tf_op jit(solution)/shard_map/ppermute | solution.py:391
  15.2 30.0 %collective-permute-start.1 = (bf16[2,34,16,128]{3,2,1,0:T(8,128)(2,1)S(1)}, bf16[2,34,16,128]{3,2,1,0:T(8,128)(2,1)S(1)}, u32[]{:S(2)}, u32[]{:S(2)}) collective-permute-start(bf16[2,34,16,128]{3,2,1,0:T(8,128)(2,1)S(1)} %get-tuple-element.26), channel_id=1, source_target_pairs={{0,1},{1,0},{2,3},{3,2},{4,5},{5,4},{6,7},{7,6},{8,9},{9,8},{10,11... | collective-permute-start | bytes 835592 | tf_op jit(solution)/shard_map/ppermute | solution.py:391
  30.8 32.3 %collective-permute-start = (bf16[66,16,128]{2,1,0:T(8,128)(2,1)S(1)}, bf16[66,16,128]{2,1,0:T(8,128)(2,1)S(1)}, u32[]{:S(2)}, u32[]{:S(2)}) collective-permute-start(bf16[66,16,128]{2,1,0:T(8,128)(2,1)S(1)} %get-tuple-element.24), channel_id=1, source_target_pairs={{0,12},{1,13},{2,14},{3,15},{4,8},{5,9},{6,10},{7,11},{8,4},{9,5},... | collective-permute-start | bytes 811016 | tf_op jit(solution)/shard_map/ppermute | solution.py:391
  32.1 12.0 %collective-permute-start.7 = (bf16[66,16,128]{2,1,0:T(8,128)(2,1)S(1)}, bf16[66,16,128]{2,1,0:T(8,128)(2,1)S(1)}, u32[]{:S(2)}, u32[]{:S(2)}) collective-permute-start(bf16[66,16,128]{2,1,0:T(8,128)(2,1)S(1)} %get-tuple-element.32), channel_id=1, source_target_pairs={{0,2},{1,3},{2,0},{3,1},{4,6},{5,7},{6,4},{7,5},{8,10},{9,11},{10,... | collective-permute-start | bytes 811016 | tf_op jit(solution)/shard_map/ppermute | solution.py:391
  44.2 6.7 %collective-permute-start.8 = (bf16[5,34,16,128]{3,2,1,0:T(8,128)(2,1)S(1)}, bf16[5,34,16,128]{3,2,1,0:T(8,128)(2,1)S(1)}, u32[]{:S(2)}, u32[]{:S(2)}) collective-permute-start(bf16[5,34,16,128]{3,2,1,0:T(8,128)(2,1)S(1)} %fusion), channel_id=1, source_target_pairs={{0,1},{1,0},{2,3},{3,2},{4,5},{5,4},{6,7},{7,6},{8,9},{9,8},{10,11... | collective-permute-start | bytes 2088968 | tf_op jit(solution)/shard_map/ppermute | solution.py:391
  45.9 17.7 %collective-permute-start.2 = (bf16[68,16,128]{2,1,0:T(8,128)(2,1)S(1)}, bf16[68,16,128]{2,1,0:T(8,128)(2,1)S(1)}, u32[]{:S(2)}, u32[]{:S(2)}) collective-permute-start(bf16[68,16,128]{2,1,0:T(8,128)(2,1)S(1)} %pad_maximum_fusion), channel_id=1, source_target_pairs={{0,14},{1,15},{2,12},{3,13},{4,10},{5,11},{6,8},{7,9},{8,6},{9,7},... | collective-permute-start | bytes 835592 | tf_op jit(solution)/shard_map/ppermute | solution.py:391
  50.8 12.6 %copy-start.4 = (f32[32,64]{1,0:T(8,128)S(1)}, f32[32,64]{1,0:T(8,128)}, u32[]{:S(2)}) copy-start(f32[32,64]{1,0:T(8,128)} %basis_ref.3) | copy-start | bytes 24580
  50.8 13.8 %copy-start.6 = (f32[6,32]{1,0:T(8,128)S(1)}, f32[6,32]{1,0:T(8,128)}, u32[]{:S(2)}) copy-start(f32[6,32]{1,0:T(8,128)} %params_ref.1) | copy-start | bytes 2308
  50.8 13.8 %copy-start.10 = (s32[32]{0:T(128)S(1)}, s32[32]{0:T(128)}, u32[]{:S(2)}) copy-start(s32[32]{0:T(128)} %param.17) | copy-start | bytes 388
  50.9 13.8 %copy-start.11 = (s32[32]{0:T(128)S(1)}, s32[32]{0:T(128)}, u32[]{:S(2)}) copy-start(s32[32]{0:T(128)} %param.18) | copy-start | bytes 388
  63.1 15.2 %copy-start.1 = (f32[512,512]{1,0:T(8,128)S(1)}, f32[512,512]{1,0:T(8,128)}, u32[]{:S(2)}) copy-start(f32[512,512]{1,0:T(8,128)} %weight_mid_ref.1) | copy-start | bytes 3145732
  63.1 15.2 %copy-start.5 = (f32[64,512]{1,0:T(8,128)S(1)}, f32[64,512]{1,0:T(8,128)}, u32[]{:S(2)}) copy-start(f32[64,512]{1,0:T(8,128)} %weight_out_ref.1) | copy-start | bytes 393220
  63.1 15.2 %copy-start.8 = (s32[32]{0:T(128)S(1)}, s32[32]{0:T(128)}, u32[]{:S(2)}) copy-start(s32[32]{0:T(128)} %param.16) | copy-start | bytes 388
  63.1 15.2 %copy-start.9 = (f32[32]{0:T(128)S(1)}, f32[32]{0:T(128)}, u32[]{:S(2)}) copy-start(f32[32]{0:T(128)} %param.27) | copy-start | bytes 388
  63.2 1.4 %collective-permute-start.9 = (bf16[1,34,16,128]{3,2,1,0:T(8,128)(2,1)S(1)}, bf16[1,34,16,128]{3,2,1,0:T(8,128)(2,1)S(1)}, u32[]{:S(2)}, u32[]{:S(2)}) collective-permute-start(bf16[1,34,16,128]{3,2,1,0:T(8,128)(2,1)S(1)} %slice_bitcast_fusion.5), channel_id=1, source_target_pairs={{0,1},{1,0},{2,3},{3,2},{4,5},{5,4},{6,7},{7,6},{8,9},{9,8},{10,11... | collective-permute-start | bytes 417800 | tf_op jit(solution)/shard_map/ppermute | solution.py:391

commit v3 on v2

--- a/solution.py
+++ b/solution.py
@@ -11,6 +11,8 @@
 LMAX = 5000
 LANES = 128
 TOPS = (2, 1, 0, 3)
+HELD = (3,)
+FIRST = 2
 HIGHEST = lax.Precision.HIGHEST
 
 
@@ -49,22 +51,34 @@
     return value.astype(jnp.bfloat16).reshape(-1, low_count, LANES)
 
 
-def arrange_kernel(group, last, waves, source_ref, multipoles_ref, basis_ref, *refs):
-    *out_refs, block_ref, rows_ref, turned_ref, sems = refs
-    blocks, times, cosmos, block = block_ref.shape
+def arrange_kernel(tops, group, last, waves, held_tops, source_ref, *refs):
+    multipoles_ref, basis_ref, whole_ref, *refs = refs
+    held_refs, refs = refs[: len(held_tops)], refs[len(held_tops) :]
+    *out_refs, block_ref, rows_ref, turned_ref, sems, held_sems = refs
+    _, times, cosmos, block = block_ref.shape
     packs = LANES // times
     low_count = cosmos // packs
     size = waves * low_count
     me = lax.axis_index("ka")
     copies = []
-    for slot, top in enumerate(TOPS):
+    for slot, top in enumerate(tops):
         start = pl.multiple_of(((me // group) ^ top) * block, block)
         copy = pltpu.make_async_copy(
             source_ref.at[:, :, pl.ds(start, block)], block_ref.at[slot], sems.at[slot]
         )
         copy.start()
         copies.append(copy)
+    holds = []
+    for slot, (top, held_ref) in enumerate(zip(held_tops, held_refs)):
+        span = group * times
+        start = pl.multiple_of(((me // group) ^ top) * span, span)
+        copy = pltpu.make_async_copy(
+            whole_ref.at[:, pl.ds(start, span), :], held_ref, held_sems.at[slot]
+        )
+        copy.start()
+        holds.append(copy)
     extra = smooth_basis(multipoles_ref, basis_ref, low_count)
+    chips = [top * group // 2 + low for top in tops for low in range(group // 2)]
     for slot, copy in enumerate(copies):
         copy.wait()
         rows_ref[...] = block_ref[slot].astype(jnp.float32).reshape(times * cosmos, block)
@@ -78,43 +92,51 @@
             start = pl.multiple_of((peer ^ (me % group)) * size, size)
             piece = turned_ref[pl.ds(start, size), :].astype(jnp.bfloat16)
             piece = piece.reshape(waves, low_count, LANES)
-            chip, core = TOPS[slot] * group // 2 + peer // 2, peer % 2
+            chip, core = tops[slot] * group // 2 + peer // 2, peer % 2
+            out_ref = out_refs[chips.index(chip)]
             if chip in (0, last):
-                out_ref = out_refs[-1].at[int(chip == last)] if core else out_refs[chip]
+                out_ref = out_refs[-1].at[int(chip == last)] if core else out_ref
                 out_ref[:waves] = piece
                 out_ref[waves:] = extra
             else:
-                out_refs[chip][core * waves : (core + 1) * waves] = piece
-                out_refs[chip][2 * waves :] = extra
-
-
-def arrange(sources, multipoles, basis, waves, group, last):
+                out_ref[core * waves : (core + 1) * waves] = piece
+                out_ref[2 * waves :] = extra
+    for copy in holds:
+        copy.wait()
+
+
+def arrange(sources, multipoles, basis, bessel, tops, group, last, held_tops=()):
     times, cosmos, total = sources.shape
+    waves, _, multipole_count = bessel.shape
     low_count = cosmos // (LANES // times)
     block = waves * group
     extras = -(-basis.shape[0] // low_count)
     one, two = (count * waves + extras for count in (1, 2))
-    chips = total // waves // 2
-    shapes = [(one if chip in (0, last) else two, low_count, LANES) for chip in range(chips)]
-    shapes.append((2, one, low_count, LANES))
-    vmem = pl.BlockSpec(memory_space=pltpu.VMEM)
+    chips = [top * group // 2 + low for top in tops for low in range(group // 2)]
+    shapes = [(one if chip in (0, last) else two, low_count, LANES) for chip in chips]
+    if last in chips:
+        shapes.append((2, one, low_count, LANES))
+    held = pltpu.VMEM((waves, group * times, multipole_count), bessel.dtype)
+    vmem, anywhere = (pl.BlockSpec(memory_space=space) for space in (pltpu.VMEM, pl.ANY))
     return pl.pallas_call(
-        functools.partial(arrange_kernel, group, last, waves),
-        in_specs=[pl.BlockSpec(memory_space=pl.ANY), vmem, vmem],
-        out_specs=[vmem] * len(shapes),
-        out_shape=[jax.ShapeDtypeStruct(shape, jnp.bfloat16) for shape in shapes],
+        functools.partial(arrange_kernel, tops, group, last, waves, held_tops),
+        in_specs=[anywhere, vmem, vmem, anywhere],
+        out_specs=[vmem] * (len(held_tops) + len(shapes)),
+        out_shape=[held] * len(held_tops)
+        + [jax.ShapeDtypeStruct(shape, jnp.bfloat16) for shape in shapes],
         scratch_shapes=[
-            pltpu.VMEM((len(TOPS), times, cosmos, block), jnp.bfloat16),
+            pltpu.VMEM((len(tops), times, cosmos, block), jnp.bfloat16),
             pltpu.VMEM((times * cosmos, block), jnp.float32),
             pltpu.VMEM((block * low_count, LANES), jnp.float32),
-            pltpu.SemaphoreType.DMA((len(TOPS),)),
+            pltpu.SemaphoreType.DMA((len(tops),)),
+            pltpu.SemaphoreType.DMA((max(1, len(held_tops)),)),
         ],
-        compiler_params=pltpu.CompilerParams(vmem_limit_bytes=24 << 20),
+        compiler_params=pltpu.CompilerParams(vmem_limit_bytes=(50 if held_tops else 61) << 20),
         cost_estimate=pl.CostEstimate(
-            flops=0, bytes_accessed=16 * times * cosmos * total, transcendentals=0
+            flops=0, bytes_accessed=16 * times * cosmos * block * len(tops), transcendentals=0
         ),
         name="arrange",
-    )(sources, multipoles, basis)
+    )(sources, multipoles, basis, bessel)
 
 
 def source_rows(stage_ref, wave, times):
@@ -126,26 +148,27 @@
     return jnp.concatenate(rows, axis=0)
 
 
-def transfer_kernel(group, chips, times, me_ref, *refs):
-    count = len(chips) * 2
-    pieces, extras, refs = refs[:count], refs[count : 2 * count], refs[2 * count :]
-    *bessel_refs, whole_ref, out_ref, held_ref, basis_ref, stage_ref, sem = refs
+def transfer_kernel(group, members, times, me_ref, *refs):
+    count = 1 + max(member[1] for member in members)
+    arrays, (*bessel_refs, out_ref, basis_ref, stage_ref) = refs[:count], refs[count:]
     me = me_ref[0]
-    span = held_ref.shape[1]
-    start = pl.multiple_of(((me // group) ^ TOPS[-1]) * span, span)
-    copy = pltpu.make_async_copy(whole_ref.at[:, pl.ds(start, span), :], held_ref, sem)
     step = pl.program_id(0)
+    waves = out_ref.shape[0]
+    extras = basis_ref.shape[1] // stage_ref.shape[3]
+
+    def tiles(array, lead, rows):
+        return arrays[array][rows] if lead is None else arrays[array][lead, rows]
 
     @pl.when(step == 0)
     def _():
-        copy.start()
-        for number, extra_ref in enumerate(extras):
-            apart = chips[number // 2] * 2 + number % 2
-            basis_ref[apart] = extra_ref[...].reshape(basis_ref.shape[1:])
-
-    for number in range(count):
-        stage_ref[number // group, (number % group) ^ (me % group)] = pieces[number][...]
-    for wave in range(out_ref.shape[0]):
+        for apart, array, lead, _, at in members:
+            extra = tiles(array, lead, pl.ds(at, extras))
+            basis_ref[apart] = extra.reshape(basis_ref.shape[1:])
+
+    for number, (_, array, lead, at, _) in enumerate(members):
+        place = (number % group) ^ (me % group)
+        stage_ref[number // group, place] = tiles(array, lead, pl.ds(at + step * waves, waves))
+    for wave in range(waves):
         total = None
         for number, bessel_ref in enumerate(bessel_refs):
             part = jnp.dot(
@@ -155,52 +178,38 @@
             )
             total = part if total is None else total + part
         out_ref[wave] = total
-    pl.when(step == pl.num_programs(0) - 1)(copy.wait)
-
-
-def tiles_spec(array, lead, start, size, moves):
-    rest = array.shape[-2:]
-    index = lambda s, me: (start // size + s * moves, 0, 0)
-    if lead is None:
-        return pl.BlockSpec((size,) + rest, index)
-    return pl.BlockSpec((None, size) + rest, lambda s, me: (lead,) + index(s, me))
-
-
-def add_groups(me, group, chips, members, bessel, times, extras):
-    low_count = members[0][0].shape[-2]
+
+
+def add_groups(me, group, arrays, members, bessel, times, extras):
+    low_count = arrays[0].shape[-2]
     waves, _, multipoles = bessel.shape
+    span = group * times
     cosmos = low_count * (LANES // times)
     block = math.gcd(waves, 8)
-    in_specs = [tiles_spec(array, lead, at, block, 1) for array, lead, at, _ in members]
-    in_specs += [tiles_spec(array, lead, at, extras, 0) for array, lead, _, at in members]
-
-    span = group * times
+    in_specs = [pl.BlockSpec(memory_space=pltpu.VMEM)] * len(arrays)
     in_specs += [
-        pl.BlockSpec((block, span, multipoles), lambda s, me, top=top: (s, (me[0] // group) ^ top, 0))
+        pl.BlockSpec(
+            (block, span, multipoles), lambda s, me, top=top: (s, (me[0] // group) ^ top, 0)
+        )
         for top in TOPS[:-1]
     ]
-    in_specs.append(pl.BlockSpec(memory_space=pl.ANY))
-    arrays = [member[0] for member in members]
     basis = (len(members) + group, extras * low_count, LANES)
     return pl.pallas_call(
-        functools.partial(transfer_kernel, group, chips, times),
+        functools.partial(transfer_kernel, group, members, times),
         grid_spec=pltpu.PrefetchScalarGridSpec(
             num_scalar_prefetch=1,
             grid=(waves // block,),
             in_specs=in_specs,
             out_specs=[
                 pl.BlockSpec((block, cosmos, multipoles), lambda s, me: (s, 0, 0)),
-                pl.BlockSpec(memory_space=pltpu.VMEM),
                 pl.BlockSpec(basis, lambda s, me: (0, 0, 0)),
             ],
             scratch_shapes=[
                 pltpu.VMEM((len(TOPS) - 1, group, block, low_count, LANES), jnp.bfloat16),
-                pltpu.SemaphoreType.DMA,
             ],
         ),
         out_shape=[
             jax.ShapeDtypeStruct((waves, cosmos, multipoles), jnp.float32),
-            jax.ShapeDtypeStruct((waves, span, multipoles), bessel.dtype),
             jax.ShapeDtypeStruct(basis, jnp.bfloat16),
         ],
         compiler_params=pltpu.CompilerParams(vmem_limit_bytes=24 << 20),
@@ -210,7 +219,7 @@
             transcendentals=0,
         ),
         name="transfer",
-    )(me, *arrays, *arrays, *[bessel] * len(TOPS))
+    )(me, *arrays, *[bessel] * (len(TOPS) - 1))
 
 
 def power_kernel(times, chips, total_waves, *refs):
@@ -426,7 +435,11 @@
 
     chips = [top * half + low for top in TOPS for low in range(half)]
     late, last = chips[-half:], chips[-1]
-    *ready, give = arrange(turned, own_multipoles, pca_basis, waves, group, last)
+    arranged = (turned, own_multipoles, pca_basis, bessel)
+    ready = arrange(*arranged, TOPS[:FIRST], group, last)
+    *rest_ready, give = arrange(*arranged, TOPS[FIRST:], group, last, HELD)
+    held, rest_ready = dict(zip(HELD, rest_ready)), rest_ready[len(HELD) :]
+    ready = dict(zip(chips, [*ready, *rest_ready]))
     given = exchange(give, 1, peers)
     got = {}
     near = [chip for chip in chips if 0 < chip < half]
@@ -444,13 +457,15 @@
     others = lambda part, *then: jnp.stack([after(got[chip], *then)[waves:] for chip in part])
     early = [chip for chip in chips[:-half] if chip]
     traded = exchange(others(early), 1, peers)
+    arrays = [traded, given, ready[0]] + [got[chip] for chip in early]
     members = []
     for chip in chips[:-half]:
         if chip:
-            members += [(got[chip], None, 0, 2 * waves), (traded, early.index(chip), 0, waves)]
+            at = early.index(chip)
+            members += [(2 * chip, 3 + at, None, 0, 2 * waves), (2 * chip + 1, 0, at, 0, waves)]
         else:
-            members += [(ready[0], None, 0, waves), (given, 0, 0, waves)]
-    rest, held, basis = add_groups(me, group, chips[:-half], members, bessel, times, extras)
+            members += [(0, 2, None, 0, waves), (1, 1, 0, 0, waves)]
+    rest, basis = add_groups(me, group, arrays, members, bessel, times, extras)
     late_traded = exchange(others(late[:-1], rest), 1, peers)
 
     inner_pre = mat(params.T, weight_in.T) + bias_in[None, :]
@@ -463,7 +478,7 @@
 
     extra = (params, window_low.reshape(1, cosmos), window_high.reshape(1, cosmos), basis, base)
     pieces = [got[chip] for chip in late]
-    parts = power_parts(pieces, late_traded, held, rest, times, late, total_waves, extra)
+    parts = power_parts(pieces, late_traded, held[TOPS[-1]], rest, times, late, total_waves, extra)
     gathered = lax.all_to_all(parts, "ka", split_axis=0, concat_axis=0, tiled=True)
     spectra, grad_basis, grad_in, grad_mid, grad_out = gradients(
         gathered, params, coeffs, hidden, weight_mid, weight_out, pca_basis, offset, own_multipoles

time: 81.7 us -> 77.5 us (0.949)
  waiting for transfers between devices: 22 us -> 13.9 us
  Pallas kernels: 21.7 us -> 26.4 us
  matrix products: 5.42 us -> 1.87 us
  local copies, waits for them, and re-layouts: 3.74 us -> 5.97 us
  starting transfers between devices: 15.2 us -> 16.1 us
    ppermute x10, waiting for transfers between devices: 22 us -> 13.9 us  [exchange(): lax.ppermute(value, 'ka', [(peer, peer ^ apart) for peer in range(peers)])]
    pallas_call x2 -> x3, Pallas kernels: 16.7 us -> 21.3 us  [the longest x1 11.1 us: add_groups(): pl.pallas_call(functools.partial(transfer_kernel, group, members, times),...]
    dot_general x5, matrix products: 5.42 us -> 1.87 us  [mat(): lax.dot_general(left, right, (dims, ((), ())), precision=HIGHEST, preferr...]
    unnamed x28 -> x36, local copies, waits for them, and re-layouts: 3.08 us -> 4.32 us
    slice x1, local copies, waits for them, and re-layouts: 0.01 us -> 0.91 us  [local(): mine[:waves]]
    ppermute x10, starting transfers between devices: 15.2 us -> 16.1 us  [exchange(): lax.ppermute(value, 'ka', [(peer, peer ^ apart) for peer in range(peers)])]
  transfers between devices with their start and end apart: 10 -> 10, of which waited for: 3 -> 4; matrix products, arithmetic and copies ran while one was open for 8% -> 5% of each run, Pallas kernels for 15% -> 22%
where the time goes in v3:
time: 77.5 us; the launch traced here: 77.1 us
  Pallas kernels  26.4 us (34%)
  starting transfers between devices  16.1 us (21%)
  waiting for transfers between devices  13.9 us (18%)
  blocking collectives  12 us (15%)
  local copies, waits for them, and re-layouts  5.97 us (8%)
  matrix products  1.87 us (2%)
  between operations  0.93 us (1%)
    ppermute x10, starting transfers between devices, exchange(): lax.ppermute(value, 'ka', [(peer, peer ^ apart) for peer in range(peers)])  16.1 us
    ppermute x10, waiting for transfers between devices, exchange(): lax.ppermute(value, 'ka', [(peer, peer ^ apart) for peer in range(peers)])  13.9 us
    all_to_all x1, blocking collectives, local(): lax.all_to_all(parts, 'ka', split_axis=0, concat_axis=0, tiled=True)  12 us
    pallas_call x1, Pallas kernels, add_groups(): pl.pallas_call(functools.partial(transfer_kernel, group, members, times),...  11.1 us
    pallas_call x2, Pallas kernels, arrange(): pl.pallas_call(functools.partial(arrange_kernel, tops, group, last, waves...  10.2 us
    unnamed x36, local copies, waits for them, and re-layouts  4.32 us
    pallas_call x1, Pallas kernels, gradients(): pl.pallas_call(gradients_kernel, out_shape=(shape(owned, cosmos), shape(o...  2.94 us
    pallas_call x1, Pallas kernels, power_parts(): pl.pallas_call(functools.partial(power_kernel, times, chips, total_waves)...  2.17 us
  transfers between devices with their start and end apart: 10, of which 4 were waited for; matrix products, arithmetic and copies ran while one was open for 5% of the time, Pallas kernels for 22%

profile of v3, /device:TPU:0, one launch (start us, length us, event | category | flops | bytes accessed | tf_op | source)
XLA Modules:
  0.0 77.1 jit_solution(18258125034961071850)
XLA Ops:
  0.6 0.0 copy-start
  0.6 4.5 %arrange.3 = (bf16[66,16,128]{2,1,0:T(8,128)(2,1)}, bf16[66,16,128]{2,1,0:T(8,128)(2,1)}, bf16[66,16,128]{2,1,0:T(8,128)(2,1)}, bf16[66,16,128]{2,1,0:T(8,128)(2,1)}) custom-call(bf16[64,32,512]{2,1,0:T(8,128)(2,1)} %bitcast.49, s32[1,32]{1,0:T(1,128)} %bitcast.43, f32[32,64]{1,0:T(8,128)} %basis_ref.1, bf16[32,1024,512]{2,1,0:T(8,128)(2,1)} %refs_10_.1), custom_call_target="tpu_custom_call" | custom-call | bytes 8388608 | tf_op jit(solution)/shard_map/arrange/pallas_call | solution.py:121
  5.2 4.1 %collective-permute-start.3 = (bf16[66,16,128]{2,1,0:T(8,128)(2,1)}, bf16[66,16,128]{2,1,0:T(8,128)(2,1)S(1)}, u32[]{:S(2)}, u32[]{:S(2)}) collective-permute-start(bf16[66,16,128]{2,1,0:T(8,128)(2,1)} %get-tuple-element.27), channel_id=1, source_target_pairs={{0,8},{1,9},{2,10},{3,11},{4,12},{5,13},{6,14},{7,15},{8,0},{9,1},... | collective-permute-start | bytes 811016 | tf_op jit(solution)/shard_map/ppermute | solution.py:400
  9.3 1.3 %collective-permute-start.4 = (bf16[66,16,128]{2,1,0:T(8,128)(2,1)}, bf16[66,16,128]{2,1,0:T(8,128)(2,1)S(1)}, u32[]{:S(2)}, u32[]{:S(2)}) collective-permute-start(bf16[66,16,128]{2,1,0:T(8,128)(2,1)} %get-tuple-element.28), channel_id=1, source_target_pairs={{0,10},{1,11},{2,8},{3,9},{4,14},{5,15},{6,12},{7,13},{8,2},{9,3},... | collective-permute-start | bytes 811016 | tf_op jit(solution)/shard_map/ppermute | solution.py:400
  10.6 1.6 %collective-permute-start.5 = (bf16[66,16,128]{2,1,0:T(8,128)(2,1)}, bf16[66,16,128]{2,1,0:T(8,128)(2,1)S(1)}, u32[]{:S(2)}, u32[]{:S(2)}) collective-permute-start(bf16[66,16,128]{2,1,0:T(8,128)(2,1)} %get-tuple-element.29), channel_id=1, source_target_pairs={{0,4},{1,5},{2,6},{3,7},{4,0},{5,1},{6,2},{7,3},{8,12},{9,13},{10,... | collective-permute-start | bytes 811016 | tf_op jit(solution)/shard_map/ppermute | solution.py:400
  12.2 0.2 collective-permute-start.6
  12.4 5.7 %arrange.2 = (bf16[32,256,512]{2,1,0:T(8,128)(2,1)S(1)}, bf16[34,16,128]{2,1,0:T(8,128)(2,1)}, bf16[66,16,128]{2,1,0:T(8,128)(2,1)}, bf16[66,16,128]{2,1,0:T(8,1...) custom-call(bf16[64,32,512]{2,1,0:T(8,128)(2,1)} %bitcast.50, s32[1,32]{1,0:T(1,128)} %bitcast.44, ...), custom_call_target="tpu_custom_call" | custom-call | bytes 8388608 | tf_op jit(solution)/shard_map/arrange/pallas_call | solution.py:121
  18.1 3.3 %copy-done.1 = bf16[32,256,512]{2,1,0:T(8,128)(2,1)} copy-done((bf16[32,256,512]{2,1,0:T(8,128)(2,1)}, bf16[32,256,512]{2,1,0:T(8,128)(2,1)S(1)}, u32[]{:S(2)}) %copy-start.1) | copy-done | bytes 8388632
  21.4 0.3 add_multiply_fusion.1
  21.7 1.1 %add_multiply_fusion = (f32[32,512]{1,0:T(8,128)S(1)}, f32[32,512]{1,0:T(8,128)S(1)}, f32[32,512]{1,0:T(8,128)S(1)}) fusion(f32[512]{0:T(512)S(1)} %copy-done.11, f32[512,512]{1,0:T(8,128)S(1)} %copy-done.2, f32[32,512]{1,0:T(8,128)S(1)} %get-tuple-element.47), kind=kOutput, calls=%fused_computation.17 | convolution fusion | flops 100876288 | bytes 1312768 | tf_op jit(solution)/shard_map/dot_general | solution.py:25
  22.8 0.2 convolution_add_fusion.3.coeffs_ref
  23.1 0.9 %slice.39 = bf16[32,16,128]{2,1,0:T(8,128)(2,1)S(1)} slice(bf16[34,16,128]{2,1,0:T(8,128)(2,1)} %get-tuple-element.25), slice={[0:32], [0:16], [0:128]} | slice | bytes 262144 | tf_op jit(solution)/shard_map/slice | solution.py:454
  24.0 0.7 slice.42
  24.7 3.4 %collective-permute-done.5.refs_5_ = bf16[66,16,128]{2,1,0:T(8,128)(2,1)S(1)} collective-permute-done((bf16[66,16,128]{2,1,0:T(8,128)(2,1)}, bf16[66,16,128]{2,1,0:T(8,128)(2,1)S(1)}, u32[]{:S(2)}, u32[]{:S(2)}) %collective-permute-start.5) | collective-permute-done | bytes 270368 | tf_op jit(solution)/shard_map/ppermute | solution.py:400
  28.1 1.3 %collective-permute-start = (bf16[66,16,128]{2,1,0:T(8,128)(2,1)}, bf16[66,16,128]{2,1,0:T(8,128)(2,1)S(1)}, u32[]{:S(2)}, u32[]{:S(2)}) collective-permute-start(bf16[66,16,128]{2,1,0:T(8,128)(2,1)} %get-tuple-element.24), channel_id=1, source_target_pairs={{0,12},{1,13},{2,14},{3,15},{4,8},{5,9},{6,10},{7,11},{8,4},{9,5},... | collective-permute-start | bytes 811016 | tf_op jit(solution)/shard_map/ppermute | solution.py:400
  29.4 1.5 %collective-permute-start.7 = (bf16[66,16,128]{2,1,0:T(8,128)(2,1)}, bf16[66,16,128]{2,1,0:T(8,128)(2,1)S(1)}, u32[]{:S(2)}, u32[]{:S(2)}) collective-permute-start(bf16[66,16,128]{2,1,0:T(8,128)(2,1)} %get-tuple-element.32), channel_id=1, source_target_pairs={{0,2},{1,3},{2,0},{3,1},{4,6},{5,7},{6,4},{7,5},{8,10},{9,11},{10,... | collective-permute-start | bytes 811016 | tf_op jit(solution)/shard_map/ppermute | solution.py:400
  30.9 5.7 %collective-permute-done.4.refs_4_ = bf16[66,16,128]{2,1,0:T(8,128)(2,1)S(1)} collective-permute-done((bf16[66,16,128]{2,1,0:T(8,128)(2,1)}, bf16[66,16,128]{2,1,0:T(8,128)(2,1)S(1)}, u32[]{:S(2)}, u32[]{:S(2)}) %collective-permute-start.4) | collective-permute-done | bytes 270368 | tf_op jit(solution)/shard_map/ppermute | solution.py:400
  36.7 3.7 %collective-permute-done.7.refs_7_ = bf16[66,16,128]{2,1,0:T(8,128)(2,1)S(1)} collective-permute-done((bf16[66,16,128]{2,1,0:T(8,128)(2,1)}, bf16[66,16,128]{2,1,0:T(8,128)(2,1)S(1)}, u32[]{:S(2)}, u32[]{:S(2)}) %collective-permute-start.7) | collective-permute-done | bytes 270368 | tf_op jit(solution)/shard_map/ppermute | solution.py:400
  40.5 0.1 collective-permute-start.8
  40.6 0.1 convolution_add_fusion.2
  40.7 0.0 collective-permute-done.1.refs_1_
  40.8 0.1 pad_maximum_fusion
  40.8 5.7 %collective-permute-start.2 = (bf16[68,16,128]{2,1,0:T(8,128)(2,1)S(1)}, bf16[68,16,128]{2,1,0:T(8,128)(2,1)S(1)}, u32[]{:S(2)}, u32[]{:S(2)}) collective-permute-start(bf16[68,16,128]{2,1,0:T(8,128)(2,1)S(1)} %pad_maximum_fusion), channel_id=1, source_target_pairs={{0,14},{1,15},{2,12},{3,13},{4,10},{5,11},{6,8},{7,9},{8,6},{9,7},... | collective-permute-start | bytes 835592 | tf_op jit(solution)/shard_map/ppermute | solution.py:400
  46.5 0.9 %copy-done.4 = bf16[34,16,128]{2,1,0:T(8,128)(2,1)S(1)} copy-done((bf16[34,16,128]{2,1,0:T(8,128)(2,1)S(1)}, bf16[34,16,128]{2,1,0:T(8,128)(2,1)}, u32[]{:S(2)}) %copy-start.4) | copy-done | bytes 139288
  47.5 11.1 %transfer.1 = (f32[32,32,512]{2,1,0:T(8,128)S(1)}, bf16[16,32,128]{2,1,0:T(8,128)(2,1)S(1)}) custom-call(s32[1]{0:T(128)} %bitcast.4.me_ref, bf16[5,34,16,128]{3,2,1,0:T(8,128)(2,1)S(1)} %collective-permute-done.8.refs_0_, bf16[2,34,16,128]{3,2,1,0:T(8,128)(2,1)S(1)} %collective-permute-done.1.refs_1_, bf16[34,16,128]{2,1,0:T(8,128)(2,1)S(1)} %copy-done.4, ...), custom_call_target="tpu_custom_call" | custom-call | flops 8589934592 | bytes 33554432 | tf_op jit(solution)/shard_map/transfer/pallas_call | solution.py:197
  58.5 0.3 collective-permute-start.9
  58.8 0.1 fusion.9.refs_9_
  58.9 0.0 collective-permute-done.2.refs_1_
  59.0 1.0 %collective-permute-done.9.refs_2_ = bf16[1,34,16,128]{3,2,1,0:T(8,128)(2,1)S(1)} collective-permute-done((bf16[1,34,16,128]{3,2,1,0:T(8,128)(2,1)S(1)}, bf16[1,34,16,128]{3,2,1,0:T(8,128)(2,1)S(1)}, u32[]{:S(2)}, u32[]{:S(2)}) %collective-permute-start.9) | collective-permute-done | bytes 139296 | tf_op jit(solution)/shard_map/ppermute | solution.py:400
  60.0 2.2 %power.1 = f32[16,24,128]{2,1,0:T(8,128)S(1)} custom-call(bf16[66,16,128]{2,1,0:T(8,128)(2,1)S(1)} %collective-permute-done.refs_0_, bf16[68,16,128]{2,1,0:T(8,128)(2,1)S(1)} %collective-permute-done.2.refs_1_, bf16[1,34,16,128]{3,2,1,0:T(8,128)(2,1)S(1)} %collective-permute-done.9.refs_2_, bf16[32,256,512]{2,1,0:T(8,128)(2,1)S(1)} %bitcast.42, ...), custom_call_target="tpu_custom_call" | custom-call | flops 2147483648 | bytes 8388608 | tf_op jit(solution)/shard_map/power/pallas_call | solution.py:284
  62.2 12.0 %all_to_all.5.parts_ref = f32[16,24,128]{2,1,0:T(8,128)S(1)} all-to-all(f32[16,24,128]{2,1,0:T(8,128)S(1)} %power.1), channel_id=1, replica_groups=mesh['grp'=2,'ka'=16] {'ka'}, dimensions={0} | all-to-all | bytes 393216 | tf_op jit(solution)/shard_map/all_to_all | solution.py:482
  74.2 2.9 %gradients.1 = (f32[32,32]{1,0:T(8,128)}, f32[32,64]{1,0:T(8,128)}, f32[6,512]{1,0:T(8,128)}, f32[512,512]{1,0:T(8,128)}, f32[64,512]{1,0:T(8,128)}) custom-call(f32[16,24,128]{2,1,0:T(8,128)S(1)} %all_to_all.5.parts_ref, f32[6,32]{1,0:T(8,128)S(1)} %copy-done.6, f32[32,64]{1,0:T(8,128)S(1)} %convolution_add_fusion.3.coeffs_ref, ...), custom_call_target="tpu_custom_call" | custom-call | tf_op jit(solution)/shard_map/gradients/pallas_call | solution.py:375
  (43 shorter events, 0.2 us)
Async XLA Ops:
  0.6 20.7 %copy-start = (f32[512,6]{0,1:T(8,128)S(1)}, f32[512,6]{0,1:T(8,128)}, u32[]{:S(2)}) copy-start(f32[512,6]{0,1:T(8,128)} %param.20) | copy-start | bytes 36868
  5.2 24.2 %collective-permute-start.3 = (bf16[66,16,128]{2,1,0:T(8,128)(2,1)}, bf16[66,16,128]{2,1,0:T(8,128)(2,1)S(1)}, u32[]{:S(2)}, u32[]{:S(2)}) collective-permute-start(bf16[66,16,128]{2,1,0:T(8,128)(2,1)} %get-tuple-element.27), channel_id=1, source_target_pairs={{0,8},{1,9},{2,10},{3,11},{4,12},{5,13},{6,14},{7,15},{8,0},{9,1},... | collective-permute-start | bytes 811016 | tf_op jit(solution)/shard_map/ppermute | solution.py:400
  9.3 27.4 %collective-permute-start.4 = (bf16[66,16,128]{2,1,0:T(8,128)(2,1)}, bf16[66,16,128]{2,1,0:T(8,128)(2,1)S(1)}, u32[]{:S(2)}, u32[]{:S(2)}) collective-permute-start(bf16[66,16,128]{2,1,0:T(8,128)(2,1)} %get-tuple-element.28), channel_id=1, source_target_pairs={{0,10},{1,11},{2,8},{3,9},{4,14},{5,15},{6,12},{7,13},{8,2},{9,3},... | collective-permute-start | bytes 811016 | tf_op jit(solution)/shard_map/ppermute | solution.py:400
  10.6 17.5 %collective-permute-start.5 = (bf16[66,16,128]{2,1,0:T(8,128)(2,1)}, bf16[66,16,128]{2,1,0:T(8,128)(2,1)S(1)}, u32[]{:S(2)}, u32[]{:S(2)}) collective-permute-start(bf16[66,16,128]{2,1,0:T(8,128)(2,1)} %get-tuple-element.29), channel_id=1, source_target_pairs={{0,4},{1,5},{2,6},{3,7},{4,0},{5,1},{6,2},{7,3},{8,12},{9,13},{10,... | collective-permute-start | bytes 811016 | tf_op jit(solution)/shard_map/ppermute | solution.py:400
  12.1 9.2 %copy-start.6 = (f32[6,32]{1,0:T(8,128)S(1)}, f32[6,32]{1,0:T(8,128)}, u32[]{:S(2)}) copy-start(f32[6,32]{1,0:T(8,128)} %params_ref.1) | copy-start | bytes 2308
  12.1 9.3 %copy-start.12 = (f32[512]{0:T(512)S(1)}, f32[512]{0:T(512)}, u32[]{:S(2)}) copy-start(f32[512]{0:T(512)} %param.21) | copy-start | bytes 6148
  12.1 9.6 %copy-start.2 = (f32[512,512]{1,0:T(8,128)S(1)}, f32[512,512]{1,0:T(8,128)}, u32[]{:S(2)}) copy-start(f32[512,512]{1,0:T(8,128)} %weight_mid_ref.1) | copy-start | bytes 3145732
  12.1 9.6 %copy-start.11 = (f32[512]{0:T(512)S(1)}, f32[512]{0:T(512)}, u32[]{:S(2)}) copy-start(f32[512]{0:T(512)} %param.23) | copy-start | bytes 6148
  12.1 10.6 %copy-start.5 = (f32[64,512]{1,0:T(8,128)S(1)}, f32[64,512]{1,0:T(8,128)}, u32[]{:S(2)}) copy-start(f32[64,512]{1,0:T(8,128)} %weight_out_ref.1) | copy-start | bytes 393220
  12.2 10.6 %copy-start.13 = (f32[64]{0:T(128)S(1)}, f32[64]{0:T(128)}, u32[]{:S(2)}) copy-start(f32[64]{0:T(128)} %param.25) | copy-start | bytes 772
  12.2 28.4 %copy-start.3 = (f32[32,64]{1,0:T(8,128)S(1)}, f32[32,64]{1,0:T(8,128)}, u32[]{:S(2)}) copy-start(f32[32,64]{1,0:T(8,128)} %basis_ref.1) | copy-start | bytes 24580
  12.2 28.4 %copy-start.8 = (f32[32]{0:T(128)S(1)}, f32[32]{0:T(128)}, u32[]{:S(2)}) copy-start(f32[32]{0:T(128)} %param.27) | copy-start | bytes 388
  12.2 24.5 %collective-permute-start.6 = (bf16[66,16,128]{2,1,0:T(8,128)(2,1)}, bf16[66,16,128]{2,1,0:T(8,128)(2,1)S(1)}, u32[]{:S(2)}, u32[]{:S(2)}) collective-permute-start(bf16[66,16,128]{2,1,0:T(8,128)(2,1)} %get-tuple-element.30), channel_id=1, source_target_pairs={{0,6},{1,7},{2,4},{3,5},{4,2},{5,3},{6,0},{7,1},{8,14},{9,15},{10,... | collective-permute-start | bytes 811016 | tf_op jit(solution)/shard_map/ppermute | solution.py:400
  18.1 3.3 %copy-start.1 = (bf16[32,256,512]{2,1,0:T(8,128)(2,1)}, bf16[32,256,512]{2,1,0:T(8,128)(2,1)S(1)}, u32[]{:S(2)}) copy-start(bf16[32,256,512]{2,1,0:T(8,128)(2,1)S(1)} %get-tuple-element.36.refs_3_) | copy-start | bytes 25165828
  21.4 19.4 %collective-permute-start.1 = (bf16[2,34,16,128]{3,2,1,0:T(8,128)(2,1)}, bf16[2,34,16,128]{3,2,1,0:T(8,128)(2,1)S(1)}, u32[]{:S(2)}, u32[]{:S(2)}) collective-permute-start(bf16[2,34,16,128]{3,2,1,0:T(8,128)(2,1)} %get-tuple-element.26), channel_id=1, source_target_pairs={{0,1},{1,0},{2,3},{3,2},{4,5},{5,4},{6,7},{7,6},{8,9},{9,8},{10,11... | collective-permute-start | bytes 835592 | tf_op jit(solution)/shard_map/ppermute | solution.py:400
  28.1 30.4 %collective-permute-start = (bf16[66,16,128]{2,1,0:T(8,128)(2,1)}, bf16[66,16,128]{2,1,0:T(8,128)(2,1)S(1)}, u32[]{:S(2)}, u32[]{:S(2)}) collective-permute-start(bf16[66,16,128]{2,1,0:T(8,128)(2,1)} %get-tuple-element.24), channel_id=1, source_target_pairs={{0,12},{1,13},{2,14},{3,15},{4,8},{5,9},{6,10},{7,11},{8,4},{9,5},... | collective-permute-start | bytes 811016 | tf_op jit(solution)/shard_map/ppermute | solution.py:400
  29.4 11.0 %collective-permute-start.7 = (bf16[66,16,128]{2,1,0:T(8,128)(2,1)}, bf16[66,16,128]{2,1,0:T(8,128)(2,1)S(1)}, u32[]{:S(2)}, u32[]{:S(2)}) collective-permute-start(bf16[66,16,128]{2,1,0:T(8,128)(2,1)} %get-tuple-element.32), channel_id=1, source_target_pairs={{0,2},{1,3},{2,0},{3,1},{4,6},{5,7},{6,4},{7,5},{8,10},{9,11},{10,... | collective-permute-start | bytes 811016 | tf_op jit(solution)/shard_map/ppermute | solution.py:400
  40.5 19.5 %slice-start = ((s8[8388608]{0:T(1024)(128)(4,1)}), s8[4194304]{0:T(1024)(128)(4,1)S(1)}, s32[]{:S(2)}) async-start(s8[8388608]{0:T(1024)(128)(4,1)} %bitcast.41), calls=%async_computation.1 | async-start | bytes 8388608
  40.5 6.1 %collective-permute-start.8 = (bf16[5,34,16,128]{3,2,1,0:T(8,128)(2,1)S(1)}, bf16[5,34,16,128]{3,2,1,0:T(8,128)(2,1)S(1)}, u32[]{:S(2)}, u32[]{:S(2)}) collective-permute-start(bf16[5,34,16,128]{3,2,1,0:T(8,128)(2,1)S(1)} %fusion), channel_id=1, source_target_pairs={{0,1},{1,0},{2,3},{3,2},{4,5},{5,4},{6,7},{7,6},{8,9},{9,8},{10,11... | collective-permute-start | bytes 2088968 | tf_op jit(solution)/shard_map/ppermute | solution.py:400
  40.8 18.1 %collective-permute-start.2 = (bf16[68,16,128]{2,1,0:T(8,128)(2,1)S(1)}, bf16[68,16,128]{2,1,0:T(8,128)(2,1)S(1)}, u32[]{:S(2)}, u32[]{:S(2)}) collective-permute-start(bf16[68,16,128]{2,1,0:T(8,128)(2,1)S(1)} %pad_maximum_fusion), channel_id=1, source_target_pairs={{0,14},{1,15},{2,12},{3,13},{4,10},{5,11},{6,8},{7,9},{8,6},{9,7},... | collective-permute-start | bytes 835592 | tf_op jit(solution)/shard_map/ppermute | solution.py:400
  46.5 0.9 %copy-start.4 = (bf16[34,16,128]{2,1,0:T(8,128)(2,1)S(1)}, bf16[34,16,128]{2,1,0:T(8,128)(2,1)}, u32[]{:S(2)}) copy-start(bf16[34,16,128]{2,1,0:T(8,128)(2,1)} %get-tuple-element.33.refs_2_) | copy-start | bytes 417796
  47.4 12.5 %slice-start.1 = ((s8[8388608]{0:T(1024)(128)(4,1)}), s8[4194304]{0:T(1024)(128)(4,1)S(1)}, s32[]{:S(2)}) async-start(s8[8388608]{0:T(1024)(128)(4,1)} %bitcast.41), calls=%async_computation.2 | async-start | bytes 8388608
  47.4 12.5 %copy-start.9 = (s32[32]{0:T(128)S(1)}, s32[32]{0:T(128)}, u32[]{:S(2)}) copy-start(s32[32]{0:T(128)} %param.17) | copy-start | bytes 388
  47.4 12.5 %copy-start.10 = (s32[32]{0:T(128)S(1)}, s32[32]{0:T(128)}, u32[]{:S(2)}) copy-start(s32[32]{0:T(128)} %param.18) | copy-start | bytes 388
  58.5 15.6 %copy-start.7 = (s32[32]{0:T(128)S(1)}, s32[32]{0:T(128)}, u32[]{:S(2)}) copy-start(s32[32]{0:T(128)} %param.16) | copy-start | bytes 388
  58.5 1.4 %collective-permute-start.9 = (bf16[1,34,16,128]{3,2,1,0:T(8,128)(2,1)S(1)}, bf16[1,34,16,128]{3,2,1,0:T(8,128)(2,1)S(1)}, u32[]{:S(2)}, u32[]{:S(2)}) collective-permute-start(bf16[1,34,16,128]{3,2,1,0:T(8,128)(2,1)S(1)} %slice_bitcast_fusion.5), channel_id=1, source_target_pairs={{0,1},{1,0},{2,3},{3,2},{4,5},{5,4},{6,7},{7,6},{8,9},{9,8},{10,11... | collective-permute-start | bytes 417800 | tf_op jit(solution)/shard_map/ppermute | solution.py:400

commit v4 on v3

--- a/solution.py
+++ b/solution.py
@@ -331,6 +331,16 @@
     return rows * strips // (strips + 1) if strips else rows
 
 
+def near_mat(left, right, dims=((1,), (0,))):
+    left_high, left_low = split_two(left)
+    right_high, right_low = split_two(right)
+    parts = ((left_low, right_high), (left_high, right_low), (left_high, right_high))
+    return sum(
+        lax.dot_general(one, other, (dims, ((), ())), preferred_element_type=jnp.float32)
+        for one, other in parts
+    )
+
+
 def gradients_kernel(
     parts_ref,
     params_ref,
@@ -344,56 +354,53 @@
     basis_ref,
     offset_ref,
     multipoles_ref,
-    spectra_ref,
-    grad_basis_ref,
-    grad_in_ref,
-    grad_mid_ref,
-    grad_out_ref,
+    *refs,
 ):
+    out_refs, (*value_refs, sems) = refs[:5], refs[5:]
     cosmos = params_ref.shape[1]
     owned, comps = basis_ref.shape
+    copies = []
+
+    def store(number, value):
+        value_refs[number][...] = value
+        copy = pltpu.make_async_copy(value_refs[number], out_refs[number], sems.at[number])
+        copy.start()
+        copies.append(copy)
+
+    rows = ((0,), (0,))
     summed = unfold(jnp.sum(parts_ref[...], axis=0), cosmos, owned + comps)
+    coef_grad = summed[:, owned : owned + comps] / cosmos
+    middle_delta = near_mat(coef_grad, weight_out_ref[...]) * middle_slope_ref[...]
+    store(3, near_mat(middle_delta, inner_act_ref[...], rows))
+    inner_delta = near_mat(middle_delta, weight_mid_ref[...]) * inner_slope_ref[...]
+    store(4, near_mat(coef_grad, middle_act_ref[...], rows))
     spectra = summed[:, :owned] * smoothing_of(multipoles_ref[...])
-    coef_grad = summed[:, owned : owned + comps] / cosmos
     coeffs = coeffs_ref[...]
-    residual = offset_ref[...] + mat(coeffs, basis_ref[...], ((1,), (1,))) - spectra
-    middle_delta = mat(coef_grad, weight_out_ref[...]) * middle_slope_ref[...]
-    inner_delta = mat(middle_delta, weight_mid_ref[...]) * inner_slope_ref[...]
-    rows = ((0,), (0,))
-    spectra_ref[...] = spectra.T
-    grad_basis_ref[...] = mat(residual, coeffs, rows) / cosmos
-    grad_out_ref[...] = mat(coef_grad, middle_act_ref[...], rows)
-    grad_mid_ref[...] = mat(middle_delta, inner_act_ref[...], rows)
-    grad_in_ref[...] = mat(params_ref[...], inner_delta)
+    residual = offset_ref[...] + near_mat(coeffs, basis_ref[...], ((1,), (1,))) - spectra
+    store(0, spectra.T)
+    store(1, near_mat(residual, coeffs, rows) / cosmos)
+    store(2, near_mat(params_ref[...], inner_delta))
+    for copy in copies:
+        copy.wait()
 
 
 def gradients(parts, params, coeffs, hidden, weight_mid, weight_out, basis, offset, multipoles):
     count, cosmos = params.shape
     owned, comps = basis.shape
     width = weight_mid.shape[0]
-    shape = lambda *dims: jax.ShapeDtypeStruct(dims, jnp.float32)
+    shapes = ((owned, cosmos), (owned, comps), (count, width), (width, width), (comps, width))
+    operands = (parts, params, coeffs, *hidden, weight_mid, weight_out, basis)
+    operands += (offset.reshape(1, owned), multipoles)
     return pl.pallas_call(
         gradients_kernel,
-        out_shape=(
-            shape(owned, cosmos),
-            shape(owned, comps),
-            shape(count, width),
-            shape(width, width),
-            shape(comps, width),
-        ),
-        compiler_params=pltpu.CompilerParams(vmem_limit_bytes=48 << 20),
+        in_specs=[pl.BlockSpec(memory_space=pltpu.VMEM)] * len(operands),
+        out_specs=[pl.BlockSpec(memory_space=pl.ANY)] * len(shapes),
+        out_shape=[jax.ShapeDtypeStruct(shape, jnp.float32) for shape in shapes],
+        scratch_shapes=[pltpu.VMEM(shape, jnp.float32) for shape in shapes]
+        + [pltpu.SemaphoreType.DMA((len(shapes),))],
+        compiler_params=pltpu.CompilerParams(vmem_limit_bytes=24 << 20),
         name="gradients",
-    )(
-        parts,
-        params,
-        coeffs,
-        *hidden,
-        weight_mid,
-        weight_out,
-        basis,
-        offset.reshape(1, owned),
-        multipoles,
-    )
+    )(*operands)
 
 
 def exchange(value, apart, peers):
@@ -440,7 +447,6 @@
     *rest_ready, give = arrange(*arranged, TOPS[FIRST:], group, last, HELD)
     held, rest_ready = dict(zip(HELD, rest_ready)), rest_ready[len(HELD) :]
     ready = dict(zip(chips, [*ready, *rest_ready]))
-    given = exchange(give, 1, peers)
     got = {}
     near = [chip for chip in chips if 0 < chip < half]
     for chip in chips:
@@ -448,8 +454,9 @@
             continue
         value = ready[chip]
         if chip in near:
-            value = after(value, got[half + near.index(chip)])
+            value = after(value, got[TOPS[0] * half])
         got[chip] = exchange(value, 2 * chip, peers)
+    given = exchange(after(give, got[TOPS[0] * half]), 1, peers)
     mine, other = ready[last], given[1]
     value = jnp.concatenate([mine[:waves], other[:waves], mine[waves:], other[waves:]])
     got[last] = exchange(value, 2 * last, peers)

time: 77.5 us -> 76.9 us (level)
  waiting for transfers between devices: 13.9 us -> 13 us
  starting transfers between devices: 16.1 us -> 16.9 us
    ppermute x10, starting transfers between devices: 16.1 us -> 16.9 us  [exchange(): lax.ppermute(value, 'ka', [(peer, peer ^ apart) for peer in range(peers)])]
    ppermute x10, waiting for transfers between devices: 13.9 us -> 13 us  [exchange(): lax.ppermute(value, 'ka', [(peer, peer ^ apart) for peer in range(peers)])]
where the time goes in v4:
time: 76.9 us; the launch traced here: 76.5 us
  Pallas kernels  25.8 us (34%)
  starting transfers between devices  16.9 us (22%)
  waiting for transfers between devices  13 us (17%)
  blocking collectives  12 us (16%)
  local copies, waits for them, and re-layouts  5.97 us (8%)
  matrix products  1.87 us (2%)
  between operations  0.91 us (1%)
    ppermute x10, starting transfers between devices, exchange(): lax.ppermute(value, 'ka', [(peer, peer ^ apart) for peer in range(peers)])  16.9 us
    ppermute x10, waiting for transfers between devices, exchange(): lax.ppermute(value, 'ka', [(peer, peer ^ apart) for peer in range(peers)])  13 us
    all_to_all x1, blocking collectives, local(): lax.all_to_all(parts, 'ka', split_axis=0, concat_axis=0, tiled=True)  12 us
    pallas_call x1, Pallas kernels, add_groups(): pl.pallas_call(functools.partial(transfer_kernel, group, members, times),...  11.1 us
    pallas_call x2, Pallas kernels, arrange(): pl.pallas_call(functools.partial(arrange_kernel, tops, group, last, waves...  10.2 us
    unnamed x36, local copies, waits for them, and re-layouts  4.32 us
    pallas_call x1, Pallas kernels, gradients(): pl.pallas_call(gradients_kernel, in_specs=[pl.BlockSpec(memory_space=pltp...  2.36 us
    pallas_call x1, Pallas kernels, power_parts(): pl.pallas_call(functools.partial(power_kernel, times, chips, total_waves)...  2.17 us
  transfers between devices with their start and end apart: 10, of which 4 were waited for; matrix products, arithmetic and copies ran while one was open for 5% of the time, Pallas kernels for 22%

profile of v4, /device:TPU:0, one launch (start us, length us, event | category | flops | bytes accessed | tf_op | source)
XLA Modules:
  0.0 76.5 jit_solution(14710014140369374015)
XLA Ops:
  0.6 0.0 copy-start
  0.6 4.5 %arrange.3 = (bf16[66,16,128]{2,1,0:T(8,128)(2,1)}, bf16[66,16,128]{2,1,0:T(8,128)(2,1)}, bf16[66,16,128]{2,1,0:T(8,128)(2,1)}, bf16[66,16,128]{2,1,0:T(8,128)(2,1)}) custom-call(bf16[64,32,512]{2,1,0:T(8,128)(2,1)} %bitcast.49, s32[1,32]{1,0:T(1,128)} %bitcast.43, f32[32,64]{1,0:T(8,128)} %basis_ref.1, bf16[32,1024,512]{2,1,0:T(8,128)(2,1)} %refs_10_.1), custom_call_target="tpu_custom_call" | custom-call | bytes 8388608 | tf_op jit(solution)/shard_map/arrange/pallas_call | solution.py:121
  5.2 4.1 %collective-permute-start.1 = (bf16[66,16,128]{2,1,0:T(8,128)(2,1)}, bf16[66,16,128]{2,1,0:T(8,128)(2,1)S(1)}, u32[]{:S(2)}, u32[]{:S(2)}) collective-permute-start(bf16[66,16,128]{2,1,0:T(8,128)(2,1)} %get-tuple-element.28), channel_id=1, source_target_pairs={{0,8},{1,9},{2,10},{3,11},{4,12},{5,13},{6,14},{7,15},{8,0},{9,1},... | collective-permute-start | bytes 811016 | tf_op jit(solution)/shard_map/ppermute | solution.py:407
  9.3 1.3 %collective-permute-start.4 = (bf16[66,16,128]{2,1,0:T(8,128)(2,1)}, bf16[66,16,128]{2,1,0:T(8,128)(2,1)S(1)}, u32[]{:S(2)}, u32[]{:S(2)}) collective-permute-start(bf16[66,16,128]{2,1,0:T(8,128)(2,1)} %get-tuple-element.30), channel_id=1, source_target_pairs={{0,10},{1,11},{2,8},{3,9},{4,14},{5,15},{6,12},{7,13},{8,2},{9,3},... | collective-permute-start | bytes 811016 | tf_op jit(solution)/shard_map/ppermute | solution.py:407
  10.6 1.6 %collective-permute-start.5 = (bf16[66,16,128]{2,1,0:T(8,128)(2,1)}, bf16[66,16,128]{2,1,0:T(8,128)(2,1)S(1)}, u32[]{:S(2)}, u32[]{:S(2)}) collective-permute-start(bf16[66,16,128]{2,1,0:T(8,128)(2,1)} %get-tuple-element.31), channel_id=1, source_target_pairs={{0,4},{1,5},{2,6},{3,7},{4,0},{5,1},{6,2},{7,3},{8,12},{9,13},{10,... | collective-permute-start | bytes 811016 | tf_op jit(solution)/shard_map/ppermute | solution.py:407
  12.1 0.0 copy-start.5
  12.2 0.2 collective-permute-start.6
  12.4 5.7 %arrange.2 = (bf16[32,256,512]{2,1,0:T(8,128)(2,1)S(1)}, bf16[34,16,128]{2,1,0:T(8,128)(2,1)}, bf16[66,16,128]{2,1,0:T(8,128)(2,1)}, bf16[66,16,128]{2,1,0:T(8,1...) custom-call(bf16[64,32,512]{2,1,0:T(8,128)(2,1)} %bitcast.50, s32[1,32]{1,0:T(1,128)} %bitcast.44, ...), custom_call_target="tpu_custom_call" | custom-call | bytes 8388608 | tf_op jit(solution)/shard_map/arrange/pallas_call | solution.py:121
  18.1 3.3 %copy-done.1 = bf16[32,256,512]{2,1,0:T(8,128)(2,1)} copy-done((bf16[32,256,512]{2,1,0:T(8,128)(2,1)}, bf16[32,256,512]{2,1,0:T(8,128)(2,1)S(1)}, u32[]{:S(2)}) %copy-start.1) | copy-done | bytes 8388632
  21.4 3.7 %collective-permute-start = (bf16[66,16,128]{2,1,0:T(8,128)(2,1)}, bf16[66,16,128]{2,1,0:T(8,128)(2,1)S(1)}, u32[]{:S(2)}, u32[]{:S(2)}) collective-permute-start(bf16[66,16,128]{2,1,0:T(8,128)(2,1)} %get-tuple-element.25), channel_id=1, source_target_pairs={{0,12},{1,13},{2,14},{3,15},{4,8},{5,9},{6,10},{7,11},{8,4},{9,5},... | collective-permute-start | bytes 811016 | tf_op jit(solution)/shard_map/ppermute | solution.py:407
  25.1 0.3 add_multiply_fusion.1
  25.4 1.1 %add_multiply_fusion = (f32[32,512]{1,0:T(8,128)S(1)}, f32[32,512]{1,0:T(8,128)S(1)}, f32[32,512]{1,0:T(8,128)S(1)}) fusion(f32[512]{0:T(512)S(1)} %copy-done.11, f32[512,512]{1,0:T(8,128)S(1)} %copy-done.2, f32[32,512]{1,0:T(8,128)S(1)} %get-tuple-element.49), kind=kOutput, calls=%fused_computation.17 | convolution fusion | flops 100876288 | bytes 1312768 | tf_op jit(solution)/shard_map/dot_general | solution.py:25
  26.5 0.2 convolution_add_fusion.3.coeffs_ref
  26.7 0.9 %slice.39 = bf16[32,16,128]{2,1,0:T(8,128)(2,1)S(1)} slice(bf16[34,16,128]{2,1,0:T(8,128)(2,1)} %get-tuple-element.26), slice={[0:32], [0:16], [0:128]} | slice | bytes 262144 | tf_op jit(solution)/shard_map/slice | solution.py:461
  27.6 0.7 slice.42
  28.3 0.1 collective-permute-done.1.refs_3_
  28.5 1.9 %collective-permute-start.7 = (bf16[66,16,128]{2,1,0:T(8,128)(2,1)}, bf16[66,16,128]{2,1,0:T(8,128)(2,1)S(1)}, u32[]{:S(2)}, u32[]{:S(2)}) collective-permute-start(bf16[66,16,128]{2,1,0:T(8,128)(2,1)} %get-tuple-element.34), channel_id=1, source_target_pairs={{0,2},{1,3},{2,0},{3,1},{4,6},{5,7},{6,4},{7,5},{8,10},{9,11},{10,... | collective-permute-start | bytes 811016 | tf_op jit(solution)/shard_map/ppermute | solution.py:407
  30.4 10.9 %collective-permute-done.4.refs_4_ = bf16[66,16,128]{2,1,0:T(8,128)(2,1)S(1)} collective-permute-done((bf16[66,16,128]{2,1,0:T(8,128)(2,1)}, bf16[66,16,128]{2,1,0:T(8,128)(2,1)S(1)}, u32[]{:S(2)}, u32[]{:S(2)}) %collective-permute-start.4) | collective-permute-done | bytes 270368 | tf_op jit(solution)/shard_map/ppermute | solution.py:407
  41.5 0.6 collective-permute-start.8
  42.1 0.1 convolution_add_fusion.2
  42.2 0.9 %collective-permute-done.2.refs_1_ = bf16[2,34,16,128]{3,2,1,0:T(8,128)(2,1)S(1)} collective-permute-done((bf16[2,34,16,128]{3,2,1,0:T(8,128)(2,1)}, bf16[2,34,16,128]{3,2,1,0:T(8,128)(2,1)S(1)}, u32[]{:S(2)}, u32[]{:S(2)}) %collective-permute-start.2) | collective-permute-done | bytes 278560 | tf_op jit(solution)/shard_map/ppermute | solution.py:407
  43.1 0.1 pad_maximum_fusion
  43.2 3.3 %collective-permute-start.3 = (bf16[68,16,128]{2,1,0:T(8,128)(2,1)S(1)}, bf16[68,16,128]{2,1,0:T(8,128)(2,1)S(1)}, u32[]{:S(2)}, u32[]{:S(2)}) collective-permute-start(bf16[68,16,128]{2,1,0:T(8,128)(2,1)S(1)} %pad_maximum_fusion), channel_id=1, source_target_pairs={{0,14},{1,15},{2,12},{3,13},{4,10},{5,11},{6,8},{7,9},{8,6},{9,7},... | collective-permute-start | bytes 835592 | tf_op jit(solution)/shard_map/ppermute | solution.py:407
  46.5 0.9 %copy-done.4 = bf16[34,16,128]{2,1,0:T(8,128)(2,1)S(1)} copy-done((bf16[34,16,128]{2,1,0:T(8,128)(2,1)S(1)}, bf16[34,16,128]{2,1,0:T(8,128)(2,1)}, u32[]{:S(2)}) %copy-start.4) | copy-done | bytes 139288
  47.4 11.1 %transfer.1 = (f32[32,32,512]{2,1,0:T(8,128)S(1)}, bf16[16,32,128]{2,1,0:T(8,128)(2,1)S(1)}) custom-call(s32[1]{0:T(128)} %bitcast.4.me_ref, bf16[5,34,16,128]{3,2,1,0:T(8,128)(2,1)S(1)} %collective-permute-done.8.refs_0_, bf16[2,34,16,128]{3,2,1,0:T(8,128)(2,1)S(1)} %collective-permute-done.2.refs_1_, bf16[34,16,128]{2,1,0:T(8,128)(2,1)S(1)} %copy-done.4, ...), custom_call_target="tpu_custom_call" | custom-call | flops 8589934592 | bytes 33554432 | tf_op jit(solution)/shard_map/transfer/pallas_call | solution.py:197
  58.5 0.3 collective-permute-start.9
  58.8 0.1 fusion.9.refs_9_
  58.9 0.0 collective-permute-done.3.refs_1_
  58.9 1.0 %collective-permute-done.9.refs_2_ = bf16[1,34,16,128]{3,2,1,0:T(8,128)(2,1)S(1)} collective-permute-done((bf16[1,34,16,128]{3,2,1,0:T(8,128)(2,1)S(1)}, bf16[1,34,16,128]{3,2,1,0:T(8,128)(2,1)S(1)}, u32[]{:S(2)}, u32[]{:S(2)}) %collective-permute-start.9) | collective-permute-done | bytes 139296 | tf_op jit(solution)/shard_map/ppermute | solution.py:407
  60.0 2.2 %power.1 = f32[16,24,128]{2,1,0:T(8,128)S(1)} custom-call(bf16[66,16,128]{2,1,0:T(8,128)(2,1)S(1)} %collective-permute-done.refs_0_, bf16[68,16,128]{2,1,0:T(8,128)(2,1)S(1)} %collective-permute-done.3.refs_1_, bf16[1,34,16,128]{3,2,1,0:T(8,128)(2,1)S(1)} %collective-permute-done.9.refs_2_, bf16[32,256,512]{2,1,0:T(8,128)(2,1)S(1)} %bitcast.42, ...), custom_call_target="tpu_custom_call" | custom-call | flops 2147483648 | bytes 8388608 | tf_op jit(solution)/shard_map/power/pallas_call | solution.py:284
  62.2 12.0 %all_to_all.5.parts_ref = f32[16,24,128]{2,1,0:T(8,128)S(1)} all-to-all(f32[16,24,128]{2,1,0:T(8,128)S(1)} %power.1), channel_id=1, replica_groups=mesh['grp'=2,'ka'=16] {'ka'}, dimensions={0} | all-to-all | bytes 393216 | tf_op jit(solution)/shard_map/all_to_all | solution.py:489
  74.1 2.4 %gradients.1 = (f32[32,32]{1,0:T(8,128)}, f32[32,64]{1,0:T(8,128)}, f32[6,512]{1,0:T(8,128)}, f32[512,512]{1,0:T(8,128)}, f32[64,512]{1,0:T(8,128)}) custom-call(f32[16,24,128]{2,1,0:T(8,128)S(1)} %all_to_all.5.parts_ref, f32[6,32]{1,0:T(8,128)S(1)} %copy-done.6, f32[32,64]{1,0:T(8,128)S(1)} %convolution_add_fusion.3.coeffs_ref, ...), custom_call_target="tpu_custom_call" | custom-call | tf_op jit(solution)/shard_map/gradients/pallas_call | solution.py:394
  (43 shorter events, 0.2 us)
Async XLA Ops:
  0.6 24.4 %copy-start = (f32[512,6]{0,1:T(8,128)S(1)}, f32[512,6]{0,1:T(8,128)}, u32[]{:S(2)}) copy-start(f32[512,6]{0,1:T(8,128)} %param.20) | copy-start | bytes 36868
  5.2 23.3 %collective-permute-start.1 = (bf16[66,16,128]{2,1,0:T(8,128)(2,1)}, bf16[66,16,128]{2,1,0:T(8,128)(2,1)S(1)}, u32[]{:S(2)}, u32[]{:S(2)}) collective-permute-start(bf16[66,16,128]{2,1,0:T(8,128)(2,1)} %get-tuple-element.28), channel_id=1, source_target_pairs={{0,8},{1,9},{2,10},{3,11},{4,12},{5,13},{6,14},{7,15},{8,0},{9,1},... | collective-permute-start | bytes 811016 | tf_op jit(solution)/shard_map/ppermute | solution.py:407
  9.3 32.1 %collective-permute-start.4 = (bf16[66,16,128]{2,1,0:T(8,128)(2,1)}, bf16[66,16,128]{2,1,0:T(8,128)(2,1)S(1)}, u32[]{:S(2)}, u32[]{:S(2)}) collective-permute-start(bf16[66,16,128]{2,1,0:T(8,128)(2,1)} %get-tuple-element.30), channel_id=1, source_target_pairs={{0,10},{1,11},{2,8},{3,9},{4,14},{5,15},{6,12},{7,13},{8,2},{9,3},... | collective-permute-start | bytes 811016 | tf_op jit(solution)/shard_map/ppermute | solution.py:407
  10.6 30.8 %collective-permute-start.5 = (bf16[66,16,128]{2,1,0:T(8,128)(2,1)}, bf16[66,16,128]{2,1,0:T(8,128)(2,1)S(1)}, u32[]{:S(2)}, u32[]{:S(2)}) collective-permute-start(bf16[66,16,128]{2,1,0:T(8,128)(2,1)} %get-tuple-element.31), channel_id=1, source_target_pairs={{0,4},{1,5},{2,6},{3,7},{4,0},{5,1},{6,2},{7,3},{8,12},{9,13},{10,... | collective-permute-start | bytes 811016 | tf_op jit(solution)/shard_map/ppermute | solution.py:407
  12.1 12.9 %copy-start.6 = (f32[6,32]{1,0:T(8,128)S(1)}, f32[6,32]{1,0:T(8,128)}, u32[]{:S(2)}) copy-start(f32[6,32]{1,0:T(8,128)} %params_ref.1) | copy-start | bytes 2308
  12.1 12.9 %copy-start.12 = (f32[512]{0:T(512)S(1)}, f32[512]{0:T(512)}, u32[]{:S(2)}) copy-start(f32[512]{0:T(512)} %param.21) | copy-start | bytes 6148
  12.1 13.2 %copy-start.2 = (f32[512,512]{1,0:T(8,128)S(1)}, f32[512,512]{1,0:T(8,128)}, u32[]{:S(2)}) copy-start(f32[512,512]{1,0:T(8,128)} %weight_mid_ref.1) | copy-start | bytes 3145732
  12.1 13.2 %copy-start.11 = (f32[512]{0:T(512)S(1)}, f32[512]{0:T(512)}, u32[]{:S(2)}) copy-start(f32[512]{0:T(512)} %param.23) | copy-start | bytes 6148
  12.1 14.3 %copy-start.5 = (f32[64,512]{1,0:T(8,128)S(1)}, f32[64,512]{1,0:T(8,128)}, u32[]{:S(2)}) copy-start(f32[64,512]{1,0:T(8,128)} %weight_out_ref.1) | copy-start | bytes 393220
  12.2 14.3 %copy-start.13 = (f32[64]{0:T(128)S(1)}, f32[64]{0:T(128)}, u32[]{:S(2)}) copy-start(f32[64]{0:T(128)} %param.25) | copy-start | bytes 772
  12.2 29.9 %copy-start.3 = (f32[32,64]{1,0:T(8,128)S(1)}, f32[32,64]{1,0:T(8,128)}, u32[]{:S(2)}) copy-start(f32[32,64]{1,0:T(8,128)} %basis_ref.1) | copy-start | bytes 24580
  12.2 29.9 %copy-start.8 = (f32[32]{0:T(128)S(1)}, f32[32]{0:T(128)}, u32[]{:S(2)}) copy-start(f32[32]{0:T(128)} %param.27) | copy-start | bytes 388
  12.2 29.2 %collective-permute-start.6 = (bf16[66,16,128]{2,1,0:T(8,128)(2,1)}, bf16[66,16,128]{2,1,0:T(8,128)(2,1)S(1)}, u32[]{:S(2)}, u32[]{:S(2)}) collective-permute-start(bf16[66,16,128]{2,1,0:T(8,128)(2,1)} %get-tuple-element.32), channel_id=1, source_target_pairs={{0,6},{1,7},{2,4},{3,5},{4,2},{5,3},{6,0},{7,1},{8,14},{9,15},{10,... | collective-permute-start | bytes 811016 | tf_op jit(solution)/shard_map/ppermute | solution.py:407
  18.1 3.3 %copy-start.1 = (bf16[32,256,512]{2,1,0:T(8,128)(2,1)}, bf16[32,256,512]{2,1,0:T(8,128)(2,1)S(1)}, u32[]{:S(2)}) copy-start(bf16[32,256,512]{2,1,0:T(8,128)(2,1)S(1)} %get-tuple-element.38.refs_3_) | copy-start | bytes 25165828
  21.4 37.1 %collective-permute-start = (bf16[66,16,128]{2,1,0:T(8,128)(2,1)}, bf16[66,16,128]{2,1,0:T(8,128)(2,1)S(1)}, u32[]{:S(2)}, u32[]{:S(2)}) collective-permute-start(bf16[66,16,128]{2,1,0:T(8,128)(2,1)} %get-tuple-element.25), channel_id=1, source_target_pairs={{0,12},{1,13},{2,14},{3,15},{4,8},{5,9},{6,10},{7,11},{8,4},{9,5},... | collective-permute-start | bytes 811016 | tf_op jit(solution)/shard_map/ppermute | solution.py:407
  28.5 13.0 %collective-permute-start.7 = (bf16[66,16,128]{2,1,0:T(8,128)(2,1)}, bf16[66,16,128]{2,1,0:T(8,128)(2,1)S(1)}, u32[]{:S(2)}, u32[]{:S(2)}) collective-permute-start(bf16[66,16,128]{2,1,0:T(8,128)(2,1)} %get-tuple-element.34), channel_id=1, source_target_pairs={{0,2},{1,3},{2,0},{3,1},{4,6},{5,7},{6,4},{7,5},{8,10},{9,11},{10,... | collective-permute-start | bytes 811016 | tf_op jit(solution)/shard_map/ppermute | solution.py:407
  41.3 1.8 %collective-permute-start.2 = (bf16[2,34,16,128]{3,2,1,0:T(8,128)(2,1)}, bf16[2,34,16,128]{3,2,1,0:T(8,128)(2,1)S(1)}, u32[]{:S(2)}, u32[]{:S(2)}) collective-permute-start(bf16[2,34,16,128]{3,2,1,0:T(8,128)(2,1)} %get-tuple-element.29), channel_id=1, source_target_pairs={{0,1},{1,0},{2,3},{3,2},{4,5},{5,4},{6,7},{7,6},{8,9},{9,8},{10,11... | collective-permute-start | bytes 835592 | tf_op jit(solution)/shard_map/ppermute | solution.py:407
  41.5 18.5 %slice-start = ((s8[8388608]{0:T(1024)(128)(4,1)}), s8[4194304]{0:T(1024)(128)(4,1)S(1)}, s32[]{:S(2)}) async-start(s8[8388608]{0:T(1024)(128)(4,1)} %bitcast.41), calls=%async_computation.1 | async-start | bytes 8388608
  41.5 5.0 %collective-permute-start.8 = (bf16[5,34,16,128]{3,2,1,0:T(8,128)(2,1)S(1)}, bf16[5,34,16,128]{3,2,1,0:T(8,128)(2,1)S(1)}, u32[]{:S(2)}, u32[]{:S(2)}) collective-permute-start(bf16[5,34,16,128]{3,2,1,0:T(8,128)(2,1)S(1)} %fusion), channel_id=1, source_target_pairs={{0,1},{1,0},{2,3},{3,2},{4,5},{5,4},{6,7},{7,6},{8,9},{9,8},{10,11... | collective-permute-start | bytes 2088968 | tf_op jit(solution)/shard_map/ppermute | solution.py:407
  43.2 15.8 %collective-permute-start.3 = (bf16[68,16,128]{2,1,0:T(8,128)(2,1)S(1)}, bf16[68,16,128]{2,1,0:T(8,128)(2,1)S(1)}, u32[]{:S(2)}, u32[]{:S(2)}) collective-permute-start(bf16[68,16,128]{2,1,0:T(8,128)(2,1)S(1)} %pad_maximum_fusion), channel_id=1, source_target_pairs={{0,14},{1,15},{2,12},{3,13},{4,10},{5,11},{6,8},{7,9},{8,6},{9,7},... | collective-permute-start | bytes 835592 | tf_op jit(solution)/shard_map/ppermute | solution.py:407
  46.5 0.9 %copy-start.4 = (bf16[34,16,128]{2,1,0:T(8,128)(2,1)S(1)}, bf16[34,16,128]{2,1,0:T(8,128)(2,1)}, u32[]{:S(2)}) copy-start(bf16[34,16,128]{2,1,0:T(8,128)(2,1)} %get-tuple-element.35.refs_2_) | copy-start | bytes 417796
  47.4 12.5 %slice-start.1 = ((s8[8388608]{0:T(1024)(128)(4,1)}), s8[4194304]{0:T(1024)(128)(4,1)S(1)}, s32[]{:S(2)}) async-start(s8[8388608]{0:T(1024)(128)(4,1)} %bitcast.41), calls=%async_computation.2 | async-start | bytes 8388608
  47.4 12.5 %copy-start.9 = (s32[32]{0:T(128)S(1)}, s32[32]{0:T(128)}, u32[]{:S(2)}) copy-start(s32[32]{0:T(128)} %param.17) | copy-start | bytes 388
  47.4 12.5 %copy-start.10 = (s32[32]{0:T(128)S(1)}, s32[32]{0:T(128)}, u32[]{:S(2)}) copy-start(s32[32]{0:T(128)} %param.18) | copy-start | bytes 388
  58.5 15.6 %copy-start.7 = (s32[32]{0:T(128)S(1)}, s32[32]{0:T(128)}, u32[]{:S(2)}) copy-start(s32[32]{0:T(128)} %param.16) | copy-start | bytes 388
  58.5 1.4 %collective-permute-start.9 = (bf16[1,34,16,128]{3,2,1,0:T(8,128)(2,1)S(1)}, bf16[1,34,16,128]{3,2,1,0:T(8,128)(2,1)S(1)}, u32[]{:S(2)}, u32[]{:S(2)}) collective-permute-start(bf16[1,34,16,128]{3,2,1,0:T(8,128)(2,1)S(1)} %slice_bitcast_fusion.5), channel_id=1, source_target_pairs={{0,1},{1,0},{2,3},{3,2},{4,5},{5,4},{6,7},{7,6},{8,9},{9,8},{10,11... | collective-permute-start | bytes 417800 | tf_op jit(solution)/shard_map/ppermute | solution.py:407

commit v5 on v4

--- a/solution.py
+++ b/solution.py
@@ -81,7 +81,8 @@
     chips = [top * group // 2 + low for top in tops for low in range(group // 2)]
     for slot, copy in enumerate(copies):
         copy.wait()
-        rows_ref[...] = block_ref[slot].astype(jnp.float32).reshape(times * cosmos, block)
+        rows = block_ref[slot].astype(jnp.float32).reshape(times * cosmos, block)
+        rows_ref[: times * cosmos] = rows
         for low in range(low_count):
             pieces = [
                 rows_ref[pl.ds(high * low_count + low, times, stride=cosmos), :]
@@ -126,8 +127,8 @@
         + [jax.ShapeDtypeStruct(shape, jnp.bfloat16) for shape in shapes],
         scratch_shapes=[
             pltpu.VMEM((len(tops), times, cosmos, block), jnp.bfloat16),
-            pltpu.VMEM((times * cosmos, block), jnp.float32),
-            pltpu.VMEM((block * low_count, LANES), jnp.float32),
+            pltpu.VMEM(((times + 1) * cosmos, block), jnp.float32),
+            pltpu.VMEM(((block + 1) * low_count, LANES), jnp.float32),
             pltpu.SemaphoreType.DMA((len(tops),)),
             pltpu.SemaphoreType.DMA((max(1, len(held_tops)),)),
         ],

time: 76.9 us -> 76.9 us (level)
  no operation moved by 1% of the time
where the time goes in v5:
time: 76.9 us; the launch traced here: 76.5 us
  Pallas kernels  25.8 us (34%)
  starting transfers between devices  16.9 us (22%)
  waiting for transfers between devices  13 us (17%)
  blocking collectives  12 us (16%)
  local copies, waits for them, and re-layouts  5.97 us (8%)
  matrix products  1.87 us (2%)
  between operations  0.91 us (1%)
    ppermute x10, starting transfers between devices, exchange(): lax.ppermute(value, 'ka', [(peer, peer ^ apart) for peer in range(peers)])  16.9 us
    ppermute x10, waiting for transfers between devices, exchange(): lax.ppermute(value, 'ka', [(peer, peer ^ apart) for peer in range(peers)])  13 us
    all_to_all x1, blocking collectives, local(): lax.all_to_all(parts, 'ka', split_axis=0, concat_axis=0, tiled=True)  12 us
    pallas_call x1, Pallas kernels, add_groups(): pl.pallas_call(functools.partial(transfer_kernel, group, members, times),...  11.1 us
    pallas_call x2, Pallas kernels, arrange(): pl.pallas_call(functools.partial(arrange_kernel, tops, group, last, waves...  10.2 us
    unnamed x36, local copies, waits for them, and re-layouts  4.32 us
    pallas_call x1, Pallas kernels, gradients(): pl.pallas_call(gradients_kernel, in_specs=[pl.BlockSpec(memory_space=pltp...  2.36 us
    pallas_call x1, Pallas kernels, power_parts(): pl.pallas_call(functools.partial(power_kernel, times, chips, total_waves)...  2.17 us
  transfers between devices with their start and end apart: 10, of which 4 were waited for; matrix products, arithmetic and copies ran while one was open for 5% of the time, Pallas kernels for 22%

profile of v5, /device:TPU:0, one launch (start us, length us, event | category | flops | bytes accessed | tf_op | source)
XLA Modules:
  0.0 76.5 jit_solution(15022674787401594391)
XLA Ops:
  0.6 0.0 copy-start
  0.6 4.5 %arrange.3 = (bf16[66,16,128]{2,1,0:T(8,128)(2,1)}, bf16[66,16,128]{2,1,0:T(8,128)(2,1)}, bf16[66,16,128]{2,1,0:T(8,128)(2,1)}, bf16[66,16,128]{2,1,0:T(8,128)(2,1)}) custom-call(bf16[64,32,512]{2,1,0:T(8,128)(2,1)} %bitcast.49, s32[1,32]{1,0:T(1,128)} %bitcast.43, f32[32,64]{1,0:T(8,128)} %basis_ref.1, bf16[32,1024,512]{2,1,0:T(8,128)(2,1)} %refs_10_.1), custom_call_target="tpu_custom_call" | custom-call | bytes 8388608 | tf_op jit(solution)/shard_map/arrange/pallas_call | solution.py:122
  5.2 4.1 %collective-permute-start.1 = (bf16[66,16,128]{2,1,0:T(8,128)(2,1)}, bf16[66,16,128]{2,1,0:T(8,128)(2,1)S(1)}, u32[]{:S(2)}, u32[]{:S(2)}) collective-permute-start(bf16[66,16,128]{2,1,0:T(8,128)(2,1)} %get-tuple-element.28), channel_id=1, source_target_pairs={{0,8},{1,9},{2,10},{3,11},{4,12},{5,13},{6,14},{7,15},{8,0},{9,1},... | collective-permute-start | bytes 811016 | tf_op jit(solution)/shard_map/ppermute | solution.py:408
  9.3 1.3 %collective-permute-start.4 = (bf16[66,16,128]{2,1,0:T(8,128)(2,1)}, bf16[66,16,128]{2,1,0:T(8,128)(2,1)S(1)}, u32[]{:S(2)}, u32[]{:S(2)}) collective-permute-start(bf16[66,16,128]{2,1,0:T(8,128)(2,1)} %get-tuple-element.30), channel_id=1, source_target_pairs={{0,10},{1,11},{2,8},{3,9},{4,14},{5,15},{6,12},{7,13},{8,2},{9,3},... | collective-permute-start | bytes 811016 | tf_op jit(solution)/shard_map/ppermute | solution.py:408
  10.6 1.6 %collective-permute-start.5 = (bf16[66,16,128]{2,1,0:T(8,128)(2,1)}, bf16[66,16,128]{2,1,0:T(8,128)(2,1)S(1)}, u32[]{:S(2)}, u32[]{:S(2)}) collective-permute-start(bf16[66,16,128]{2,1,0:T(8,128)(2,1)} %get-tuple-element.31), channel_id=1, source_target_pairs={{0,4},{1,5},{2,6},{3,7},{4,0},{5,1},{6,2},{7,3},{8,12},{9,13},{10,... | collective-permute-start | bytes 811016 | tf_op jit(solution)/shard_map/ppermute | solution.py:408
  12.1 0.0 copy-start.5
  12.2 0.2 collective-permute-start.6
  12.4 5.7 %arrange.2 = (bf16[32,256,512]{2,1,0:T(8,128)(2,1)S(1)}, bf16[34,16,128]{2,1,0:T(8,128)(2,1)}, bf16[66,16,128]{2,1,0:T(8,128)(2,1)}, bf16[66,16,128]{2,1,0:T(8,1...) custom-call(bf16[64,32,512]{2,1,0:T(8,128)(2,1)} %bitcast.50, s32[1,32]{1,0:T(1,128)} %bitcast.44, ...), custom_call_target="tpu_custom_call" | custom-call | bytes 8388608 | tf_op jit(solution)/shard_map/arrange/pallas_call | solution.py:122
  18.1 3.3 %copy-done.1 = bf16[32,256,512]{2,1,0:T(8,128)(2,1)} copy-done((bf16[32,256,512]{2,1,0:T(8,128)(2,1)}, bf16[32,256,512]{2,1,0:T(8,128)(2,1)S(1)}, u32[]{:S(2)}) %copy-start.1) | copy-done | bytes 8388632
  21.4 3.7 %collective-permute-start = (bf16[66,16,128]{2,1,0:T(8,128)(2,1)}, bf16[66,16,128]{2,1,0:T(8,128)(2,1)S(1)}, u32[]{:S(2)}, u32[]{:S(2)}) collective-permute-start(bf16[66,16,128]{2,1,0:T(8,128)(2,1)} %get-tuple-element.25), channel_id=1, source_target_pairs={{0,12},{1,13},{2,14},{3,15},{4,8},{5,9},{6,10},{7,11},{8,4},{9,5},... | collective-permute-start | bytes 811016 | tf_op jit(solution)/shard_map/ppermute | solution.py:408
  25.1 0.3 add_multiply_fusion.1
  25.4 1.1 %add_multiply_fusion = (f32[32,512]{1,0:T(8,128)S(1)}, f32[32,512]{1,0:T(8,128)S(1)}, f32[32,512]{1,0:T(8,128)S(1)}) fusion(f32[512]{0:T(512)S(1)} %copy-done.11, f32[512,512]{1,0:T(8,128)S(1)} %copy-done.2, f32[32,512]{1,0:T(8,128)S(1)} %get-tuple-element.49), kind=kOutput, calls=%fused_computation.17 | convolution fusion | flops 100876288 | bytes 1312768 | tf_op jit(solution)/shard_map/dot_general | solution.py:25
  26.5 0.2 convolution_add_fusion.3.coeffs_ref
  26.7 0.9 %slice.39 = bf16[32,16,128]{2,1,0:T(8,128)(2,1)S(1)} slice(bf16[34,16,128]{2,1,0:T(8,128)(2,1)} %get-tuple-element.26), slice={[0:32], [0:16], [0:128]} | slice | bytes 262144 | tf_op jit(solution)/shard_map/slice | solution.py:462
  27.6 0.7 slice.42
  28.3 0.1 collective-permute-done.1.refs_3_
  28.5 1.9 %collective-permute-start.7 = (bf16[66,16,128]{2,1,0:T(8,128)(2,1)}, bf16[66,16,128]{2,1,0:T(8,128)(2,1)S(1)}, u32[]{:S(2)}, u32[]{:S(2)}) collective-permute-start(bf16[66,16,128]{2,1,0:T(8,128)(2,1)} %get-tuple-element.34), channel_id=1, source_target_pairs={{0,2},{1,3},{2,0},{3,1},{4,6},{5,7},{6,4},{7,5},{8,10},{9,11},{10,... | collective-permute-start | bytes 811016 | tf_op jit(solution)/shard_map/ppermute | solution.py:408
  30.4 10.9 %collective-permute-done.4.refs_4_ = bf16[66,16,128]{2,1,0:T(8,128)(2,1)S(1)} collective-permute-done((bf16[66,16,128]{2,1,0:T(8,128)(2,1)}, bf16[66,16,128]{2,1,0:T(8,128)(2,1)S(1)}, u32[]{:S(2)}, u32[]{:S(2)}) %collective-permute-start.4) | collective-permute-done | bytes 270368 | tf_op jit(solution)/shard_map/ppermute | solution.py:408
  41.5 0.6 collective-permute-start.8
  42.1 0.1 convolution_add_fusion.2
  42.2 0.9 %collective-permute-done.2.refs_1_ = bf16[2,34,16,128]{3,2,1,0:T(8,128)(2,1)S(1)} collective-permute-done((bf16[2,34,16,128]{3,2,1,0:T(8,128)(2,1)}, bf16[2,34,16,128]{3,2,1,0:T(8,128)(2,1)S(1)}, u32[]{:S(2)}, u32[]{:S(2)}) %collective-permute-start.2) | collective-permute-done | bytes 278560 | tf_op jit(solution)/shard_map/ppermute | solution.py:408
  43.1 0.1 pad_maximum_fusion
  43.2 3.3 %collective-permute-start.3 = (bf16[68,16,128]{2,1,0:T(8,128)(2,1)S(1)}, bf16[68,16,128]{2,1,0:T(8,128)(2,1)S(1)}, u32[]{:S(2)}, u32[]{:S(2)}) collective-permute-start(bf16[68,16,128]{2,1,0:T(8,128)(2,1)S(1)} %pad_maximum_fusion), channel_id=1, source_target_pairs={{0,14},{1,15},{2,12},{3,13},{4,10},{5,11},{6,8},{7,9},{8,6},{9,7},... | collective-permute-start | bytes 835592 | tf_op jit(solution)/shard_map/ppermute | solution.py:408
  46.5 0.9 %copy-done.4 = bf16[34,16,128]{2,1,0:T(8,128)(2,1)S(1)} copy-done((bf16[34,16,128]{2,1,0:T(8,128)(2,1)S(1)}, bf16[34,16,128]{2,1,0:T(8,128)(2,1)}, u32[]{:S(2)}) %copy-start.4) | copy-done | bytes 139288
  47.4 11.1 %transfer.1 = (f32[32,32,512]{2,1,0:T(8,128)S(1)}, bf16[16,32,128]{2,1,0:T(8,128)(2,1)S(1)}) custom-call(s32[1]{0:T(128)} %bitcast.4.me_ref, bf16[5,34,16,128]{3,2,1,0:T(8,128)(2,1)S(1)} %collective-permute-done.8.refs_0_, bf16[2,34,16,128]{3,2,1,0:T(8,128)(2,1)S(1)} %collective-permute-done.2.refs_1_, bf16[34,16,128]{2,1,0:T(8,128)(2,1)S(1)} %copy-done.4, ...), custom_call_target="tpu_custom_call" | custom-call | flops 8589934592 | bytes 33554432 | tf_op jit(solution)/shard_map/transfer/pallas_call | solution.py:198
  58.5 0.3 collective-permute-start.9
  58.8 0.1 fusion.9.refs_9_
  58.9 0.0 collective-permute-done.3.refs_1_
  58.9 1.0 %collective-permute-done.9.refs_2_ = bf16[1,34,16,128]{3,2,1,0:T(8,128)(2,1)S(1)} collective-permute-done((bf16[1,34,16,128]{3,2,1,0:T(8,128)(2,1)S(1)}, bf16[1,34,16,128]{3,2,1,0:T(8,128)(2,1)S(1)}, u32[]{:S(2)}, u32[]{:S(2)}) %collective-permute-start.9) | collective-permute-done | bytes 139296 | tf_op jit(solution)/shard_map/ppermute | solution.py:408
  60.0 2.2 %power.1 = f32[16,24,128]{2,1,0:T(8,128)S(1)} custom-call(bf16[66,16,128]{2,1,0:T(8,128)(2,1)S(1)} %collective-permute-done.refs_0_, bf16[68,16,128]{2,1,0:T(8,128)(2,1)S(1)} %collective-permute-done.3.refs_1_, bf16[1,34,16,128]{3,2,1,0:T(8,128)(2,1)S(1)} %collective-permute-done.9.refs_2_, bf16[32,256,512]{2,1,0:T(8,128)(2,1)S(1)} %bitcast.42, ...), custom_call_target="tpu_custom_call" | custom-call | flops 2147483648 | bytes 8388608 | tf_op jit(solution)/shard_map/power/pallas_call | solution.py:285
  62.2 12.0 %all_to_all.5.parts_ref = f32[16,24,128]{2,1,0:T(8,128)S(1)} all-to-all(f32[16,24,128]{2,1,0:T(8,128)S(1)} %power.1), channel_id=1, replica_groups=mesh['grp'=2,'ka'=16] {'ka'}, dimensions={0} | all-to-all | bytes 393216 | tf_op jit(solution)/shard_map/all_to_all | solution.py:490
  74.1 2.4 %gradients.1 = (f32[32,32]{1,0:T(8,128)}, f32[32,64]{1,0:T(8,128)}, f32[6,512]{1,0:T(8,128)}, f32[512,512]{1,0:T(8,128)}, f32[64,512]{1,0:T(8,128)}) custom-call(f32[16,24,128]{2,1,0:T(8,128)S(1)} %all_to_all.5.parts_ref, f32[6,32]{1,0:T(8,128)S(1)} %copy-done.6, f32[32,64]{1,0:T(8,128)S(1)} %convolution_add_fusion.3.coeffs_ref, ...), custom_call_target="tpu_custom_call" | custom-call | tf_op jit(solution)/shard_map/gradients/pallas_call | solution.py:395
  (43 shorter events, 0.2 us)
Async XLA Ops:
  0.6 24.4 %copy-start = (f32[512,6]{0,1:T(8,128)S(1)}, f32[512,6]{0,1:T(8,128)}, u32[]{:S(2)}) copy-start(f32[512,6]{0,1:T(8,128)} %param.20) | copy-start | bytes 36868
  5.2 23.3 %collective-permute-start.1 = (bf16[66,16,128]{2,1,0:T(8,128)(2,1)}, bf16[66,16,128]{2,1,0:T(8,128)(2,1)S(1)}, u32[]{:S(2)}, u32[]{:S(2)}) collective-permute-start(bf16[66,16,128]{2,1,0:T(8,128)(2,1)} %get-tuple-element.28), channel_id=1, source_target_pairs={{0,8},{1,9},{2,10},{3,11},{4,12},{5,13},{6,14},{7,15},{8,0},{9,1},... | collective-permute-start | bytes 811016 | tf_op jit(solution)/shard_map/ppermute | solution.py:408
  9.3 32.1 %collective-permute-start.4 = (bf16[66,16,128]{2,1,0:T(8,128)(2,1)}, bf16[66,16,128]{2,1,0:T(8,128)(2,1)S(1)}, u32[]{:S(2)}, u32[]{:S(2)}) collective-permute-start(bf16[66,16,128]{2,1,0:T(8,128)(2,1)} %get-tuple-element.30), channel_id=1, source_target_pairs={{0,10},{1,11},{2,8},{3,9},{4,14},{5,15},{6,12},{7,13},{8,2},{9,3},... | collective-permute-start | bytes 811016 | tf_op jit(solution)/shard_map/ppermute | solution.py:408
  10.6 30.8 %collective-permute-start.5 = (bf16[66,16,128]{2,1,0:T(8,128)(2,1)}, bf16[66,16,128]{2,1,0:T(8,128)(2,1)S(1)}, u32[]{:S(2)}, u32[]{:S(2)}) collective-permute-start(bf16[66,16,128]{2,1,0:T(8,128)(2,1)} %get-tuple-element.31), channel_id=1, source_target_pairs={{0,4},{1,5},{2,6},{3,7},{4,0},{5,1},{6,2},{7,3},{8,12},{9,13},{10,... | collective-permute-start | bytes 811016 | tf_op jit(solution)/shard_map/ppermute | solution.py:408
  12.1 12.9 %copy-start.6 = (f32[6,32]{1,0:T(8,128)S(1)}, f32[6,32]{1,0:T(8,128)}, u32[]{:S(2)}) copy-start(f32[6,32]{1,0:T(8,128)} %params_ref.1) | copy-start | bytes 2308
  12.1 12.9 %copy-start.12 = (f32[512]{0:T(512)S(1)}, f32[512]{0:T(512)}, u32[]{:S(2)}) copy-start(f32[512]{0:T(512)} %param.21) | copy-start | bytes 6148
  12.1 13.2 %copy-start.2 = (f32[512,512]{1,0:T(8,128)S(1)}, f32[512,512]{1,0:T(8,128)}, u32[]{:S(2)}) copy-start(f32[512,512]{1,0:T(8,128)} %weight_mid_ref.1) | copy-start | bytes 3145732
  12.1 13.2 %copy-start.11 = (f32[512]{0:T(512)S(1)}, f32[512]{0:T(512)}, u32[]{:S(2)}) copy-start(f32[512]{0:T(512)} %param.23) | copy-start | bytes 6148
  12.1 14.3 %copy-start.5 = (f32[64,512]{1,0:T(8,128)S(1)}, f32[64,512]{1,0:T(8,128)}, u32[]{:S(2)}) copy-start(f32[64,512]{1,0:T(8,128)} %weight_out_ref.1) | copy-start | bytes 393220
  12.2 14.3 %copy-start.13 = (f32[64]{0:T(128)S(1)}, f32[64]{0:T(128)}, u32[]{:S(2)}) copy-start(f32[64]{0:T(128)} %param.25) | copy-start | bytes 772
  12.2 29.9 %copy-start.3 = (f32[32,64]{1,0:T(8,128)S(1)}, f32[32,64]{1,0:T(8,128)}, u32[]{:S(2)}) copy-start(f32[32,64]{1,0:T(8,128)} %basis_ref.1) | copy-start | bytes 24580
  12.2 29.9 %copy-start.8 = (f32[32]{0:T(128)S(1)}, f32[32]{0:T(128)}, u32[]{:S(2)}) copy-start(f32[32]{0:T(128)} %param.27) | copy-start | bytes 388
  12.2 29.2 %collective-permute-start.6 = (bf16[66,16,128]{2,1,0:T(8,128)(2,1)}, bf16[66,16,128]{2,1,0:T(8,128)(2,1)S(1)}, u32[]{:S(2)}, u32[]{:S(2)}) collective-permute-start(bf16[66,16,128]{2,1,0:T(8,128)(2,1)} %get-tuple-element.32), channel_id=1, source_target_pairs={{0,6},{1,7},{2,4},{3,5},{4,2},{5,3},{6,0},{7,1},{8,14},{9,15},{10,... | collective-permute-start | bytes 811016 | tf_op jit(solution)/shard_map/ppermute | solution.py:408
  18.1 3.3 %copy-start.1 = (bf16[32,256,512]{2,1,0:T(8,128)(2,1)}, bf16[32,256,512]{2,1,0:T(8,128)(2,1)S(1)}, u32[]{:S(2)}) copy-start(bf16[32,256,512]{2,1,0:T(8,128)(2,1)S(1)} %get-tuple-element.38.refs_3_) | copy-start | bytes 25165828
  21.4 37.1 %collective-permute-start = (bf16[66,16,128]{2,1,0:T(8,128)(2,1)}, bf16[66,16,128]{2,1,0:T(8,128)(2,1)S(1)}, u32[]{:S(2)}, u32[]{:S(2)}) collective-permute-start(bf16[66,16,128]{2,1,0:T(8,128)(2,1)} %get-tuple-element.25), channel_id=1, source_target_pairs={{0,12},{1,13},{2,14},{3,15},{4,8},{5,9},{6,10},{7,11},{8,4},{9,5},... | collective-permute-start | bytes 811016 | tf_op jit(solution)/shard_map/ppermute | solution.py:408
  28.5 13.0 %collective-permute-start.7 = (bf16[66,16,128]{2,1,0:T(8,128)(2,1)}, bf16[66,16,128]{2,1,0:T(8,128)(2,1)S(1)}, u32[]{:S(2)}, u32[]{:S(2)}) collective-permute-start(bf16[66,16,128]{2,1,0:T(8,128)(2,1)} %get-tuple-element.34), channel_id=1, source_target_pairs={{0,2},{1,3},{2,0},{3,1},{4,6},{5,7},{6,4},{7,5},{8,10},{9,11},{10,... | collective-permute-start | bytes 811016 | tf_op jit(solution)/shard_map/ppermute | solution.py:408
  41.3 1.8 %collective-permute-start.2 = (bf16[2,34,16,128]{3,2,1,0:T(8,128)(2,1)}, bf16[2,34,16,128]{3,2,1,0:T(8,128)(2,1)S(1)}, u32[]{:S(2)}, u32[]{:S(2)}) collective-permute-start(bf16[2,34,16,128]{3,2,1,0:T(8,128)(2,1)} %get-tuple-element.29), channel_id=1, source_target_pairs={{0,1},{1,0},{2,3},{3,2},{4,5},{5,4},{6,7},{7,6},{8,9},{9,8},{10,11... | collective-permute-start | bytes 835592 | tf_op jit(solution)/shard_map/ppermute | solution.py:408
  41.5 18.5 %slice-start = ((s8[8388608]{0:T(1024)(128)(4,1)}), s8[4194304]{0:T(1024)(128)(4,1)S(1)}, s32[]{:S(2)}) async-start(s8[8388608]{0:T(1024)(128)(4,1)} %bitcast.41), calls=%async_computation.1 | async-start | bytes 8388608
  41.5 5.0 %collective-permute-start.8 = (bf16[5,34,16,128]{3,2,1,0:T(8,128)(2,1)S(1)}, bf16[5,34,16,128]{3,2,1,0:T(8,128)(2,1)S(1)}, u32[]{:S(2)}, u32[]{:S(2)}) collective-permute-start(bf16[5,34,16,128]{3,2,1,0:T(8,128)(2,1)S(1)} %fusion), channel_id=1, source_target_pairs={{0,1},{1,0},{2,3},{3,2},{4,5},{5,4},{6,7},{7,6},{8,9},{9,8},{10,11... | collective-permute-start | bytes 2088968 | tf_op jit(solution)/shard_map/ppermute | solution.py:408
  43.2 15.7 %collective-permute-start.3 = (bf16[68,16,128]{2,1,0:T(8,128)(2,1)S(1)}, bf16[68,16,128]{2,1,0:T(8,128)(2,1)S(1)}, u32[]{:S(2)}, u32[]{:S(2)}) collective-permute-start(bf16[68,16,128]{2,1,0:T(8,128)(2,1)S(1)} %pad_maximum_fusion), channel_id=1, source_target_pairs={{0,14},{1,15},{2,12},{3,13},{4,10},{5,11},{6,8},{7,9},{8,6},{9,7},... | collective-permute-start | bytes 835592 | tf_op jit(solution)/shard_map/ppermute | solution.py:408
  46.5 0.9 %copy-start.4 = (bf16[34,16,128]{2,1,0:T(8,128)(2,1)S(1)}, bf16[34,16,128]{2,1,0:T(8,128)(2,1)}, u32[]{:S(2)}) copy-start(bf16[34,16,128]{2,1,0:T(8,128)(2,1)} %get-tuple-element.35.refs_2_) | copy-start | bytes 417796
  47.4 12.5 %slice-start.1 = ((s8[8388608]{0:T(1024)(128)(4,1)}), s8[4194304]{0:T(1024)(128)(4,1)S(1)}, s32[]{:S(2)}) async-start(s8[8388608]{0:T(1024)(128)(4,1)} %bitcast.41), calls=%async_computation.2 | async-start | bytes 8388608
  47.4 12.5 %copy-start.9 = (s32[32]{0:T(128)S(1)}, s32[32]{0:T(128)}, u32[]{:S(2)}) copy-start(s32[32]{0:T(128)} %param.17) | copy-start | bytes 388
  47.4 12.5 %copy-start.10 = (s32[32]{0:T(128)S(1)}, s32[32]{0:T(128)}, u32[]{:S(2)}) copy-start(s32[32]{0:T(128)} %param.18) | copy-start | bytes 388
  58.5 15.6 %copy-start.7 = (s32[32]{0:T(128)S(1)}, s32[32]{0:T(128)}, u32[]{:S(2)}) copy-start(s32[32]{0:T(128)} %param.16) | copy-start | bytes 388
  58.5 1.4 %collective-permute-start.9 = (bf16[1,34,16,128]{3,2,1,0:T(8,128)(2,1)S(1)}, bf16[1,34,16,128]{3,2,1,0:T(8,128)(2,1)S(1)}, u32[]{:S(2)}, u32[]{:S(2)}) collective-permute-start(bf16[1,34,16,128]{3,2,1,0:T(8,128)(2,1)S(1)} %slice_bitcast_fusion.5), channel_id=1, source_target_pairs={{0,1},{1,0},{2,3},{3,2},{4,5},{5,4},{6,7},{7,6},{8,9},{9,8},{10,11... | collective-permute-start | bytes 417800 | tf_op jit(solution)/shard_map/ppermute | solution.py:408

commit v6 on v5

--- a/solution.py
+++ b/solution.py
@@ -98,10 +98,12 @@
             if chip in (0, last):
                 out_ref = out_refs[-1].at[int(chip == last)] if core else out_ref
                 out_ref[:waves] = piece
-                out_ref[waves:] = extra
+                if core or chip == 0:
+                    out_ref[waves:] = extra
             else:
                 out_ref[core * waves : (core + 1) * waves] = piece
-                out_ref[2 * waves :] = extra
+                if tops[slot] != TOPS[-1]:
+                    out_ref[2 * waves :] = extra
     for copy in holds:
         copy.wait()
 
@@ -114,7 +116,9 @@
     extras = -(-basis.shape[0] // low_count)
     one, two = (count * waves + extras for count in (1, 2))
     chips = [top * group // 2 + low for top in tops for low in range(group // 2)]
-    shapes = [(one if chip in (0, last) else two, low_count, LANES) for chip in chips]
+    late = range(TOPS[-1] * group // 2, TOPS[-1] * group // 2 + group // 2)
+    tiles = [(one if chip in (0, last) else two) - (extras if chip in late else 0) for chip in chips]
+    shapes = [(count, low_count, LANES) for count in tiles]
     if last in chips:
         shapes.append((2, one, low_count, LANES))
     held = pltpu.VMEM((waves, group * times, multipole_count), bessel.dtype)
@@ -151,7 +155,8 @@
 
 def transfer_kernel(group, members, times, me_ref, *refs):
     count = 1 + max(member[1] for member in members)
-    arrays, (*bessel_refs, out_ref, basis_ref, stage_ref) = refs[:count], refs[count:]
+    arrays, refs = refs[:count], refs[count:]
+    own_ref, own_extra_ref, *bessel_refs, out_ref, basis_ref, stage_ref = refs
     me = me_ref[0]
     step = pl.program_id(0)
     waves = out_ref.shape[0]
@@ -163,12 +168,13 @@
     @pl.when(step == 0)
     def _():
         for apart, array, lead, _, at in members:
-            extra = tiles(array, lead, pl.ds(at, extras))
+            extra = tiles(array, lead, pl.ds(at, extras)) if apart else own_extra_ref[...]
             basis_ref[apart] = extra.reshape(basis_ref.shape[1:])
 
-    for number, (_, array, lead, at, _) in enumerate(members):
+    for number, (apart, array, lead, at, _) in enumerate(members):
         place = (number % group) ^ (me % group)
-        stage_ref[number // group, place] = tiles(array, lead, pl.ds(at + step * waves, waves))
+        rows = pl.ds(at + step * waves, waves)
+        stage_ref[number // group, place] = tiles(array, lead, rows) if apart else own_ref[...]
     for wave in range(waves):
         total = None
         for number, bessel_ref in enumerate(bessel_refs):
@@ -181,13 +187,17 @@
         out_ref[wave] = total
 
 
-def add_groups(me, group, arrays, members, bessel, times, extras):
+def add_groups(me, group, arrays, members, own, bessel, times, extras):
     low_count = arrays[0].shape[-2]
     waves, _, multipoles = bessel.shape
     span = group * times
     cosmos = low_count * (LANES // times)
     block = math.gcd(waves, 8)
     in_specs = [pl.BlockSpec(memory_space=pltpu.VMEM)] * len(arrays)
+    in_specs += [
+        pl.BlockSpec((block, low_count, LANES), lambda s, me: (s, 0, 0)),
+        pl.BlockSpec((extras, low_count, LANES), lambda s, me: (waves // extras, 0, 0)),
+    ]
     in_specs += [
         pl.BlockSpec(
             (block, span, multipoles), lambda s, me, top=top: (s, (me[0] // group) ^ top, 0)
@@ -220,30 +230,28 @@
             transcendentals=0,
         ),
         name="transfer",
-    )(me, *arrays, *[bessel] * (len(TOPS) - 1))
+    )(me, *arrays, own, own, *[bessel] * (len(TOPS) - 1))
 
 
 def power_kernel(times, chips, total_waves, *refs):
-    piece_refs, traded_ref, held_ref, rest_ref, *refs = refs[: len(chips)], *refs[len(chips) :]
-    params_ref, low_ref, high_ref, basis_ref, base_ref, out_ref, stage_ref, all_ref = refs
+    piece_refs, traded_ref, extra_ref, held_ref, *refs = refs[: len(chips)], *refs[len(chips) :]
+    rest_ref, params_ref, low_ref, high_ref, basis_ref, base_ref, out_ref, stage_ref, all_ref = refs
     waves, cosmos, multipoles = rest_ref.shape
     comps = base_ref.shape[1]
     peers = all_ref.shape[0]
     owned = multipoles // peers
     group = 2 * len(chips)
-    extras = traded_ref.shape[1] - waves
     me = lax.axis_index("ka")
     all_ref[...] = basis_ref[...]
     for low, (chip, piece_ref) in enumerate(zip(chips, piece_refs)):
         joined = low == len(chips) - 1
         for core in range(2):
             if core and not joined:
-                piece, extra = traded_ref[low, :waves], traded_ref[low, waves:]
+                piece = traded_ref[low]
             else:
-                start = 2 * waves + core * extras
-                piece, extra = piece_ref[core * waves : (core + 1) * waves], piece_ref[start : start + extras]
+                piece = piece_ref[core * waves : (core + 1) * waves]
             stage_ref[(2 * low + core) ^ (me % group)] = piece
-            all_ref[2 * chip + core] = extra.reshape(all_ref.shape[1:])
+            all_ref[2 * chip + core] = extra_ref[2 * low + core].reshape(all_ref.shape[1:])
     first_param, second_param = column(params_ref[0:1]), column(params_ref[1:2])
     low, high = column(low_ref[...]), column(high_ref[...])
     total = jnp.zeros((cosmos, multipoles), jnp.float32)
@@ -275,12 +283,12 @@
         out_ref[peer] = fold(jnp.concatenate([own, part], axis=1))
 
 
-def power_parts(pieces, traded, held, rest, times, chips, total_waves, extra):
+def power_parts(pieces, traded, extras, held, rest, times, chips, total_waves, extra):
     low_count = traded.shape[2]
     waves, cosmos, multipoles = rest.shape
     basis, base = extra[-2:]
     peers = basis.shape[0]
-    operands = [*pieces, traded, held, rest, *extra]
+    operands = [*pieces, traded, extras, held, rest, *extra]
     rows = folded_rows(cosmos, multipoles // peers + base.shape[1])
     return pl.pallas_call(
         functools.partial(power_kernel, times, chips, total_waves),
@@ -454,26 +462,26 @@
         if chip in (0, last):
             continue
         value = ready[chip]
-        if chip in near:
-            value = after(value, got[TOPS[0] * half])
         got[chip] = exchange(value, 2 * chip, peers)
-    given = exchange(after(give, got[TOPS[0] * half]), 1, peers)
+    given = exchange(give, 1, peers)
     mine, other = ready[last], given[1]
-    value = jnp.concatenate([mine[:waves], other[:waves], mine[waves:], other[waves:]])
+    value = jnp.concatenate([mine, other[:waves]])
     got[last] = exchange(value, 2 * last, peers)
 
     others = lambda part, *then: jnp.stack([after(got[chip], *then)[waves:] for chip in part])
     early = [chip for chip in chips[:-half] if chip]
     traded = exchange(others(early), 1, peers)
-    arrays = [traded, given, ready[0]] + [got[chip] for chip in early]
+    extra = [part for chip in chips[:half] for part in (got[chip][2 * waves :], traded[early.index(chip), waves:])]
+    forwarded = exchange(jnp.stack(extra), TOPS[1] * group, peers)
+    arrays = [traded, given] + [got[chip] for chip in early]
     members = []
     for chip in chips[:-half]:
         if chip:
             at = early.index(chip)
-            members += [(2 * chip, 3 + at, None, 0, 2 * waves), (2 * chip + 1, 0, at, 0, waves)]
+            members += [(2 * chip, 2 + at, None, 0, 2 * waves), (2 * chip + 1, 0, at, 0, waves)]
         else:
-            members += [(0, 2, None, 0, waves), (1, 1, 0, 0, waves)]
-    rest, basis = add_groups(me, group, arrays, members, bessel, times, extras)
+            members += [(0, 0, None, 0, waves), (1, 1, 0, 0, waves)]
+    rest, basis = add_groups(me, group, arrays, members, ready[0], bessel, times, extras)
     late_traded = exchange(others(late[:-1], rest), 1, peers)
 
     inner_pre = mat(params.T, weight_in.T) + bias_in[None, :]
@@ -486,7 +494,7 @@
 
     extra = (params, window_low.reshape(1, cosmos), window_high.reshape(1, cosmos), basis, base)
     pieces = [got[chip] for chip in late]
-    parts = power_parts(pieces, late_traded, held[TOPS[-1]], rest, times, late, total_waves, extra)
+    parts = power_parts(pieces, late_traded, forwarded, held[TOPS[-1]], rest, times, late, total_waves, extra)
     gathered = lax.all_to_all(parts, "ka", split_axis=0, concat_axis=0, tiled=True)
     spectra, grad_basis, grad_in, grad_mid, grad_out = gradients(
         gathered, params, coeffs, hidden, weight_mid, weight_out, pca_basis, offset, own_multipoles

time: 76.9 us -> 75.7 us (0.984)
  local copies, waits for them, and re-layouts: 5.97 us -> 4.36 us
  other arithmetic: 0.05 us -> 1.09 us
  starting transfers between devices: 16.9 us -> 16 us
    slice x4 -> x2, local copies, waits for them, and re-layouts: 1.62 us -> 0.01 us  [the longest x1 0.01 us: local(): value = jnp.concatenate([mine, other[:waves]])]
    concatenate x1, other arithmetic: 0.05 us -> 1.08 us  [local(): value = jnp.concatenate([mine, other[:waves]])]
    ppermute x10 -> x11, starting transfers between devices: 16.9 us -> 16 us  [exchange(): lax.ppermute(value, 'ka', [(peer, peer ^ apart) for peer in range(peers)])]
    ppermute x10 -> x11, waiting for transfers between devices: 13 us -> 13.4 us  [exchange(): lax.ppermute(value, 'ka', [(peer, peer ^ apart) for peer in range(peers)])]
  transfers between devices with their start and end apart: 10 -> 11, of which waited for: 4 -> 3; matrix products, arithmetic and copies ran while one was open for 5% -> 4% of each run, Pallas kernels for 22% -> 22%
where the time goes in v6:
time: 75.7 us; the launch traced here: 75.3 us
  Pallas kernels  25.8 us (34%)
  starting transfers between devices  16 us (21%)
  waiting for transfers between devices  13.4 us (18%)
  blocking collectives  11.9 us (16%)
  local copies, waits for them, and re-layouts  4.36 us (6%)
  matrix products  1.87 us (2%)
  other arithmetic  1.09 us (1%)
  between operations  0.96 us (1%)
    ppermute x11, starting transfers between devices, exchange(): lax.ppermute(value, 'ka', [(peer, peer ^ apart) for peer in range(peers)])  16 us
    ppermute x11, waiting for transfers between devices, exchange(): lax.ppermute(value, 'ka', [(peer, peer ^ apart) for peer in range(peers)])  13.4 us
    all_to_all x1, blocking collectives, local(): lax.all_to_all(parts, 'ka', split_axis=0, concat_axis=0, tiled=True)  11.9 us
    pallas_call x1, Pallas kernels, add_groups(): pl.pallas_call(functools.partial(transfer_kernel, group, members, times),...  11.1 us
    pallas_call x2, Pallas kernels, arrange(): pl.pallas_call(functools.partial(arrange_kernel, tops, group, last, waves...  10.2 us
    unnamed x36, local copies, waits for them, and re-layouts  4.31 us
    pallas_call x1, Pallas kernels, gradients(): pl.pallas_call(gradients_kernel, in_specs=[pl.BlockSpec(memory_space=pltp...  2.36 us
    pallas_call x1, Pallas kernels, power_parts(): pl.pallas_call(functools.partial(power_kernel, times, chips, total_waves)...  2.17 us
  transfers between devices with their start and end apart: 11, of which 3 were waited for; matrix products, arithmetic and copies ran while one was open for 4% of the time, Pallas kernels for 22%

profile of v6, /device:TPU:0, one launch (start us, length us, event | category | flops | bytes accessed | tf_op | source)
XLA Modules:
  0.0 75.3 jit_solution(1723382100049773894)
XLA Ops:
  0.6 0.0 copy-start
  0.6 4.5 %arrange.3 = (bf16[66,16,128]{2,1,0:T(8,128)(2,1)}, bf16[66,16,128]{2,1,0:T(8,128)(2,1)}, bf16[66,16,128]{2,1,0:T(8,128)(2,1)}, bf16[66,16,128]{2,1,0:T(8,128)(2,1)}) custom-call(bf16[64,32,512]{2,1,0:T(8,128)(2,1)} %bitcast.51, s32[1,32]{1,0:T(1,128)} %bitcast.45, f32[32,64]{1,0:T(8,128)} %basis_ref.1, bf16[32,1024,512]{2,1,0:T(8,128)(2,1)} %refs_11_.1), custom_call_target="tpu_custom_call" | custom-call | bytes 8388608 | tf_op jit(solution)/shard_map/arrange/pallas_call | solution.py:126
  5.2 4.1 %collective-permute-start.3 = (bf16[66,16,128]{2,1,0:T(8,128)(2,1)}, bf16[66,16,128]{2,1,0:T(8,128)(2,1)S(1)}, u32[]{:S(2)}, u32[]{:S(2)}) collective-permute-start(bf16[66,16,128]{2,1,0:T(8,128)(2,1)} %get-tuple-element.26), channel_id=1, source_target_pairs={{0,8},{1,9},{2,10},{3,11},{4,12},{5,13},{6,14},{7,15},{8,0},{9,1},... | collective-permute-start | bytes 811016 | tf_op jit(solution)/shard_map/ppermute | solution.py:416
  9.3 1.3 %collective-permute-start.4 = (bf16[66,16,128]{2,1,0:T(8,128)(2,1)}, bf16[66,16,128]{2,1,0:T(8,128)(2,1)S(1)}, u32[]{:S(2)}, u32[]{:S(2)}) collective-permute-start(bf16[66,16,128]{2,1,0:T(8,128)(2,1)} %get-tuple-element.27), channel_id=1, source_target_pairs={{0,10},{1,11},{2,8},{3,9},{4,14},{5,15},{6,12},{7,13},{8,2},{9,3},... | collective-permute-start | bytes 811016 | tf_op jit(solution)/shard_map/ppermute | solution.py:416
  10.6 1.6 %collective-permute-start.5 = (bf16[66,16,128]{2,1,0:T(8,128)(2,1)}, bf16[66,16,128]{2,1,0:T(8,128)(2,1)S(1)}, u32[]{:S(2)}, u32[]{:S(2)}) collective-permute-start(bf16[66,16,128]{2,1,0:T(8,128)(2,1)} %get-tuple-element.28), channel_id=1, source_target_pairs={{0,4},{1,5},{2,6},{3,7},{4,0},{5,1},{6,2},{7,3},{8,12},{9,13},{10,... | collective-permute-start | bytes 811016 | tf_op jit(solution)/shard_map/ppermute | solution.py:416
  12.2 0.0 copy-start.5
  12.2 0.0 copy-start.13
  12.2 0.0 copy-start.8
  12.2 0.2 collective-permute-start.6
  12.4 5.7 %arrange.2 = (bf16[32,256,512]{2,1,0:T(8,128)(2,1)S(1)}, bf16[34,16,128]{2,1,0:T(8,128)(2,1)}, bf16[66,16,128]{2,1,0:T(8,128)(2,1)}, bf16[64,16,128]{2,1,0:T(8,1...) custom-call(bf16[64,32,512]{2,1,0:T(8,128)(2,1)} %bitcast.52, s32[1,32]{1,0:T(1,128)} %bitcast.46, ...), custom_call_target="tpu_custom_call" | custom-call | bytes 8388608 | tf_op jit(solution)/shard_map/arrange/pallas_call | solution.py:126
  18.1 3.3 %copy-done.1 = bf16[32,256,512]{2,1,0:T(8,128)(2,1)} copy-done((bf16[32,256,512]{2,1,0:T(8,128)(2,1)}, bf16[32,256,512]{2,1,0:T(8,128)(2,1)S(1)}, u32[]{:S(2)}) %copy-start.1) | copy-done | bytes 8388632
  21.4 1.6 %collective-permute-start.7 = (bf16[66,16,128]{2,1,0:T(8,128)(2,1)}, bf16[66,16,128]{2,1,0:T(8,128)(2,1)S(1)}, u32[]{:S(2)}, u32[]{:S(2)}) collective-permute-start(bf16[66,16,128]{2,1,0:T(8,128)(2,1)} %get-tuple-element.30), channel_id=1, source_target_pairs={{0,2},{1,3},{2,0},{3,1},{4,6},{5,7},{6,4},{7,5},{8,10},{9,11},{10,... | collective-permute-start | bytes 811016 | tf_op jit(solution)/shard_map/ppermute | solution.py:416
  23.0 0.3 add_multiply_fusion.1
  23.3 1.1 %add_multiply_fusion = (f32[32,512]{1,0:T(8,128)S(1)}, f32[32,512]{1,0:T(8,128)S(1)}, f32[32,512]{1,0:T(8,128)S(1)}) fusion(f32[512]{0:T(512)S(1)} %copy-done.11, f32[512,512]{1,0:T(8,128)S(1)} %copy-done.2, f32[32,512]{1,0:T(8,128)S(1)} %get-tuple-element.47), kind=kOutput, calls=%fused_computation.17 | convolution fusion | flops 100876288 | bytes 1312768 | tf_op jit(solution)/shard_map/dot_general | solution.py:25
  24.4 0.2 convolution_add_fusion.3.coeffs_ref
  24.6 0.1 convolution_add_fusion.2
  24.8 3.7 %collective-permute-done.3.refs_2_ = bf16[66,16,128]{2,1,0:T(8,128)(2,1)S(1)} collective-permute-done((bf16[66,16,128]{2,1,0:T(8,128)(2,1)}, bf16[66,16,128]{2,1,0:T(8,128)(2,1)S(1)}, u32[]{:S(2)}, u32[]{:S(2)}) %collective-permute-start.3) | collective-permute-done | bytes 270368 | tf_op jit(solution)/shard_map/ppermute | solution.py:416
  28.5 6.0 %collective-permute-done.4.refs_3_ = bf16[66,16,128]{2,1,0:T(8,128)(2,1)S(1)} collective-permute-done((bf16[66,16,128]{2,1,0:T(8,128)(2,1)}, bf16[66,16,128]{2,1,0:T(8,128)(2,1)S(1)}, u32[]{:S(2)}, u32[]{:S(2)}) %collective-permute-start.4) | collective-permute-done | bytes 270368 | tf_op jit(solution)/shard_map/ppermute | solution.py:416
  34.6 3.5 %collective-permute-start = (bf16[64,16,128]{2,1,0:T(8,128)(2,1)}, bf16[64,16,128]{2,1,0:T(8,128)(2,1)S(1)}, u32[]{:S(2)}, u32[]{:S(2)}) collective-permute-start(bf16[64,16,128]{2,1,0:T(8,128)(2,1)} %get-tuple-element.23), channel_id=1, source_target_pairs={{0,12},{1,13},{2,14},{3,15},{4,8},{5,9},{6,10},{7,11},{8,4},{9,5},... | collective-permute-start | bytes 786440 | tf_op jit(solution)/shard_map/ppermute | solution.py:416
  38.2 0.1 collective-permute-start.8
  38.3 1.1 %pad_maximum_fusion = bf16[64,16,128]{2,1,0:T(8,128)(2,1)S(1)} fusion(bf16[32,16,128]{2,1,0:T(8,128)(2,1)S(1)} %slice_bitcast_fusion.5, bf16[32,16,128]{2,1,0:T(8,128)(2,1)} %get-tuple-element.24), kind=kLoop, calls=%fused_computation.4 | loop fusion | flops 131072 | bytes 524288 | tf_op jit(solution)/shard_map/concatenate | solution.py:468
  39.4 3.3 %collective-permute-start.2 = (bf16[64,16,128]{2,1,0:T(8,128)(2,1)S(1)}, bf16[64,16,128]{2,1,0:T(8,128)(2,1)S(1)}, u32[]{:S(2)}, u32[]{:S(2)}) collective-permute-start(bf16[64,16,128]{2,1,0:T(8,128)(2,1)S(1)} %pad_maximum_fusion), channel_id=1, source_target_pairs={{0,14},{1,15},{2,12},{3,13},{4,10},{5,11},{6,8},{7,9},{8,6},{9,7},... | collective-permute-start | bytes 786440 | tf_op jit(solution)/shard_map/ppermute | solution.py:416
  42.8 0.9 %copy-done.3 = bf16[34,16,128]{2,1,0:T(8,128)(2,1)S(1)} copy-done((bf16[34,16,128]{2,1,0:T(8,128)(2,1)S(1)}, bf16[34,16,128]{2,1,0:T(8,128)(2,1)}, u32[]{:S(2)}) %copy-start.3) | copy-done | bytes 139288
  43.7 11.1 %transfer.1 = (f32[32,32,512]{2,1,0:T(8,128)S(1)}, bf16[16,32,128]{2,1,0:T(8,128)(2,1)S(1)}) custom-call(s32[1]{0:T(128)} %bitcast.3.me_ref, bf16[5,34,16,128]{3,2,1,0:T(8,128)(2,1)S(1)} %collective-permute-done.8.refs_0_, bf16[2,34,16,128]{3,2,1,0:T(8,128)(2,1)S(1)} %collective-permute-done.1.refs_1_, ...), custom_call_target="tpu_custom_call" | custom-call | flops 8589934592 | bytes 33554432 | tf_op jit(solution)/shard_map/transfer/pallas_call | solution.py:208
  54.8 0.1 collective-permute-start.9
  54.9 0.2 collective-permute-start.10
  55.1 0.1 fusion.10.refs_10_
  55.2 0.0 collective-permute-done.2.refs_1_
  55.2 3.6 %collective-permute-done.10.refs_3_ = bf16[4,2,16,128]{3,2,1,0:T(8,128)(2,1)S(1)} collective-permute-done((bf16[4,2,16,128]{3,2,1,0:T(8,128)(2,1)S(1)}, bf16[4,2,16,128]{3,2,1,0:T(8,128)(2,1)S(1)}, u32[]{:S(2)}, u32[]{:S(2)}) %collective-permute-start.10) | collective-permute-done | bytes 32800 | tf_op jit(solution)/shard_map/ppermute | solution.py:416
  58.9 2.2 %power.1 = f32[16,24,128]{2,1,0:T(8,128)S(1)} custom-call(bf16[64,16,128]{2,1,0:T(8,128)(2,1)S(1)} %collective-permute-done.refs_0_, bf16[64,16,128]{2,1,0:T(8,128)(2,1)S(1)} %collective-permute-done.2.refs_1_, bf16[1,32,16,128]{3,2,1,0:T(8,128)(2,1)S(1)} %collective-permute-done.9.refs_2_, bf16[4,2,16,128]{3,2,1,0:T(8,128)(2,1)S(1)} %collective-permute-done.10.refs_3_, ...), custom_call_target="tpu_custom_call" | custom-call | flops 2147483648 | bytes 8388608 | tf_op jit(solution)/shard_map/power/pallas_call | solution.py:293
  61.1 11.9 %all_to_all.5.parts_ref = f32[16,24,128]{2,1,0:T(8,128)S(1)} all-to-all(f32[16,24,128]{2,1,0:T(8,128)S(1)} %power.1), channel_id=1, replica_groups=mesh['grp'=2,'ka'=16] {'ka'}, dimensions={0} | all-to-all | bytes 393216 | tf_op jit(solution)/shard_map/all_to_all | solution.py:498
  72.9 2.4 %gradients.1 = (f32[32,32]{1,0:T(8,128)}, f32[32,64]{1,0:T(8,128)}, f32[6,512]{1,0:T(8,128)}, f32[512,512]{1,0:T(8,128)}, f32[64,512]{1,0:T(8,128)}) custom-call(f32[16,24,128]{2,1,0:T(8,128)S(1)} %all_to_all.5.parts_ref, f32[6,32]{1,0:T(8,128)S(1)} %copy-done.6, f32[32,64]{1,0:T(8,128)S(1)} %convolution_add_fusion.3.coeffs_ref, ...), custom_call_target="tpu_custom_call" | custom-call | tf_op jit(solution)/shard_map/gradients/pallas_call | solution.py:403
  (46 shorter events, 0.2 us)
Async XLA Ops:
  0.6 22.3 %copy-start = (f32[512,6]{0,1:T(8,128)S(1)}, f32[512,6]{0,1:T(8,128)}, u32[]{:S(2)}) copy-start(f32[512,6]{0,1:T(8,128)} %param.20) | copy-start | bytes 36868
  5.2 23.3 %collective-permute-start.3 = (bf16[66,16,128]{2,1,0:T(8,128)(2,1)}, bf16[66,16,128]{2,1,0:T(8,128)(2,1)S(1)}, u32[]{:S(2)}, u32[]{:S(2)}) collective-permute-start(bf16[66,16,128]{2,1,0:T(8,128)(2,1)} %get-tuple-element.26), channel_id=1, source_target_pairs={{0,8},{1,9},{2,10},{3,11},{4,12},{5,13},{6,14},{7,15},{8,0},{9,1},... | collective-permute-start | bytes 811016 | tf_op jit(solution)/shard_map/ppermute | solution.py:416
  9.3 25.3 %collective-permute-start.4 = (bf16[66,16,128]{2,1,0:T(8,128)(2,1)}, bf16[66,16,128]{2,1,0:T(8,128)(2,1)S(1)}, u32[]{:S(2)}, u32[]{:S(2)}) collective-permute-start(bf16[66,16,128]{2,1,0:T(8,128)(2,1)} %get-tuple-element.27), channel_id=1, source_target_pairs={{0,10},{1,11},{2,8},{3,9},{4,14},{5,15},{6,12},{7,13},{8,2},{9,3},... | collective-permute-start | bytes 811016 | tf_op jit(solution)/shard_map/ppermute | solution.py:416
  10.6 27.5 %collective-permute-start.5 = (bf16[66,16,128]{2,1,0:T(8,128)(2,1)}, bf16[66,16,128]{2,1,0:T(8,128)(2,1)S(1)}, u32[]{:S(2)}, u32[]{:S(2)}) collective-permute-start(bf16[66,16,128]{2,1,0:T(8,128)(2,1)} %get-tuple-element.28), channel_id=1, source_target_pairs={{0,4},{1,5},{2,6},{3,7},{4,0},{5,1},{6,2},{7,3},{8,12},{9,13},{10,... | collective-permute-start | bytes 811016 | tf_op jit(solution)/shard_map/ppermute | solution.py:416
  12.1 10.8 %copy-start.6 = (f32[6,32]{1,0:T(8,128)S(1)}, f32[6,32]{1,0:T(8,128)}, u32[]{:S(2)}) copy-start(f32[6,32]{1,0:T(8,128)} %params_ref.1) | copy-start | bytes 2308
  12.1 10.8 %copy-start.12 = (f32[512]{0:T(512)S(1)}, f32[512]{0:T(512)}, u32[]{:S(2)}) copy-start(f32[512]{0:T(512)} %param.21) | copy-start | bytes 6148
  12.1 11.1 %copy-start.2 = (f32[512,512]{1,0:T(8,128)S(1)}, f32[512,512]{1,0:T(8,128)}, u32[]{:S(2)}) copy-start(f32[512,512]{1,0:T(8,128)} %weight_mid_ref.1) | copy-start | bytes 3145732
  12.2 11.1 %copy-start.11 = (f32[512]{0:T(512)S(1)}, f32[512]{0:T(512)}, u32[]{:S(2)}) copy-start(f32[512]{0:T(512)} %param.23) | copy-start | bytes 6148
  12.2 12.2 %copy-start.5 = (f32[64,512]{1,0:T(8,128)S(1)}, f32[64,512]{1,0:T(8,128)}, u32[]{:S(2)}) copy-start(f32[64,512]{1,0:T(8,128)} %weight_out_ref.1) | copy-start | bytes 393220
  12.2 12.2 %copy-start.13 = (f32[64]{0:T(128)S(1)}, f32[64]{0:T(128)}, u32[]{:S(2)}) copy-start(f32[64]{0:T(128)} %param.25) | copy-start | bytes 772
  12.2 12.5 %copy-start.4 = (f32[32,64]{1,0:T(8,128)S(1)}, f32[32,64]{1,0:T(8,128)}, u32[]{:S(2)}) copy-start(f32[32,64]{1,0:T(8,128)} %basis_ref.1) | copy-start | bytes 24580
  12.2 12.4 %copy-start.8 = (f32[32]{0:T(128)S(1)}, f32[32]{0:T(128)}, u32[]{:S(2)}) copy-start(f32[32]{0:T(128)} %param.27) | copy-start | bytes 388
  12.2 25.9 %collective-permute-start.6 = (bf16[66,16,128]{2,1,0:T(8,128)(2,1)}, bf16[66,16,128]{2,1,0:T(8,128)(2,1)S(1)}, u32[]{:S(2)}, u32[]{:S(2)}) collective-permute-start(bf16[66,16,128]{2,1,0:T(8,128)(2,1)} %get-tuple-element.29), channel_id=1, source_target_pairs={{0,6},{1,7},{2,4},{3,5},{4,2},{5,3},{6,0},{7,1},{8,14},{9,15},{10,... | collective-permute-start | bytes 811016 | tf_op jit(solution)/shard_map/ppermute | solution.py:416
  18.1 3.3 %copy-start.1 = (bf16[32,256,512]{2,1,0:T(8,128)(2,1)}, bf16[32,256,512]{2,1,0:T(8,128)(2,1)S(1)}, u32[]{:S(2)}) copy-start(bf16[32,256,512]{2,1,0:T(8,128)(2,1)S(1)} %get-tuple-element.34.refs_4_) | copy-start | bytes 25165828
  21.4 16.8 %collective-permute-start.7 = (bf16[66,16,128]{2,1,0:T(8,128)(2,1)}, bf16[66,16,128]{2,1,0:T(8,128)(2,1)S(1)}, u32[]{:S(2)}, u32[]{:S(2)}) collective-permute-start(bf16[66,16,128]{2,1,0:T(8,128)(2,1)} %get-tuple-element.30), channel_id=1, source_target_pairs={{0,2},{1,3},{2,0},{3,1},{4,6},{5,7},{6,4},{7,5},{8,10},{9,11},{10,... | collective-permute-start | bytes 811016 | tf_op jit(solution)/shard_map/ppermute | solution.py:416
  28.5 9.8 %collective-permute-start.1 = (bf16[2,34,16,128]{3,2,1,0:T(8,128)(2,1)}, bf16[2,34,16,128]{3,2,1,0:T(8,128)(2,1)S(1)}, u32[]{:S(2)}, u32[]{:S(2)}) collective-permute-start(bf16[2,34,16,128]{3,2,1,0:T(8,128)(2,1)} %get-tuple-element.25), channel_id=1, source_target_pairs={{0,1},{1,0},{2,3},{3,2},{4,5},{5,4},{6,7},{7,6},{8,9},{9,8},{10,11... | collective-permute-start | bytes 835592 | tf_op jit(solution)/shard_map/ppermute | solution.py:416
  34.6 20.2 %collective-permute-start = (bf16[64,16,128]{2,1,0:T(8,128)(2,1)}, bf16[64,16,128]{2,1,0:T(8,128)(2,1)S(1)}, u32[]{:S(2)}, u32[]{:S(2)}) collective-permute-start(bf16[64,16,128]{2,1,0:T(8,128)(2,1)} %get-tuple-element.23), channel_id=1, source_target_pairs={{0,12},{1,13},{2,14},{3,15},{4,8},{5,9},{6,10},{7,11},{8,4},{9,5},... | collective-permute-start | bytes 786440 | tf_op jit(solution)/shard_map/ppermute | solution.py:416
  38.2 20.7 %slice-start = ((s8[8388608]{0:T(1024)(128)(4,1)}), s8[4194304]{0:T(1024)(128)(4,1)S(1)}, s32[]{:S(2)}) async-start(s8[8388608]{0:T(1024)(128)(4,1)} %bitcast.43), calls=%async_computation.1 | async-start | bytes 8388608
  38.2 4.6 %collective-permute-start.8 = (bf16[5,34,16,128]{3,2,1,0:T(8,128)(2,1)S(1)}, bf16[5,34,16,128]{3,2,1,0:T(8,128)(2,1)S(1)}, u32[]{:S(2)}, u32[]{:S(2)}) collective-permute-start(bf16[5,34,16,128]{3,2,1,0:T(8,128)(2,1)S(1)} %fusion), channel_id=1, source_target_pairs={{0,1},{1,0},{2,3},{3,2},{4,5},{5,4},{6,7},{7,6},{8,9},{9,8},{10,11... | collective-permute-start | bytes 2088968 | tf_op jit(solution)/shard_map/ppermute | solution.py:416
  39.4 15.8 %collective-permute-start.2 = (bf16[64,16,128]{2,1,0:T(8,128)(2,1)S(1)}, bf16[64,16,128]{2,1,0:T(8,128)(2,1)S(1)}, u32[]{:S(2)}, u32[]{:S(2)}) collective-permute-start(bf16[64,16,128]{2,1,0:T(8,128)(2,1)S(1)} %pad_maximum_fusion), channel_id=1, source_target_pairs={{0,14},{1,15},{2,12},{3,13},{4,10},{5,11},{6,8},{7,9},{8,6},{9,7},... | collective-permute-start | bytes 786440 | tf_op jit(solution)/shard_map/ppermute | solution.py:416
  42.7 0.9 %copy-start.3 = (bf16[34,16,128]{2,1,0:T(8,128)(2,1)S(1)}, bf16[34,16,128]{2,1,0:T(8,128)(2,1)}, u32[]{:S(2)}) copy-start(bf16[34,16,128]{2,1,0:T(8,128)(2,1)} %get-tuple-element.31.refs_7_.refs_8_) | copy-start | bytes 417796
  43.7 15.2 %slice-start.1 = ((s8[8388608]{0:T(1024)(128)(4,1)}), s8[4194304]{0:T(1024)(128)(4,1)S(1)}, s32[]{:S(2)}) async-start(s8[8388608]{0:T(1024)(128)(4,1)} %bitcast.43), calls=%async_computation.2 | async-start | bytes 8388608
  43.7 15.2 %copy-start.9 = (s32[32]{0:T(128)S(1)}, s32[32]{0:T(128)}, u32[]{:S(2)}) copy-start(s32[32]{0:T(128)} %param.17) | copy-start | bytes 388
  43.7 15.2 %copy-start.10 = (s32[32]{0:T(128)S(1)}, s32[32]{0:T(128)}, u32[]{:S(2)}) copy-start(s32[32]{0:T(128)} %param.18) | copy-start | bytes 388
  54.7 18.2 %copy-start.7 = (s32[32]{0:T(128)S(1)}, s32[32]{0:T(128)}, u32[]{:S(2)}) copy-start(s32[32]{0:T(128)} %param.16) | copy-start | bytes 388
  54.8 4.1 %collective-permute-start.9 = (bf16[1,32,16,128]{3,2,1,0:T(8,128)(2,1)S(1)}, bf16[1,32,16,128]{3,2,1,0:T(8,128)(2,1)S(1)}, u32[]{:S(2)}, u32[]{:S(2)}) collective-permute-start(bf16[1,32,16,128]{3,2,1,0:T(8,128)(2,1)S(1)} %slice_bitcast_fusion.6), channel_id=1, source_target_pairs={{0,1},{1,0},{2,3},{3,2},{4,5},{5,4},{6,7},{7,6},{8,9},{9,8},{10,11... | collective-permute-start | bytes 393224 | tf_op jit(solution)/shard_map/ppermute | solution.py:416
  54.9 4.0 %collective-permute-start.10 = (bf16[4,2,16,128]{3,2,1,0:T(8,128)(2,1)S(1)}, bf16[4,2,16,128]{3,2,1,0:T(8,128)(2,1)S(1)}, u32[]{:S(2)}, u32[]{:S(2)}) collective-permute-start(bf16[4,2,16,128]{3,2,1,0:T(8,128)(2,1)S(1)} %pad_maximum_fusion.1), channel_id=1, source_target_pairs={{0,4},{1,5},{2,6},{3,7},{4,0},{5,1},{6,2},{7,3},{8,12},{9,13},{10,... | collective-permute-start | bytes 98312 | tf_op jit(solution)/shard_map/ppermute | solution.py:416

commit v7 on v6

--- a/solution.py
+++ b/solution.py
@@ -136,7 +136,7 @@
             pltpu.SemaphoreType.DMA((len(tops),)),
             pltpu.SemaphoreType.DMA((max(1, len(held_tops)),)),
         ],
-        compiler_params=pltpu.CompilerParams(vmem_limit_bytes=(50 if held_tops else 61) << 20),
+        compiler_params=pltpu.CompilerParams(vmem_limit_bytes=(24 if held_tops else 61) << 20),
         cost_estimate=pl.CostEstimate(
             flops=0, bytes_accessed=16 * times * cosmos * block * len(tops), transcendentals=0
         ),

time: 75.7 us -> 75.7 us (level)
  blocking collectives: 11.9 us -> 13.3 us
  Pallas kernels: 25.8 us -> 24.6 us
  starting transfers between devices: 16 us -> 17 us
  local copies, waits for them, and re-layouts: 4.36 us -> 3.48 us
    all_to_all x1, blocking collectives: 11.9 us -> 13.3 us  [local(): lax.all_to_all(parts, 'ka', split_axis=0, concat_axis=0, tiled=True)]
    pallas_call x2, Pallas kernels: 10.2 us -> 8.99 us  [arrange(): pl.pallas_call(functools.partial(arrange_kernel, tops, group, last, waves...]
    ppermute x11, starting transfers between devices: 16 us -> 17 us  [exchange(): lax.ppermute(value, 'ka', [(peer, peer ^ apart) for peer in range(peers)])]
    unnamed x36 -> x46, local copies, waits for them, and re-layouts: 4.31 us -> 3.44 us
  transfers between devices with their start and end apart: 11 -> 11, of which waited for: 3 -> 3; matrix products, arithmetic and copies ran while one was open for 4% -> 4% of each run, Pallas kernels for 22% -> 20%
where the time goes in v7:
time: 75.7 us; the launch traced here: 75.4 us
  Pallas kernels  24.6 us (32%)
  starting transfers between devices  17 us (22%)
  blocking collectives  13.3 us (18%)
  waiting for transfers between devices  13.1 us (17%)
  local copies, waits for them, and re-layouts  3.48 us (5%)
  matrix products  1.87 us (2%)
  other arithmetic  1.09 us (1%)
  between operations  1.01 us (1%)
    ppermute x11, starting transfers between devices, exchange(): lax.ppermute(value, 'ka', [(peer, peer ^ apart) for peer in range(peers)])  17 us
    all_to_all x1, blocking collectives, local(): lax.all_to_all(parts, 'ka', split_axis=0, concat_axis=0, tiled=True)  13.3 us
    ppermute x11, waiting for transfers between devices, exchange(): lax.ppermute(value, 'ka', [(peer, peer ^ apart) for peer in range(peers)])  13.1 us
    pallas_call x1, Pallas kernels, add_groups(): pl.pallas_call(functools.partial(transfer_kernel, group, members, times),...  11.1 us
    pallas_call x2, Pallas kernels, arrange(): pl.pallas_call(functools.partial(arrange_kernel, tops, group, last, waves...  8.99 us
    unnamed x46, local copies, waits for them, and re-layouts  3.44 us
    pallas_call x1, Pallas kernels, gradients(): pl.pallas_call(gradients_kernel, in_specs=[pl.BlockSpec(memory_space=pltp...  2.35 us
    pallas_call x1, Pallas kernels, power_parts(): pl.pallas_call(functools.partial(power_kernel, times, chips, total_waves)...  2.17 us
  transfers between devices with their start and end apart: 11, of which 3 were waited for; matrix products, arithmetic and copies ran while one was open for 4% of the time, Pallas kernels for 20%

profile of v7, /device:TPU:0, one launch (start us, length us, event | category | flops | bytes accessed | tf_op | source)
XLA Modules:
  0.0 75.4 jit_solution(1218177901184424098)
XLA Ops:
  0.6 0.0 copy-start
  0.7 4.7 %arrange.3 = (bf16[66,16,128]{2,1,0:T(8,128)(2,1)}, bf16[66,16,128]{2,1,0:T(8,128)(2,1)}, bf16[66,16,128]{2,1,0:T(8,128)(2,1)}, bf16[66,16,128]{2,1,0:T(8,128)(2,1)}) custom-call(bf16[64,32,512]{2,1,0:T(8,128)(2,1)} %bitcast.43, s32[1,32]{1,0:T(1,128)} %bitcast.47, f32[32,64]{1,0:T(8,128)} %basis_ref.1, bf16[32,1024,512]{2,1,0:T(8,128)(2,1)} %refs_11_.1), custom_call_target="tpu_custom_call" | custom-call | bytes 8388608 | tf_op jit(solution)/shard_map/arrange/pallas_call | solution.py:126
  5.3 4.1 %collective-permute-start.3 = (bf16[66,16,128]{2,1,0:T(8,128)(2,1)}, bf16[66,16,128]{2,1,0:T(8,128)(2,1)S(1)}, u32[]{:S(2)}, u32[]{:S(2)}) collective-permute-start(bf16[66,16,128]{2,1,0:T(8,128)(2,1)} %get-tuple-element.26), channel_id=1, source_target_pairs={{0,8},{1,9},{2,10},{3,11},{4,12},{5,13},{6,14},{7,15},{8,0},{9,1},... | collective-permute-start | bytes 811016 | tf_op jit(solution)/shard_map/ppermute | solution.py:416
  9.4 1.3 %collective-permute-start.4 = (bf16[66,16,128]{2,1,0:T(8,128)(2,1)}, bf16[66,16,128]{2,1,0:T(8,128)(2,1)S(1)}, u32[]{:S(2)}, u32[]{:S(2)}) collective-permute-start(bf16[66,16,128]{2,1,0:T(8,128)(2,1)} %get-tuple-element.27), channel_id=1, source_target_pairs={{0,10},{1,11},{2,8},{3,9},{4,14},{5,15},{6,12},{7,13},{8,2},{9,3},... | collective-permute-start | bytes 811016 | tf_op jit(solution)/shard_map/ppermute | solution.py:416
  10.7 1.6 %collective-permute-start.5 = (bf16[66,16,128]{2,1,0:T(8,128)(2,1)}, bf16[66,16,128]{2,1,0:T(8,128)(2,1)S(1)}, u32[]{:S(2)}, u32[]{:S(2)}) collective-permute-start(bf16[66,16,128]{2,1,0:T(8,128)(2,1)} %get-tuple-element.28), channel_id=1, source_target_pairs={{0,4},{1,5},{2,6},{3,7},{4,0},{5,1},{6,2},{7,3},{8,12},{9,13},{10,... | collective-permute-start | bytes 811016 | tf_op jit(solution)/shard_map/ppermute | solution.py:416
  12.3 0.0 copy-start.6
  12.3 0.0 copy-start.18
  12.3 0.0 copy-start.10
  12.4 0.2 collective-permute-start.6
  12.6 4.3 %arrange.2 = (bf16[32,256,512]{2,1,0:T(8,128)(2,1)S(1)}, bf16[34,16,128]{2,1,0:T(8,128)(2,1)S(1)}, bf16[66,16,128]{2,1,0:T(8,128)(2,1)}, bf16[64,16,128]{2,1,0:T...) custom-call(bf16[64,32,512]{2,1,0:T(8,128)(2,1)S(1)} %bitcast.44, ...), custom_call_target="tpu_custom_call" | custom-call | bytes 8388608 | tf_op jit(solution)/shard_map/arrange/pallas_call | solution.py:126
  16.9 3.3 %copy-done.2 = bf16[32,256,512]{2,1,0:T(8,128)(2,1)} copy-done((bf16[32,256,512]{2,1,0:T(8,128)(2,1)}, bf16[32,256,512]{2,1,0:T(8,128)(2,1)S(1)}, u32[]{:S(2)}) %copy-start.2) | copy-done | bytes 8388632
  20.2 1.8 %collective-permute-start.7 = (bf16[66,16,128]{2,1,0:T(8,128)(2,1)}, bf16[66,16,128]{2,1,0:T(8,128)(2,1)S(1)}, u32[]{:S(2)}, u32[]{:S(2)}) collective-permute-start(bf16[66,16,128]{2,1,0:T(8,128)(2,1)} %get-tuple-element.30), channel_id=1, source_target_pairs={{0,2},{1,3},{2,0},{3,1},{4,6},{5,7},{6,4},{7,5},{8,10},{9,11},{10,... | collective-permute-start | bytes 811016 | tf_op jit(solution)/shard_map/ppermute | solution.py:416
  22.0 0.3 add_multiply_fusion.1
  22.3 1.1 %add_multiply_fusion = (f32[32,512]{1,0:T(8,128)S(1)}, f32[32,512]{1,0:T(8,128)S(1)}, f32[32,512]{1,0:T(8,128)S(1)}) fusion(f32[512]{0:T(512)S(1)} %copy-done.16, f32[512,512]{1,0:T(8,128)S(1)} %copy-done.3, f32[32,512]{1,0:T(8,128)S(1)} %get-tuple-element.47), kind=kOutput, calls=%fused_computation.17 | convolution fusion | flops 100876288 | bytes 1312768 | tf_op jit(solution)/shard_map/dot_general | solution.py:25
  23.4 0.2 convolution_add_fusion.3.coeffs_ref
  23.7 0.1 convolution_add_fusion.2
  23.8 4.8 %collective-permute-done.3.refs_2_ = bf16[66,16,128]{2,1,0:T(8,128)(2,1)S(1)} collective-permute-done((bf16[66,16,128]{2,1,0:T(8,128)(2,1)}, bf16[66,16,128]{2,1,0:T(8,128)(2,1)S(1)}, u32[]{:S(2)}, u32[]{:S(2)}) %collective-permute-start.3) | collective-permute-done | bytes 270368 | tf_op jit(solution)/shard_map/ppermute | solution.py:416
  28.7 6.0 %collective-permute-done.4.refs_3_ = bf16[66,16,128]{2,1,0:T(8,128)(2,1)S(1)} collective-permute-done((bf16[66,16,128]{2,1,0:T(8,128)(2,1)}, bf16[66,16,128]{2,1,0:T(8,128)(2,1)S(1)}, u32[]{:S(2)}, u32[]{:S(2)}) %collective-permute-start.4) | collective-permute-done | bytes 270368 | tf_op jit(solution)/shard_map/ppermute | solution.py:416
  34.7 3.5 %collective-permute-start = (bf16[64,16,128]{2,1,0:T(8,128)(2,1)}, bf16[64,16,128]{2,1,0:T(8,128)(2,1)S(1)}, u32[]{:S(2)}, u32[]{:S(2)}) collective-permute-start(bf16[64,16,128]{2,1,0:T(8,128)(2,1)} %copy-done.15), channel_id=1, source_target_pairs={{0,12},{1,13},{2,14},{3,15},{4,8},{5,9},{6,10},{7,11},{8,4},{9,5},... | collective-permute-start | bytes 786440 | tf_op jit(solution)/shard_map/ppermute | solution.py:416
  38.4 0.1 collective-permute-start.8
  38.5 1.1 %pad_maximum_fusion = bf16[64,16,128]{2,1,0:T(8,128)(2,1)S(1)} fusion(bf16[32,16,128]{2,1,0:T(8,128)(2,1)S(1)} %slice_bitcast_fusion.5, bf16[32,16,128]{2,1,0:T(8,128)(2,1)} %copy-done.7), kind=kLoop, calls=%fused_computation.4 | loop fusion | flops 131072 | bytes 524288 | tf_op jit(solution)/shard_map/concatenate | solution.py:468
  39.6 2.8 %collective-permute-start.2 = (bf16[64,16,128]{2,1,0:T(8,128)(2,1)S(1)}, bf16[64,16,128]{2,1,0:T(8,128)(2,1)S(1)}, u32[]{:S(2)}, u32[]{:S(2)}) collective-permute-start(bf16[64,16,128]{2,1,0:T(8,128)(2,1)S(1)} %pad_maximum_fusion), channel_id=1, source_target_pairs={{0,14},{1,15},{2,12},{3,13},{4,10},{5,11},{6,8},{7,9},{8,6},{9,7},... | collective-permute-start | bytes 786440 | tf_op jit(solution)/shard_map/ppermute | solution.py:416
  42.4 11.1 %transfer.1 = (f32[32,32,512]{2,1,0:T(8,128)S(1)}, bf16[16,32,128]{2,1,0:T(8,128)(2,1)S(1)}) custom-call(s32[1]{0:T(128)} %bitcast.3.me_ref, bf16[5,34,16,128]{3,2,1,0:T(8,128)(2,1)S(1)} %collective-permute-done.8.refs_0_, bf16[2,34,16,128]{3,2,1,0:T(8,128)(2,1)S(1)} %collective-permute-done.1.refs_1_, ...), custom_call_target="tpu_custom_call" | custom-call | flops 8589934592 | bytes 33554432 | tf_op jit(solution)/shard_map/transfer/pallas_call | solution.py:208
  53.4 0.0 copy-start.11
  53.5 0.1 collective-permute-start.9
  53.6 1.6 %collective-permute-start.10 = (bf16[4,2,16,128]{3,2,1,0:T(8,128)(2,1)S(1)}, bf16[4,2,16,128]{3,2,1,0:T(8,128)(2,1)S(1)}, u32[]{:S(2)}, u32[]{:S(2)}) collective-permute-start(bf16[4,2,16,128]{3,2,1,0:T(8,128)(2,1)S(1)} %pad_maximum_fusion.1), channel_id=1, source_target_pairs={{0,4},{1,5},{2,6},{3,7},{4,0},{5,1},{6,2},{7,3},{8,12},{9,13},{10,... | collective-permute-start | bytes 98312 | tf_op jit(solution)/shard_map/ppermute | solution.py:416
  55.2 0.1 fusion.10.refs_10_
  55.4 0.0 collective-permute-done.2.refs_1_
  55.4 2.2 %collective-permute-done.10.refs_3_ = bf16[4,2,16,128]{3,2,1,0:T(8,128)(2,1)S(1)} collective-permute-done((bf16[4,2,16,128]{3,2,1,0:T(8,128)(2,1)S(1)}, bf16[4,2,16,128]{3,2,1,0:T(8,128)(2,1)S(1)}, u32[]{:S(2)}, u32[]{:S(2)}) %collective-permute-start.10) | collective-permute-done | bytes 32800 | tf_op jit(solution)/shard_map/ppermute | solution.py:416
  57.6 2.2 %power.1 = f32[16,24,128]{2,1,0:T(8,128)S(1)} custom-call(bf16[64,16,128]{2,1,0:T(8,128)(2,1)S(1)} %collective-permute-done.refs_0_, bf16[64,16,128]{2,1,0:T(8,128)(2,1)S(1)} %collective-permute-done.2.refs_1_, bf16[1,32,16,128]{3,2,1,0:T(8,128)(2,1)S(1)} %collective-permute-done.9.refs_2_, bf16[4,2,16,128]{3,2,1,0:T(8,128)(2,1)S(1)} %collective-permute-done.10.refs_3_, ...), custom_call_target="tpu_custom_call" | custom-call | flops 2147483648 | bytes 8388608 | tf_op jit(solution)/shard_map/power/pallas_call | solution.py:293
  59.8 13.3 %all_to_all.5.parts_ref = f32[16,24,128]{2,1,0:T(8,128)S(1)} all-to-all(f32[16,24,128]{2,1,0:T(8,128)S(1)} %power.1), channel_id=1, replica_groups=mesh['grp'=2,'ka'=16] {'ka'}, dimensions={0} | all-to-all | bytes 393216 | tf_op jit(solution)/shard_map/all_to_all | solution.py:498
  73.1 2.4 %gradients.1 = (f32[32,32]{1,0:T(8,128)}, f32[32,64]{1,0:T(8,128)}, f32[6,512]{1,0:T(8,128)}, f32[512,512]{1,0:T(8,128)}, f32[64,512]{1,0:T(8,128)}) custom-call(f32[16,24,128]{2,1,0:T(8,128)S(1)} %all_to_all.5.parts_ref, f32[6,32]{1,0:T(8,128)S(1)} %copy-done.8, f32[32,64]{1,0:T(8,128)S(1)} %convolution_add_fusion.3.coeffs_ref, ...), custom_call_target="tpu_custom_call" | custom-call | tf_op jit(solution)/shard_map/gradients/pallas_call | solution.py:403
  (56 shorter events, 0.2 us)
Async XLA Ops:
  0.6 21.3 %copy-start = (f32[512,6]{0,1:T(8,128)S(1)}, f32[512,6]{0,1:T(8,128)}, u32[]{:S(2)}) copy-start(f32[512,6]{0,1:T(8,128)} %param.20) | copy-start | bytes 36868
  0.6 11.9 %copy-start.1 = (bf16[64,512,32]{1,2,0:T(8,128)(2,1)S(1)}, bf16[64,512,32]{1,2,0:T(8,128)(2,1)}, u32[]{:S(2)}) copy-start(bf16[64,512,32]{1,2,0:T(8,128)(2,1)} %param.14) | copy-start | bytes 6291460
  0.7 11.9 %copy-start.5 = (f32[32,64]{1,0:T(8,128)S(1)}, f32[32,64]{1,0:T(8,128)}, u32[]{:S(2)}) copy-start(f32[32,64]{1,0:T(8,128)} %basis_ref.1) | copy-start | bytes 24580
  0.7 11.9 %copy-start.9 = (s32[32]{0:T(128)S(1)}, s32[32]{0:T(128)}, u32[]{:S(2)}) copy-start(s32[32]{0:T(128)} %param.16) | copy-start | bytes 388
  5.3 23.3 %collective-permute-start.3 = (bf16[66,16,128]{2,1,0:T(8,128)(2,1)}, bf16[66,16,128]{2,1,0:T(8,128)(2,1)S(1)}, u32[]{:S(2)}, u32[]{:S(2)}) collective-permute-start(bf16[66,16,128]{2,1,0:T(8,128)(2,1)} %get-tuple-element.26), channel_id=1, source_target_pairs={{0,8},{1,9},{2,10},{3,11},{4,12},{5,13},{6,14},{7,15},{8,0},{9,1},... | collective-permute-start | bytes 811016 | tf_op jit(solution)/shard_map/ppermute | solution.py:416
  9.4 25.3 %collective-permute-start.4 = (bf16[66,16,128]{2,1,0:T(8,128)(2,1)}, bf16[66,16,128]{2,1,0:T(8,128)(2,1)S(1)}, u32[]{:S(2)}, u32[]{:S(2)}) collective-permute-start(bf16[66,16,128]{2,1,0:T(8,128)(2,1)} %get-tuple-element.27), channel_id=1, source_target_pairs={{0,10},{1,11},{2,8},{3,9},{4,14},{5,15},{6,12},{7,13},{8,2},{9,3},... | collective-permute-start | bytes 811016 | tf_op jit(solution)/shard_map/ppermute | solution.py:416
  10.7 27.5 %collective-permute-start.5 = (bf16[66,16,128]{2,1,0:T(8,128)(2,1)}, bf16[66,16,128]{2,1,0:T(8,128)(2,1)S(1)}, u32[]{:S(2)}, u32[]{:S(2)}) collective-permute-start(bf16[66,16,128]{2,1,0:T(8,128)(2,1)} %get-tuple-element.28), channel_id=1, source_target_pairs={{0,4},{1,5},{2,6},{3,7},{4,0},{5,1},{6,2},{7,3},{8,12},{9,13},{10,... | collective-permute-start | bytes 811016 | tf_op jit(solution)/shard_map/ppermute | solution.py:416
  12.3 9.7 %copy-start.8 = (f32[6,32]{1,0:T(8,128)S(1)}, f32[6,32]{1,0:T(8,128)}, u32[]{:S(2)}) copy-start(f32[6,32]{1,0:T(8,128)} %params_ref.1) | copy-start | bytes 2308
  12.3 9.7 %copy-start.17 = (f32[512]{0:T(512)S(1)}, f32[512]{0:T(512)}, u32[]{:S(2)}) copy-start(f32[512]{0:T(512)} %param.21) | copy-start | bytes 6148
  12.3 10.0 %copy-start.3 = (f32[512,512]{1,0:T(8,128)S(1)}, f32[512,512]{1,0:T(8,128)}, u32[]{:S(2)}) copy-start(f32[512,512]{1,0:T(8,128)} %weight_mid_ref.1) | copy-start | bytes 3145732
  12.3 10.0 %copy-start.16 = (f32[512]{0:T(512)S(1)}, f32[512]{0:T(512)}, u32[]{:S(2)}) copy-start(f32[512]{0:T(512)} %param.23) | copy-start | bytes 6148
  12.3 11.1 %copy-start.6 = (f32[64,512]{1,0:T(8,128)S(1)}, f32[64,512]{1,0:T(8,128)}, u32[]{:S(2)}) copy-start(f32[64,512]{1,0:T(8,128)} %weight_out_ref.1) | copy-start | bytes 393220
  12.3 11.1 %copy-start.18 = (f32[64]{0:T(128)S(1)}, f32[64]{0:T(128)}, u32[]{:S(2)}) copy-start(f32[64]{0:T(128)} %param.25) | copy-start | bytes 772
  12.3 11.3 %copy-start.10 = (f32[32]{0:T(128)S(1)}, f32[32]{0:T(128)}, u32[]{:S(2)}) copy-start(f32[32]{0:T(128)} %param.27) | copy-start | bytes 388
  12.4 25.9 %collective-permute-start.6 = (bf16[66,16,128]{2,1,0:T(8,128)(2,1)}, bf16[66,16,128]{2,1,0:T(8,128)(2,1)S(1)}, u32[]{:S(2)}, u32[]{:S(2)}) collective-permute-start(bf16[66,16,128]{2,1,0:T(8,128)(2,1)} %get-tuple-element.29), channel_id=1, source_target_pairs={{0,6},{1,7},{2,4},{3,5},{4,2},{5,3},{6,0},{7,1},{8,14},{9,15},{10,... | collective-permute-start | bytes 811016 | tf_op jit(solution)/shard_map/ppermute | solution.py:416
  16.9 3.3 %copy-start.2 = (bf16[32,256,512]{2,1,0:T(8,128)(2,1)}, bf16[32,256,512]{2,1,0:T(8,128)(2,1)S(1)}, u32[]{:S(2)}) copy-start(bf16[32,256,512]{2,1,0:T(8,128)(2,1)S(1)} %get-tuple-element.34.refs_4_) | copy-start | bytes 25165828
  20.2 3.2 %copy-start.7 = (bf16[32,16,128]{2,1,0:T(8,128)(2,1)}, bf16[32,16,128]{2,1,0:T(8,128)(2,1)S(1)}, u32[]{:S(2)}) copy-start(bf16[32,16,128]{2,1,0:T(8,128)(2,1)S(1)} %get-tuple-element.24) | copy-start | bytes 393220
  20.2 3.6 %copy-start.14 = (bf16[2,34,16,128]{3,2,1,0:T(8,128)(2,1)}, bf16[2,34,16,128]{3,2,1,0:T(8,128)(2,1)S(1)}, u32[]{:S(2)}) copy-start(bf16[2,34,16,128]{3,2,1,0:T(8,128)(2,1)S(1)} %get-tuple-element.25) | copy-start | bytes 835588
  20.2 3.6 %copy-start.15 = (bf16[64,16,128]{2,1,0:T(8,128)(2,1)}, bf16[64,16,128]{2,1,0:T(8,128)(2,1)S(1)}, u32[]{:S(2)}) copy-start(bf16[64,16,128]{2,1,0:T(8,128)(2,1)S(1)} %get-tuple-element.23) | copy-start | bytes 786436
  20.2 18.1 %collective-permute-start.7 = (bf16[66,16,128]{2,1,0:T(8,128)(2,1)}, bf16[66,16,128]{2,1,0:T(8,128)(2,1)S(1)}, u32[]{:S(2)}, u32[]{:S(2)}) collective-permute-start(bf16[66,16,128]{2,1,0:T(8,128)(2,1)} %get-tuple-element.30), channel_id=1, source_target_pairs={{0,2},{1,3},{2,0},{3,1},{4,6},{5,7},{6,4},{7,5},{8,10},{9,11},{10,... | collective-permute-start | bytes 811016 | tf_op jit(solution)/shard_map/ppermute | solution.py:416
  28.6 9.8 %collective-permute-start.1 = (bf16[2,34,16,128]{3,2,1,0:T(8,128)(2,1)}, bf16[2,34,16,128]{3,2,1,0:T(8,128)(2,1)S(1)}, u32[]{:S(2)}, u32[]{:S(2)}) collective-permute-start(bf16[2,34,16,128]{3,2,1,0:T(8,128)(2,1)} %copy-done.14), channel_id=1, source_target_pairs={{0,1},{1,0},{2,3},{3,2},{4,5},{5,4},{6,7},{7,6},{8,9},{9,8},{10,11... | collective-permute-start | bytes 835592 | tf_op jit(solution)/shard_map/ppermute | solution.py:416
  34.7 18.7 %collective-permute-start = (bf16[64,16,128]{2,1,0:T(8,128)(2,1)}, bf16[64,16,128]{2,1,0:T(8,128)(2,1)S(1)}, u32[]{:S(2)}, u32[]{:S(2)}) collective-permute-start(bf16[64,16,128]{2,1,0:T(8,128)(2,1)} %copy-done.15), channel_id=1, source_target_pairs={{0,12},{1,13},{2,14},{3,15},{4,8},{5,9},{6,10},{7,11},{8,4},{9,5},... | collective-permute-start | bytes 786440 | tf_op jit(solution)/shard_map/ppermute | solution.py:416
  38.3 19.3 %slice-start = ((s8[8388608]{0:T(1024)(128)(4,1)}), s8[4194304]{0:T(1024)(128)(4,1)S(1)}, s32[]{:S(2)}) async-start(s8[8388608]{0:T(1024)(128)(4,1)} %bitcast.45), calls=%async_computation.1 | async-start | bytes 8388608
  38.4 4.0 %collective-permute-start.8 = (bf16[5,34,16,128]{3,2,1,0:T(8,128)(2,1)S(1)}, bf16[5,34,16,128]{3,2,1,0:T(8,128)(2,1)S(1)}, u32[]{:S(2)}, u32[]{:S(2)}) collective-permute-start(bf16[5,34,16,128]{3,2,1,0:T(8,128)(2,1)S(1)} %fusion), channel_id=1, source_target_pairs={{0,1},{1,0},{2,3},{3,2},{4,5},{5,4},{6,7},{7,6},{8,9},{9,8},{10,11... | collective-permute-start | bytes 2088968 | tf_op jit(solution)/shard_map/ppermute | solution.py:416
  39.6 15.8 %collective-permute-start.2 = (bf16[64,16,128]{2,1,0:T(8,128)(2,1)S(1)}, bf16[64,16,128]{2,1,0:T(8,128)(2,1)S(1)}, u32[]{:S(2)}, u32[]{:S(2)}) collective-permute-start(bf16[64,16,128]{2,1,0:T(8,128)(2,1)S(1)} %pad_maximum_fusion), channel_id=1, source_target_pairs={{0,14},{1,15},{2,12},{3,13},{4,10},{5,11},{6,8},{7,9},{8,6},{9,7},... | collective-permute-start | bytes 786440 | tf_op jit(solution)/shard_map/ppermute | solution.py:416
  42.4 15.2 %slice-start.1 = ((s8[8388608]{0:T(1024)(128)(4,1)}), s8[4194304]{0:T(1024)(128)(4,1)S(1)}, s32[]{:S(2)}) async-start(s8[8388608]{0:T(1024)(128)(4,1)} %bitcast.45), calls=%async_computation.2 | async-start | bytes 8388608
  42.4 15.2 %copy-start.12 = (s32[32]{0:T(128)S(1)}, s32[32]{0:T(128)}, u32[]{:S(2)}) copy-start(s32[32]{0:T(128)} %param.17) | copy-start | bytes 388
  42.4 15.2 %copy-start.13 = (s32[32]{0:T(128)S(1)}, s32[32]{0:T(128)}, u32[]{:S(2)}) copy-start(s32[32]{0:T(128)} %param.18) | copy-start | bytes 388
  53.4 19.6 %copy-start.4 = (f32[512,512]{1,0:T(8,128)S(1)}, f32[512,512]{1,0:T(8,128)}, u32[]{:S(2)}) copy-start(f32[512,512]{1,0:T(8,128)} %weight_mid_ref.1) | copy-start | bytes 3145732
  53.4 19.6 %copy-start.11 = (f32[32]{0:T(128)S(1)}, f32[32]{0:T(128)}, u32[]{:S(2)}) copy-start(f32[32]{0:T(128)} %param.27) | copy-start | bytes 388
  53.5 4.1 %collective-permute-start.9 = (bf16[1,32,16,128]{3,2,1,0:T(8,128)(2,1)S(1)}, bf16[1,32,16,128]{3,2,1,0:T(8,128)(2,1)S(1)}, u32[]{:S(2)}, u32[]{:S(2)}) collective-permute-start(bf16[1,32,16,128]{3,2,1,0:T(8,128)(2,1)S(1)} %slice_bitcast_fusion.6), channel_id=1, source_target_pairs={{0,1},{1,0},{2,3},{3,2},{4,5},{5,4},{6,7},{7,6},{8,9},{9,8},{10,11... | collective-permute-start | bytes 393224 | tf_op jit(solution)/shard_map/ppermute | solution.py:416
  53.6 4.0 %collective-permute-start.10 = (bf16[4,2,16,128]{3,2,1,0:T(8,128)(2,1)S(1)}, bf16[4,2,16,128]{3,2,1,0:T(8,128)(2,1)S(1)}, u32[]{:S(2)}, u32[]{:S(2)}) collective-permute-start(bf16[4,2,16,128]{3,2,1,0:T(8,128)(2,1)S(1)} %pad_maximum_fusion.1), channel_id=1, source_target_pairs={{0,4},{1,5},{2,6},{3,7},{4,0},{5,1},{6,2},{7,3},{8,12},{9,13},{10,... | collective-permute-start | bytes 98312 | tf_op jit(solution)/shard_map/ppermute | solution.py:416
